TPU v7x, 32 devices: a whole 2x2x4 slice. The times are simulated.
32 devices in a mesh: groups: 2 (over y), ctx: 4 (over z), dp: 2 (over x), mp: 2 (over core).
Axes of the slice: x: 2, y: 2, z: 4, core: 2. Of those that a mesh axis runs over, the one named last changes fastest.
Arguments:
- positions: int32 [4, 512], P(('groups', 'dp')), parts along dimension 0, may hold values from 0 to 4095, as said below
- queries: bfloat16 [4, 1024, 4096], P(('groups', 'dp'), 'ctx', 'mp'), parts along dimension 0, may hold values from -4 to 4
- keys: bfloat16 [4, 1024, 512], P(('groups', 'dp'), 'ctx', 'mp'), parts along dimension 0, may hold values from -36 to 36
- values: bfloat16 [4, 1024, 512], P(('groups', 'dp'), 'ctx', 'mp'), parts along dimension 0, may hold values from -6 to 6
- out_grad: bfloat16 [4, 1024, 4096], P(('groups', 'dp'), 'ctx', 'mp'), parts along dimension 0, may hold values from -6 to 6
Outputs:
- query_grad: bfloat16 [4, 1024, 4096], P(('groups', 'dp'), 'ctx', 'mp'), parts along dimension 0
- key_grad: bfloat16 [4, 1024, 512], P(('groups', 'dp'), 'ctx', 'mp'), parts along dimension 0
- value_grad: bfloat16 [4, 1024, 512], P(('groups', 'dp'), 'ctx', 'mp'), parts along dimension 0
There are 2 independent parts, one for each index of `groups`. A program takes and returns all parts, laid end to end along the dimension named above; each array names one. Nothing has to cross between parts.
Inputs may be any that keep to these rules, and one draw needn't show every extreme that they name: In each sequence the positions rise strictly with the rank; the shard k * 1024 to (k + 1) * 1024 - 1 holds at most 256 of them, and some shard holds exactly 256.
All inputs are finite; a program needn't handle non-finite values.
Results may differ from a plain program's by a relative error of at most 0.007.
The roundings to bfloat16 on the way count: a program that leaves them out, or rounds other values in their place, can miss the bound.
Values may be sent and summed in bfloat16 or wider, within the bound.
No kernel may reach another device: no remote copies, remote signals or barrier semaphores. Data moves between devices by JAX's collectives and lax.ppermute only.
A program may use at most 128 MiB of HBM per device.

v0:
```python
import math

import jax
import jax.numpy as jnp
from jax import lax
from jax.sharding import PartitionSpec as P

HEAD_DIM = 128
TOK_SHARD = 1024


rope_base = 500000.0


def rope_tables(seq_pos, head_dim):
    half_dim = head_dim // 2
    ladder = jnp.arange(half_dim).astype(jnp.float32)
    inverse_freq = jnp.exp(ladder * (-2.0 * math.log(rope_base) / head_dim))
    angles = seq_pos.astype(jnp.float32)[:, None] * inverse_freq[None, :]
    return (jnp.cos(angles), jnp.sin(angles))


def rotate(field, cos_table, sin_table, rotation):
    half_dim = field.shape[-1] // 2
    front_part = field[..., :half_dim]
    back_part = field[..., half_dim:]
    cos_part = cos_table[:, None, :]
    sin_part = rotation * sin_table[:, None, :]
    return jnp.concatenate(
        [
            front_part * cos_part - back_part * sin_part,
            back_part * cos_part + front_part * sin_part,
        ],
        axis=-1,
    )


def body(positions, queries, keys, values, out_grad):
    ctx_size = lax.axis_size("ctx")
    ctx_rank = lax.axis_index("ctx")
    seq_pos = positions[0]
    routed = seq_pos.shape[0]
    row_count = routed // ctx_size
    capacity = queries.shape[1]
    per_peer = capacity // ctx_size
    head_dim = HEAD_DIM
    query_heads = queries.shape[2] // head_dim
    key_heads = keys.shape[2] // head_dim
    group_size = query_heads // key_heads
    score_scale = 1.0 / math.sqrt(head_dim)
    shard_of = seq_pos // TOK_SHARD
    shard_ids = jnp.arange(ctx_size, dtype=jnp.int32)
    member = (shard_of[:, None] == shard_ids[None, :]).astype(jnp.int32)
    counts = jnp.sum(member, axis=0)
    firsts = jnp.cumsum(counts) - counts
    is_mine = shard_ids == ctx_rank
    my_first = jnp.sum(jnp.where(is_mine, firsts, 0))
    my_count = jnp.sum(jnp.where(is_mine, counts, 0))
    my_lead = my_first % ctx_size
    send_pos = jnp.arange(capacity, dtype=jnp.int32)
    target = send_pos // per_peer
    offset = send_pos % per_peer
    local_slot = (offset + (target < my_lead).astype(jnp.int32)) * ctx_size + target - my_lead
    send_live = local_slot < my_count
    send_index = jnp.minimum(local_slot, capacity - 1)

    def pack_rows(source):
        picked = jnp.take(source, send_index, axis=0)
        return jnp.where(send_live[:, None], picked, jnp.zeros((), source.dtype))

    my_ranks = jnp.arange(row_count, dtype=jnp.int32) * ctx_size + ctx_rank
    my_shards = jnp.take(shard_of, my_ranks)
    their_first = jnp.take(firsts, my_shards)
    their_lead = their_first % ctx_size
    recv_index = (
        my_shards * per_peer
        + (my_ranks - their_first + their_lead) // ctx_size
        - (ctx_rank < their_lead).astype(jnp.int32)
    )
    cos_mine, sin_mine = rope_tables(jnp.take(seq_pos, my_ranks), head_dim)
    arrived = (
        lax.all_to_all(pack_rows(queries[0]), "ctx", split_axis=0, concat_axis=0, tiled=True),
        lax.all_to_all(pack_rows(keys[0]), "ctx", split_axis=0, concat_axis=0, tiled=True),
        lax.all_to_all(pack_rows(values[0]), "ctx", split_axis=0, concat_axis=0, tiled=True),
        lax.all_to_all(pack_rows(out_grad[0]), "ctx", split_axis=0, concat_axis=0, tiled=True),
    )
    own_query, own_key, own_value, own_grad = [
        jnp.take(source, recv_index, axis=0) for source in arrived
    ]
    key_mine = rotate(
        own_key.reshape(row_count, key_heads, head_dim).astype(jnp.float32), cos_mine, sin_mine, 1.0
    )
    key_mine = key_mine.astype(jnp.bfloat16).reshape(row_count, key_heads * head_dim)
    key_all, value_all = (
        lax.all_gather(key_mine, "ctx", axis=0, tiled=True),
        lax.all_gather(own_value, "ctx", axis=0, tiled=True),
    )
    key_sorted = key_all.reshape(ctx_size, row_count, -1).transpose(1, 0, 2).reshape(routed, -1)
    value_sorted = value_all.reshape(ctx_size, row_count, -1).transpose(1, 0, 2).reshape(routed, -1)
    query_rot = rotate(
        own_query.reshape(row_count, query_heads, head_dim).astype(jnp.float32),
        cos_mine,
        sin_mine,
        1.0,
    )
    query_view = query_rot.astype(jnp.bfloat16).reshape(row_count, key_heads, group_size, head_dim)
    grad_view = own_grad.reshape(row_count, key_heads, group_size, head_dim)
    key_view = key_sorted.reshape(routed, key_heads, head_dim)
    value_view = value_sorted.reshape(routed, key_heads, head_dim)
    block_total = 4
    block_len = routed // block_total
    stride_rows = row_count // block_total

    def block_scores(block_num):
        row_start = block_num * stride_rows
        key_part = key_view[block_num * block_len : (block_num + 1) * block_len]
        value_part = value_view[block_num * block_len : (block_num + 1) * block_len]
        scores = (
            jnp.einsum(
                "ikgd,skd->kgis",
                query_view[row_start:],
                key_part,
                preferred_element_type=jnp.float32,
            )
            * score_scale
        )
        key_ranks = block_num * block_len + jnp.arange(block_len, dtype=jnp.int32)
        allowed = key_ranks[None, :] <= my_ranks[row_start:, None]
        scores = jnp.where(allowed, scores, -jnp.inf)
        prob_grad = jnp.einsum(
            "ikgd,skd->kgis", grad_view[row_start:], value_part, preferred_element_type=jnp.float32
        )
        return (row_start, key_part, scores, prob_grad)

    row_peak = jnp.full((key_heads, group_size, row_count), -jnp.inf, jnp.float32)
    row_total = jnp.zeros((key_heads, group_size, row_count), jnp.float32)
    weighted = jnp.zeros((key_heads, group_size, row_count), jnp.float32)
    for block_num in range(block_total):
        row_start, key_part, scores, prob_grad = block_scores(block_num)
        old_peak = row_peak[..., row_start:]
        new_peak = jnp.maximum(old_peak, jnp.max(scores, axis=-1))
        rescale = jnp.exp(old_peak - new_peak)
        exp_scores = jnp.exp(scores - new_peak[..., None])
        row_total = row_total.at[..., row_start:].set(
            row_total[..., row_start:] * rescale + jnp.sum(exp_scores, axis=-1)
        )
        weighted = weighted.at[..., row_start:].set(
            weighted[..., row_start:] * rescale + jnp.sum(exp_scores * prob_grad, axis=-1)
        )
        row_peak = row_peak.at[..., row_start:].set(new_peak)
    row_delta = weighted / row_total
    query_acc = jnp.zeros((row_count, key_heads, group_size, head_dim), jnp.float32)
    key_terms = []
    value_terms = []
    for block_num in range(block_total):
        row_start, key_part, scores, prob_grad = block_scores(block_num)
        prob_rows = (
            jnp.exp(scores - row_peak[..., row_start:, None]) / row_total[..., row_start:, None]
        )
        score_grad = (prob_rows * (prob_grad - row_delta[..., row_start:, None])).astype(
            jnp.bfloat16
        )
        prob_half = prob_rows.astype(jnp.bfloat16)
        value_terms.append(
            jnp.einsum(
                "kgis,ikgd->skd",
                prob_half,
                grad_view[row_start:],
                preferred_element_type=jnp.float32,
            )
        )
        key_terms.append(
            jnp.einsum(
                "kgis,ikgd->skd",
                score_grad,
                query_view[row_start:],
                preferred_element_type=jnp.float32,
            )
            * score_scale
        )
        query_step = (
            jnp.einsum("kgis,skd->ikgd", score_grad, key_part, preferred_element_type=jnp.float32)
            * score_scale
        )
        query_acc = query_acc.at[row_start:].add(query_step)
    key_term = jnp.concatenate(key_terms, axis=0).reshape(row_count, ctx_size, key_heads * head_dim)
    value_term = jnp.concatenate(value_terms, axis=0).reshape(
        row_count, ctx_size, key_heads * head_dim
    )
    source_first = jnp.take(firsts, target)
    source_count = jnp.take(counts, target)
    source_lead = source_first % ctx_size
    back_rank = (
        source_first
        - source_lead
        + (offset + (ctx_rank < source_lead).astype(jnp.int32)) * ctx_size
        + ctx_rank
    )
    back_live = back_rank < source_first + source_count
    back_index = jnp.clip(back_rank // ctx_size, 0, row_count - 1)

    def pack_back(source):
        picked = jnp.take(source, back_index, axis=0)
        return jnp.where(back_live[:, None], picked, jnp.zeros((), source.dtype))

    query_mine = rotate(
        query_acc.reshape(row_count, query_heads, head_dim), cos_mine, sin_mine, -1.0
    )
    query_send = pack_back(
        query_mine.astype(jnp.bfloat16).reshape(row_count, query_heads * head_dim)
    )
    key_sum, value_sum = (
        lax.psum_scatter(key_term, "ctx", scatter_dimension=1, tiled=True),
        lax.psum_scatter(value_term, "ctx", scatter_dimension=1, tiled=True),
    )
    key_mine = rotate(key_sum.reshape(row_count, key_heads, head_dim), cos_mine, sin_mine, -1.0)
    key_send = pack_back(key_mine.astype(jnp.bfloat16).reshape(row_count, key_heads * head_dim))
    value_send = pack_back(value_sum.reshape(row_count, key_heads * head_dim).astype(jnp.bfloat16))
    query_home, key_home, value_home = (
        lax.all_to_all(query_send, "ctx", split_axis=0, concat_axis=0, tiled=True),
        lax.all_to_all(key_send, "ctx", split_axis=0, concat_axis=0, tiled=True),
        lax.all_to_all(value_send, "ctx", split_axis=0, concat_axis=0, tiled=True),
    )
    slot_ids = jnp.arange(capacity, dtype=jnp.int32)
    slot_owner = (my_first + slot_ids) % ctx_size
    slot_pos = (
        slot_owner * per_peer
        + (slot_ids + my_lead) // ctx_size
        - (slot_owner < my_lead).astype(jnp.int32)
    )
    slot_pos = jnp.clip(slot_pos, 0, capacity - 1)
    slot_live = slot_ids < my_count

    def place_rows(source):
        picked = jnp.take(source, slot_pos, axis=0)
        return jnp.where(slot_live[:, None], picked, jnp.zeros((), source.dtype))

    return (place_rows(query_home)[None], place_rows(key_home)[None], place_rows(value_home)[None])


def solution(mesh):
    placed = (
        P(("groups", "dp"), None),
        P(("groups", "dp"), "ctx", "mp"),
        P(("groups", "dp"), "ctx", "mp"),
        P(("groups", "dp"), "ctx", "mp"),
        P(("groups", "dp"), "ctx", "mp"),
    )
    return jax.shard_map(
        body,
        mesh=mesh,
        in_specs=placed,
        out_specs=(
            P(("groups", "dp"), "ctx", "mp"),
            P(("groups", "dp"), "ctx", "mp"),
            P(("groups", "dp"), "ctx", "mp"),
        ),
        check_vma=False,
    )
```

profile of v0, /device:TPU:0, one launch (start us, length us, event | category | flops | bytes accessed | tf_op | source)
XLA Modules:
  0.0 283.1 jit_solution(3704470652849833624)
XLA Ops:
  11.6 1.9 gather_fusion.1
  15.5 6.3 %all-to-all-start = ((bf16[4,64,256]{2,1,0:T(8,128)(2,1)}), bf16[4,64,256]{2,1,0:T(8,128)(2,1)S(1)}, u32[]{:S(2)}, u32[]{:S(2)}) async-start(bf16[4,64,256]{2,1,0:T(8,128)(2,1)} %bitcast.16), calls=%async_computation | async-start | bytes 262144 | tf_op jit(solution)/shard_map/all_to_all | solution.py:83
  23.9 2.3 gather_fusion.9
  26.8 2.9 %select_select_fusion.2 = (bf16[256,2048]{1,0:T(8,128)(2,1)}, bf16[256,2048]{1,0:T(8,128)(2,1)}) fusion(bf16[256,2048]{1,0:T(8,128)(2,1)S(1)} %gather_fusion.5, pred[256]{0:T(512)(128)(4,1)S(1)} %get-tuple-element.320, pred[256]{0:T(512)(128)(4,1)S(1)} %get-tuple-element.321, bf16[256,2048]{1,0:T(8,128)(2,1)} %gather_fusion.9), kind=kLoop, calls=%fused_computation.63 | loop fusion | flops 2097152 | bytes 4194816 | tf_op jit(solution)/shard_map/jit(_where)/select_n | solution.py:69
  29.7 4.9 %compare_and_fusion.5 = (pred[256]{0:T(512)(128)(4,1)S(1)}, s32[256]{0:T(256)S(1)}, pred[256]{0:T(512)(128)(4,1)S(1)}) fusion(s32[]{:T(128)S(6)} %axis_index.15, s32[]{:T(128)} %bitcast.6, s32[]{:T(128)} %bitcast.5, s32[]{:T(128)} %bitcast.4, s32[]{:T(128)} %bitcast.3, s32[]{:T(128)} %bitcast.10, s32[]{:T(128)} %bitcast.9, s32[]{:T(128)} %bitcast.8, s32[]{:T(128)} %bitcast.7), kind=kLoop, calls=%fused_computation.221 | loop fusion | flops 18176 | bytes 1572 | tf_op jit(solution)/shard_map/jit(_take)/and | solution.py:203
  34.7 5.1 %all-to-all-start.2 = ((bf16[4,64,256]{2,1,0:T(8,128)(2,1)}), bf16[4,64,256]{2,1,0:T(8,128)(2,1)S(1)}, u32[]{:S(2)}, u32[]{:S(2)}) async-start(bf16[4,64,256]{2,1,0:T(8,128)(2,1)} %bitcast.39), calls=%async_computation.2 | async-start | bytes 262144 | tf_op jit(solution)/shard_map/all_to_all | solution.py:84
  39.8 5.9 %all-to-all-done.2 = bf16[4,64,256]{2,1,0:T(8,128)(2,1)S(1)} async-done(((bf16[4,64,256]{2,1,0:T(8,128)(2,1)}), bf16[4,64,256]{2,1,0:T(8,128)(2,1)S(1)}, u32[]{:S(2)}, u32[]{:S(2)}) %all-to-all-start.2) | async-done | bytes 131104 | tf_op jit(solution)/shard_map/all_to_all | solution.py:84
  45.7 3.5 %all-to-all-start.1 = ((bf16[4,64,2048]{2,1,0:T(8,128)(2,1)}), bf16[4,64,2048]{2,1,0:T(8,128)(2,1)S(1)}, u32[]{:S(2)}, u32[]{:S(2)}) async-start(bf16[4,64,2048]{2,1,0:T(8,128)(2,1)} %bitcast.23), calls=%async_computation.1 | async-start | bytes 2097152 | tf_op jit(solution)/shard_map/all_to_all | solution.py:82
  53.2 2.5 compare_and_fusion.1
  59.0 14.2 %all-to-all-done.1 = bf16[4,64,2048]{2,1,0:T(8,128)(2,1)S(1)} async-done(((bf16[4,64,2048]{2,1,0:T(8,128)(2,1)}), bf16[4,64,2048]{2,1,0:T(8,128)(2,1)S(1)}, u32[]{:S(2)}, u32[]{:S(2)}) %all-to-all-start.1) | async-done | bytes 1048608 | tf_op jit(solution)/shard_map/all_to_all | solution.py:82
  73.2 3.5 %all-to-all-start.3 = ((bf16[4,64,2048]{2,1,0:T(8,128)(2,1)}), bf16[4,64,2048]{2,1,0:T(8,128)(2,1)S(1)}, u32[]{:S(2)}, u32[]{:S(2)}) async-start(bf16[4,64,2048]{2,1,0:T(8,128)(2,1)} %bitcast.235), calls=%async_computation.3 | async-start | bytes 2097152 | tf_op jit(solution)/shard_map/all_to_all | solution.py:85
  77.7 1.5 gather_fusion.3
  81.4 28.2 %all_gather.6 = bf16[512,256]{1,0:T(8,128)(2,1)S(1)} all-gather(bf16[128,256]{1,0:T(8,128)(2,1)S(1)} %bitcast.265), channel_id=1, replica_groups=mesh['groups'=2,'ctx'=4,'dp'=2,'mp'=2] {'ctx'}, dimensions={0}, use_global_device_ids=true | all-gather | bytes 327680 | tf_op jit(solution)/shard_map/all_gather | solution.py:95
  112.0 14.6 %all_gather.7 = bf16[512,256]{1,0:T(8,128)(2,1)S(1)} all-gather(bf16[128,256]{1,0:T(8,128)(2,1)} %get-tuple-element.299), channel_id=1, replica_groups=mesh['groups'=2,'ctx'=4,'dp'=2,'mp'=2] {'ctx'}, dimensions={0}, use_global_device_ids=true | all-gather | bytes 327680 | tf_op jit(solution)/shard_map/all_gather | solution.py:96
  131.3 1.7 gather_fusion.6
  145.6 1.5 scatter.40
  147.1 2.0 fusion.94
  152.4 1.8 fusion.95
  155.0 2.1 fusion.28
  157.8 1.5 scatter.41
  160.3 2.0 fusion.38
  164.6 1.5 scatter.44
  171.1 2.3 fusion.32
  175.0 1.4 fusion.36
  193.7 11.1 %reduce-scatter.3.cloned.1.call-done = f32[128,1,256]{2,0,1:T(8,128)} async-done(((f32[128,4,256]{2,0,1:T(8,128)}), f32[128,1,256]{2,0,1:T(8,128)}) %reduce-scatter.3.cloned.1.call-update) | async-done | bytes 131088 | tf_op jit(solution)/shard_map/reduce_scatter | solution.py:213
  208.1 19.0 %reduce-scatter.5.cloned.1.call-done = f32[128,1,256]{2,0,1:T(8,128)} async-done(((f32[128,4,256]{2,0,1:T(8,128)}), f32[128,1,256]{2,0,1:T(8,128)}) %reduce-scatter.5.cloned.1.call-update) | async-done | bytes 131088 | tf_op jit(solution)/shard_map/reduce_scatter | solution.py:214
  230.0 3.3 %all-to-all-start.5 = ((bf16[4,64,256]{2,1,0:T(8,128)(2,1)}), bf16[4,64,256]{2,1,0:T(8,128)(2,1)S(1)}, u32[]{:S(2)}, u32[]{:S(2)}) async-start(bf16[4,64,256]{2,1,0:T(8,128)(2,1)} %bitcast.77), calls=%async_computation.6 | async-start | bytes 262144 | tf_op jit(solution)/shard_map/all_to_all | solution.py:221
  235.0 4.2 %all-to-all-done.5 = bf16[4,64,256]{2,1,0:T(8,128)(2,1)S(1)} async-done(((bf16[4,64,256]{2,1,0:T(8,128)(2,1)}), bf16[4,64,256]{2,1,0:T(8,128)(2,1)S(1)}, u32[]{:S(2)}, u32[]{:S(2)}) %all-to-all-start.5) | async-done | bytes 131104 | tf_op jit(solution)/shard_map/all_to_all | solution.py:221
  239.2 3.3 %all-to-all-start.6 = ((bf16[4,64,256]{2,1,0:T(8,128)(2,1)}), bf16[4,64,256]{2,1,0:T(8,128)(2,1)S(1)}, u32[]{:S(2)}, u32[]{:S(2)}) async-start(bf16[4,64,256]{2,1,0:T(8,128)(2,1)} %bitcast.89), calls=%async_computation.8 | async-start | bytes 262144 | tf_op jit(solution)/shard_map/all_to_all | solution.py:222
  244.4 4.1 %all-to-all-done.6 = bf16[4,64,256]{2,1,0:T(8,128)(2,1)S(1)} async-done(((bf16[4,64,256]{2,1,0:T(8,128)(2,1)}), bf16[4,64,256]{2,1,0:T(8,128)(2,1)S(1)}, u32[]{:S(2)}, u32[]{:S(2)}) %all-to-all-start.6) | async-done | bytes 131104 | tf_op jit(solution)/shard_map/all_to_all | solution.py:222
  248.5 3.5 %all-to-all-start.4 = ((bf16[4,64,2048]{2,1,0:T(8,128)(2,1)}), bf16[4,64,2048]{2,1,0:T(8,128)(2,1)S(1)}, u32[]{:S(2)}, u32[]{:S(2)}) async-start(bf16[4,64,2048]{2,1,0:T(8,128)(2,1)} %select_select_fusion.3), calls=%async_computation.4 | async-start | bytes 2097152 | tf_op jit(solution)/shard_map/all_to_all | solution.py:220
  257.1 16.6 %all-to-all-done.4 = bf16[4,64,2048]{2,1,0:T(8,128)(2,1)S(1)} async-done(((bf16[4,64,2048]{2,1,0:T(8,128)(2,1)}), bf16[4,64,2048]{2,1,0:T(8,128)(2,1)S(1)}, u32[]{:S(2)}, u32[]{:S(2)}) %all-to-all-start.4) | async-done | bytes 1048608 | tf_op jit(solution)/shard_map/all_to_all | solution.py:220
  (291 shorter events, 85.9 us)
Async XLA Ops:
  7.2 15.3 %copy-start = (bf16[1,256,2048]{2,1,0:T(8,128)(2,1)S(1)}, bf16[1,256,2048]{2,1,0:T(8,128)(2,1)}, u32[]{:S(2)}) copy-start(bf16[1,256,2048]{2,1,0:T(8,128)(2,1)} %param.60) | copy-start | bytes 3145732
  11.6 1.9 copy-start.3
  15.5 19.2 %all-to-all-start = ((bf16[4,64,256]{2,1,0:T(8,128)(2,1)}), bf16[4,64,256]{2,1,0:T(8,128)(2,1)S(1)}, u32[]{:S(2)}, u32[]{:S(2)}) async-start(bf16[4,64,256]{2,1,0:T(8,128)(2,1)} %bitcast.16), calls=%async_computation | async-start | bytes 262144 | tf_op jit(solution)/shard_map/all_to_all | solution.py:83
  34.6 17.4 %copy-start.69 = (pred[256]{0:T(512)(128)(4,1)}, pred[256]{0:T(512)(128)(4,1)S(1)}, u32[]{:S(2)}) copy-start(pred[256]{0:T(512)(128)(4,1)S(1)} %get-tuple-element.322) | copy-start | bytes 772
  34.6 18.0 %copy-start.67 = (pred[256]{0:T(512)(128)(4,1)}, pred[256]{0:T(512)(128)(4,1)S(1)}, u32[]{:S(2)}) copy-start(pred[256]{0:T(512)(128)(4,1)S(1)} %get-tuple-element.242) | copy-start | bytes 772
  34.7 11.0 %all-to-all-start.2 = ((bf16[4,64,256]{2,1,0:T(8,128)(2,1)}), bf16[4,64,256]{2,1,0:T(8,128)(2,1)S(1)}, u32[]{:S(2)}, u32[]{:S(2)}) async-start(bf16[4,64,256]{2,1,0:T(8,128)(2,1)} %bitcast.39), calls=%async_computation.2 | async-start | bytes 262144 | tf_op jit(solution)/shard_map/all_to_all | solution.py:84
  45.7 27.5 %all-to-all-start.1 = ((bf16[4,64,2048]{2,1,0:T(8,128)(2,1)}), bf16[4,64,2048]{2,1,0:T(8,128)(2,1)S(1)}, u32[]{:S(2)}, u32[]{:S(2)}) async-start(bf16[4,64,2048]{2,1,0:T(8,128)(2,1)} %bitcast.23), calls=%async_computation.1 | async-start | bytes 2097152 | tf_op jit(solution)/shard_map/all_to_all | solution.py:82
  73.2 59.8 %all-to-all-start.3 = ((bf16[4,64,2048]{2,1,0:T(8,128)(2,1)}), bf16[4,64,2048]{2,1,0:T(8,128)(2,1)S(1)}, u32[]{:S(2)}, u32[]{:S(2)}) async-start(bf16[4,64,2048]{2,1,0:T(8,128)(2,1)} %bitcast.235), calls=%async_computation.3 | async-start | bytes 2097152 | tf_op jit(solution)/shard_map/all_to_all | solution.py:85
  76.7 128.1 %reduce-scatter.3.cloned.1.call-start = ((), (), s32[]{:S(2)}) async-start(), calls=%async_computation.9 | async-start | bytes 655360 | tf_op jit(solution)/shard_map/reduce_scatter | solution.py:213
  77.7 57.0 %copy-start.24 = (f32[128,64]{1,0:T(8,128)}, f32[128,64]{1,0:T(8,128)S(1)}, u32[]{:S(2)}) copy-start(f32[128,64]{1,0:T(8,128)S(1)} %get-tuple-element.288) | copy-start | bytes 98308
  138.9 3.9 %copy-start.13 = (bf16[12,8,16,128]{3,2,1,0:T(8,128)(2,1)}, bf16[12,8,16,128]{3,2,1,0:T(8,128)(2,1)S(1)}, u32[]{:S(2)}) copy-start(bf16[12,8,16,128]{3,2,1,0:T(8,128)(2,1)S(1)} %copy.248) | copy-start | bytes 1179652
  139.0 2.2 copy-start.9
  140.3 2.5 copy-start.4
  141.2 2.8 copy-start.41
  147.1 2.0 copy-start.42
  147.1 2.7 copy-start.30
  152.4 2.5 copy-start.18
  152.4 1.9 copy-start.39
  152.4 2.5 copy-start.44
  154.9 2.1 copy-start.43
  155.0 2.1 copy-start.57
  155.0 2.1 copy-start.58
  160.2 2.0 copy-start.40
  160.2 2.0 copy-start.51
  160.2 2.0 copy-start.59
  160.3 2.0 copy-start.60
  175.0 2.2 copy-start.21
  182.6 44.4 %reduce-scatter.5.cloned.1.call-start = ((), (), s32[]{:S(2)}) async-start(), calls=%async_computation.10 | async-start | bytes 655360 | tf_op jit(solution)/shard_map/reduce_scatter | solution.py:214
  229.2 4.2 %copy-start.20 = (bf16[128,16,64]{2,0,1:T(8,128)(2,1)S(1)}, bf16[128,16,64]{2,0,1:T(8,128)(2,1)}, u32[]{:S(2)}) copy-start(bf16[128,16,64]{2,0,1:T(8,128)(2,1)} %get-tuple-element.251) | copy-start | bytes 786436
  230.0 9.2 %all-to-all-start.5 = ((bf16[4,64,256]{2,1,0:T(8,128)(2,1)}), bf16[4,64,256]{2,1,0:T(8,128)(2,1)S(1)}, u32[]{:S(2)}, u32[]{:S(2)}) async-start(bf16[4,64,256]{2,1,0:T(8,128)(2,1)} %bitcast.77), calls=%async_computation.6 | async-start | bytes 262144 | tf_op jit(solution)/shard_map/all_to_all | solution.py:221
  239.2 9.2 %all-to-all-start.6 = ((bf16[4,64,256]{2,1,0:T(8,128)(2,1)}), bf16[4,64,256]{2,1,0:T(8,128)(2,1)S(1)}, u32[]{:S(2)}, u32[]{:S(2)}) async-start(bf16[4,64,256]{2,1,0:T(8,128)(2,1)} %bitcast.89), calls=%async_computation.8 | async-start | bytes 262144 | tf_op jit(solution)/shard_map/all_to_all | solution.py:222
  248.5 25.2 %all-to-all-start.4 = ((bf16[4,64,2048]{2,1,0:T(8,128)(2,1)}), bf16[4,64,2048]{2,1,0:T(8,128)(2,1)S(1)}, u32[]{:S(2)}, u32[]{:S(2)}) async-start(bf16[4,64,2048]{2,1,0:T(8,128)(2,1)} %select_select_fusion.3), calls=%async_computation.4 | async-start | bytes 2097152 | tf_op jit(solution)/shard_map/all_to_all | solution.py:220
  (50 other events, 50.0 us)
Sparse Core Ops, SparseCore 0:
  182.7 22.0 reduce-scatter.2
  207.1 19.9 reduce-scatter.4
where the time goes:
time: 286 us; the launch traced here: 283 us
  waiting for transfers between devices  75.2 us (26%)
  local copies, waits for them, and re-layouts  65.8 us (23%)
  blocking collectives  42.7 us (15%)
  other arithmetic  38.7 us (14%)
  starting transfers between devices  29 us (10%)
  between operations  16.8 us (6%)
  matrix products  14.9 us (5%)
    all_gather x1, blocking collectives, body(): lax.all_gather(key_mine, 'ctx', axis=0, tiled=True)  28.2 us
    reduce_scatter x1, waiting for transfers between devices, body(): lax.psum_scatter(value_term, 'ctx', scatter_dimension=1, tiled=True)  19 us
    unnamed x156, local copies, waits for them, and re-layouts  16.6 us
    all_to_all x1, waiting for transfers between devices, body(): lax.all_to_all(query_send, 'ctx', split_axis=0, concat_axis=0, tiled=True)  16.6 us
    all_gather x1, blocking collectives, body(): lax.all_gather(own_value, 'ctx', axis=0, tiled=True)  14.6 us
    all_to_all x1, waiting for transfers between devices, body(): lax.all_to_all(pack_rows(queries[0]), 'ctx', split_axis=0, concat_axis=0,...  14.2 us
    reduce_scatter x1, waiting for transfers between devices, body(): lax.psum_scatter(key_term, 'ctx', scatter_dimension=1, tiled=True)  11.1 us
    gather x4, local copies, waits for them, and re-layouts, pack_rows(): picked = jnp.take(source, send_index, axis=0)  6.76 us
  transfers between devices with their start and end apart: 9, of which 7 were waited for; matrix products, arithmetic and copies ran while one was open for 18% of the time, Pallas kernels for 0%

commit v1 on v0

v1 whole, which is shorter than its diff:
```python
import functools
import math

import jax
import jax.numpy as jnp
from jax import lax
from jax.experimental import pallas as pl
from jax.experimental.pallas import tpu as pltpu
from jax.sharding import PartitionSpec as P

HEAD_DIM = 128
TOK_SHARD = 1024
ROPE_BASE = 500000.0
SCORE_SCALE = 1.0 / math.sqrt(HEAD_DIM)
EXP2_SCALE = SCORE_SCALE * math.log2(math.e)
HIDDEN = -1e30


def rope_tables(seq_pos):
    half_dim = HEAD_DIM // 2
    ladder = jnp.arange(half_dim).astype(jnp.float32)
    inverse_freq = jnp.exp(ladder * (-2.0 * math.log(ROPE_BASE) / HEAD_DIM))
    angles = seq_pos.astype(jnp.float32)[:, None] * inverse_freq[None, :]
    cos_part, sin_part = jnp.cos(angles), jnp.sin(angles)
    return (
        jnp.concatenate([cos_part, cos_part], axis=-1),
        jnp.concatenate([-sin_part, sin_part], axis=-1),
    )


def rotate(field, cos_full, sin_full, rotation):
    rows, width = field.shape
    half_dim = HEAD_DIM // 2
    heads = field.reshape(rows, width // HEAD_DIM, HEAD_DIM).astype(jnp.float32)
    swapped = jnp.concatenate([heads[..., half_dim:], heads[..., :half_dim]], axis=-1)
    turned = heads * cos_full[:, None, :] + swapped * (rotation * sin_full[:, None, :])
    return turned.reshape(rows, width)


def dot(left, right, contract):
    return lax.dot_general(left, right, (contract, ((), ())), preferred_element_type=jnp.float32)


def attention_kernel(
    hops,
    key_heads,
    group_size,
    step_heads,
    meta_ref,
    cos_ref,
    sin_ref,
    query_ref,
    grad_ref,
    *refs,
):
    blocks = refs[:hops]
    dq_ref, dkv_ref, key_ref, value_ref, key_t_ref, bias_ref = refs[hops:]
    slots = query_ref.shape[0]
    routed = dkv_ref.shape[0]
    width = key_heads * HEAD_DIM
    my_first, my_count = meta_ref[hops], meta_ref[hops + 1]

    key_rank = lax.broadcasted_iota(jnp.int32, (routed, slots), 0)
    slot_id = lax.broadcasted_iota(jnp.int32, (routed, slots), 1)
    gap = key_rank - slot_id
    ranked = None
    for hop in range(hops):
        named = (gap == meta_ref[hop]) & (slot_id < meta_ref[hops + 2 + hop])
        term = dot(named.astype(jnp.float32).astype(jnp.bfloat16), blocks[hop][...], ((1,), (0,)))
        ranked = term if ranked is None else ranked + term
    key_ref[...] = ranked[:, :width].astype(jnp.bfloat16)
    value_ref[...] = ranked[:, width:].astype(jnp.bfloat16)
    for head in range(key_heads):
        key_t_ref[head] = ranked[:, head * HEAD_DIM : (head + 1) * HEAD_DIM].T.astype(jnp.bfloat16)
    bias_ref[...] = jnp.where(gap <= my_first, 0.0, HIDDEN)
    dkv_ref[...] = jnp.zeros_like(dkv_ref)
    live = lax.broadcasted_iota(jnp.int32, (slots, HEAD_DIM), 0) < my_count

    for key_head in range(key_heads):
        lanes = slice(key_head * HEAD_DIM, (key_head + 1) * HEAD_DIM)
        value_lanes = slice(width + key_head * HEAD_DIM, width + (key_head + 1) * HEAD_DIM)

        def step(index, carry):
            queries, grads, probs, score_grads = [], [], [], []
            for part in range(step_heads):
                head = key_head * group_size + index * step_heads + part
                columns = pl.ds(pl.multiple_of(head * HEAD_DIM, HEAD_DIM), HEAD_DIM)
                query = query_ref[:, columns].astype(jnp.float32)
                query = query * cos_ref[...] + pltpu.roll(query, HEAD_DIM // 2, 1) * sin_ref[...]
                query = jnp.where(live, query, 0.0).astype(jnp.bfloat16)
                grad = jnp.where(live, grad_ref[:, columns].astype(jnp.float32), 0.0)
                grad = grad.astype(jnp.bfloat16)
                scores = dot(key_ref[:, lanes], query, ((1,), (1,))) + bias_ref[...]
                prob_grad = dot(value_ref[:, lanes], grad, ((1,), (1,)))
                peak = jnp.max(scores, axis=0, keepdims=True)
                weights = jnp.exp2((scores - peak) * EXP2_SCALE)
                inverse = 1.0 / jnp.sum(weights, axis=0, keepdims=True)
                delta = jnp.sum(weights * prob_grad, axis=0, keepdims=True) * inverse
                prob = weights * inverse
                score_grad = (prob * (prob_grad - delta)).astype(jnp.bfloat16)
                turned = dot(key_t_ref[key_head], score_grad, ((1,), (0,))) * SCORE_SCALE
                turned = turned.T
                turned = turned * cos_ref[...] - pltpu.roll(turned, HEAD_DIM // 2, 1) * sin_ref[...]
                dq_ref[:, columns] = turned.astype(jnp.bfloat16)
                queries.append(query)
                grads.append(grad)
                probs.append(prob.astype(jnp.bfloat16))
                score_grads.append(score_grad)
            dkv_ref[:, lanes] += dot(
                jnp.concatenate(score_grads, axis=1),
                jnp.concatenate(queries, axis=0),
                ((1,), (0,)),
            )
            dkv_ref[:, value_lanes] += dot(
                jnp.concatenate(probs, axis=1), jnp.concatenate(grads, axis=0), ((1,), (0,))
            )
            return carry

        lax.fori_loop(0, group_size // step_heads, step, 0)
    dkv_ref[:, :width] = dkv_ref[:, :width] * SCORE_SCALE


def attention(meta, cos_full, sin_full, queries, out_grad, blocks, routed):
    slots, width = blocks[0].shape
    key_heads = width // HEAD_DIM // 2
    heads = queries.shape[1] // HEAD_DIM
    step_heads = 2 if routed <= 512 else 1
    whole = pl.BlockSpec(memory_space=pltpu.VMEM)
    flops = 10 * slots * routed * queries.shape[1]
    return pl.pallas_call(
        functools.partial(
            attention_kernel, len(blocks), key_heads, heads // key_heads, step_heads
        ),
        out_shape=(
            jax.ShapeDtypeStruct(queries.shape, jnp.bfloat16),
            jax.ShapeDtypeStruct((routed, width), jnp.float32),
        ),
        in_specs=[pl.BlockSpec(memory_space=pltpu.SMEM)] + [whole] * (4 + len(blocks)),
        out_specs=(whole, whole),
        scratch_shapes=[
            pltpu.VMEM((routed, width // 2), jnp.bfloat16),
            pltpu.VMEM((routed, width // 2), jnp.bfloat16),
            pltpu.VMEM((key_heads, HEAD_DIM, routed), jnp.bfloat16),
            pltpu.VMEM((routed, slots), jnp.float32),
        ],
        compiler_params=pltpu.CompilerParams(vmem_limit_bytes=48 * 1024 * 1024),
        cost_estimate=pl.CostEstimate(
            flops=flops, bytes_accessed=8 * 1024 * 1024, transcendentals=flops // 1280
        ),
        name="attention_backward",
    )(meta, cos_full, sin_full, queries, out_grad, *blocks)


def body(positions, queries, keys, values, out_grad):
    ctx_size = lax.axis_size("ctx")
    ctx_rank = lax.axis_index("ctx")
    seq_pos = positions[0]
    routed = seq_pos.shape[0]
    row_count = routed // ctx_size
    slots = queries.shape[1]
    width = keys.shape[2]
    shard_of = seq_pos // TOK_SHARD
    my_first = jnp.sum((shard_of < ctx_rank).astype(jnp.int32))
    my_count = jnp.sum((shard_of == ctx_rank).astype(jnp.int32))
    padded_pos = jnp.concatenate([seq_pos, jnp.zeros((slots,), jnp.int32)])
    cos_full, sin_full = rope_tables(lax.dynamic_slice(padded_pos, (my_first,), (slots,)))

    own = jnp.concatenate(
        [rotate(keys[0], cos_full, sin_full, 1.0).astype(jnp.bfloat16), values[0]], axis=1
    )
    blocks = [own]
    forward = [(shard, shard + 1) for shard in range(ctx_size - 1)]
    for hop in range(ctx_size - 1):
        blocks.append(lax.ppermute(blocks[-1], "ctx", forward[hop:]))
    blocks = blocks[::-1]
    sources = ctx_rank - jnp.arange(ctx_size - 1, -1, -1, dtype=jnp.int32)
    starts = jnp.sum((shard_of[None, :] < sources[:, None]).astype(jnp.int32), axis=1)
    counts = jnp.sum((shard_of[None, :] == sources[:, None]).astype(jnp.int32), axis=1)
    meta = jnp.concatenate([starts, my_first[None], my_count[None], counts])
    query_grad, terms = attention(
        meta, cos_full, sin_full, queries[0], out_grad[0], blocks, routed
    )

    total = lax.psum_scatter(terms, "ctx", scatter_dimension=0, tiled=True)
    owned_pos = lax.dynamic_slice(seq_pos, (ctx_rank * row_count,), (row_count,))
    cos_owned, sin_owned = rope_tables(owned_pos)
    owned = jnp.concatenate(
        [rotate(total[:, :width], cos_owned, sin_owned, -1.0), total[:, width:]], axis=1
    ).astype(jnp.bfloat16)
    ranked = lax.all_gather(owned, "ctx", axis=0, tiled=True)
    padded = jnp.concatenate([ranked, jnp.zeros((slots, 2 * width), jnp.bfloat16)], axis=0)
    placed = lax.dynamic_slice(padded, (my_first, 0), (slots, 2 * width))
    placed = jnp.where(
        jnp.arange(slots)[:, None] < my_count, placed, jnp.zeros((), jnp.bfloat16)
    )
    return (query_grad[None], placed[None, :, :width], placed[None, :, width:])


def solution(mesh):
    split = P(("groups", "dp"), "ctx", "mp")
    return jax.shard_map(
        body,
        mesh=mesh,
        in_specs=(P(("groups", "dp"), None), split, split, split, split),
        out_specs=(split, split, split),
        check_vma=False,
    )
```

time: 286 us -> 112 us (0.39)
  local copies, waits for them, and re-layouts: 65.8 us -> 5.26 us
  other arithmetic: 38.7 us -> 4.86 us
  waiting for transfers between devices: 75.2 us -> 48.2 us
  blocking collectives: 42.7 us -> 16.1 us
  starting transfers between devices: 29 us -> 6.32 us
  matrix products: 14.9 us -> 0 us
  Pallas kernels: 0 us -> 14.9 us
    all_to_all x7 -> x0, waiting for transfers between devices: 45.1 us -> none  [the longest x1 16.6 us: body(): lax.all_to_all(query_send, 'ctx', split_axis=0, concat_axis=0, tiled=True)]
    all_to_all x7 -> x0, starting transfers between devices: 28.6 us -> none  [the longest x1 6.32 us: body(): lax.all_to_all(pack_rows(keys[0]), 'ctx', split_axis=0, concat_axis=0, ti...]
    all_gather x2 -> x1, blocking collectives: 42.7 us -> 16.1 us  [body(): ranked = lax.all_gather(owned, 'ctx', axis=0, tiled=True)]
    gather x18 -> x0, local copies, waits for them, and re-layouts: 22.9 us -> none  [the longest x4 6.76 us: pack_rows(): picked = jnp.take(source, send_index, axis=0)]
    dot_general x20 -> x0, matrix products: 14.9 us -> none  [the longest x4 6.54 us: block_scores(): jnp.einsum('ikgd,skd->kgis', grad_view[row_start:], value_part, preferred...]
    pallas_call x0 -> x1, Pallas kernels: none -> 14.9 us  [attention(): pl.pallas_call(functools.partial(attention_kernel, len(blocks), key_heads...]
    unnamed x156 -> x12, local copies, waits for them, and re-layouts: 16.6 us -> 1.85 us
    reduce_scatter x2 -> x1, waiting for transfers between devices: 30.1 us -> 42.7 us  [body(): total = lax.psum_scatter(terms, 'ctx', scatter_dimension=0, tiled=True)]
  transfers between devices with their start and end apart: 9 -> 4, of which waited for: 7 -> 2; matrix products, arithmetic and copies ran while one was open for 18% -> 2% of each run, Pallas kernels for 0% -> 0%
where the time goes in v1:
time: 112 us
  waiting for transfers between devices  48.2 us (43%)
  between operations  16.2 us (14%)
  blocking collectives  16.1 us (14%)
  Pallas kernels  14.9 us (13%)
  starting transfers between devices  6.32 us (6%)
  local copies, waits for them, and re-layouts  5.26 us (5%)
  other arithmetic  4.86 us (4%)
    reduce_scatter x1, waiting for transfers between devices, body(): total = lax.psum_scatter(terms, 'ctx', scatter_dimension=0, tiled=True)  42.7 us
    all_gather x1, blocking collectives, body(): ranked = lax.all_gather(owned, 'ctx', axis=0, tiled=True)  16.1 us
    pallas_call x1, Pallas kernels, attention(): pl.pallas_call(functools.partial(attention_kernel, len(blocks), key_heads...  14.9 us
    ppermute x3, starting transfers between devices, body(): blocks.append(lax.ppermute(blocks[-1], 'ctx', forward[hop:]))  6.29 us
    ppermute x3, waiting for transfers between devices, body(): blocks.append(lax.ppermute(blocks[-1], 'ctx', forward[hop:]))  5.54 us
  transfers between devices with their start and end apart: 4, of which 2 were waited for; matrix products, arithmetic and copies ran while one was open for 2% of the time, Pallas kernels for 0%

profile of v1, /device:TPU:0, one launch (start us, length us, event | category | flops | bytes accessed | tf_op | source)
XLA Modules:
  0.0 111.8 jit_solution(6103581459144877966)
XLA Ops:
  7.2 0.0 reduce-scatter.2.cloned.1.call-start
  7.2 0.7 copy-done.5
  7.9 0.6 convert_reduce_fusion.3
  10.5 0.1 fusion.7
  10.6 1.0 reshape.86
  11.6 0.3 fusion.8
  12.0 0.5 fusion.3
  12.5 0.1 pad_maximum_fusion.1
  12.7 0.4 maximum_multiply_fusion
  13.0 0.1 mul.112
  13.1 0.4 copy-done.2
  13.6 0.0 copy-done.4
  13.6 4.9 %collective-permute-start = (bf16[256,512]{1,0:T(8,128)(2,1)S(1)}, bf16[256,512]{1,0:T(8,128)(2,1)S(1)}, u32[]{:S(2)}, u32[]{:S(2)}) collective-permute-start(bf16[256,512]{1,0:T(8,128)(2,1)S(1)} %pad_maximum_fusion.refs_3_), channel_id=1, source_target_pairs={{0,4},{4,8},{8,12},{1,5},{5,9},{9,13},{2,6},{6,10},{10,14},{3,7},{... | collective-permute-start | bytes 786440 | tf_op jit(solution)/shard_map/ppermute | solution.py:174
  18.6 5.5 %collective-permute-done.refs_2_ = bf16[256,512]{1,0:T(8,128)(2,1)S(1)} collective-permute-done((bf16[256,512]{1,0:T(8,128)(2,1)S(1)}, bf16[256,512]{1,0:T(8,128)(2,1)S(1)}, u32[]{:S(2)}, u32[]{:S(2)}) %collective-permute-start) | collective-permute-done | bytes 262176 | tf_op jit(solution)/shard_map/ppermute | solution.py:174
  24.1 0.7 collective-permute-start.1
  24.8 0.7 collective-permute-start.2
  25.5 0.2 convert_reduce_fusion.1
  25.7 1.4 %pad_add_fusion.meta_ref = s32[10]{0:T(128)S(1)} fusion(s32[4]{0:T(128)S(1)} %get-tuple-element.8, s32[1]{0:T(128)} %bitcast.3, s32[1]{0:T(128)} %bitcast.2, s32[4]{0:T(128)S(1)} %get-tuple-element.7), kind=kLoop, calls=%fused_computation.43 | loop fusion | flops 30 | bytes 80 | tf_op jit(solution)/shard_map/concatenate | solution.py:179
  27.1 14.9 %attention_backward.1 = (bf16[256,2048]{1,0:T(8,128)(2,1)}, f32[512,512]{1,0:T(8,128)}) custom-call(s32[10]{0:T(128)S(1)} %pad_add_fusion.meta_ref, f32[256,128]{1,0:T(8,128)S(1)} %get-tuple-element.23.cos_ref, f32[256,128]{1,0:T(8,128)S(1)} %get-tuple-element.24.sin_ref, bf16[256,2048]{1,0:T(8,128)(2,1)S(1)} %bitcast.36, bf16[256,2048]{1,0:T(8,128)(2,1)S(1)} %bitcast.37, ...), custom_call_target="tpu_custom_call" | custom-call | flops 2684354560 | bytes 8388608 | tf_op jit(solution)/shard_map/attention_backward/pallas_call | solution.py:130
  42.0 0.0 reduce-scatter.2.cloned.1.call-update
  42.0 0.7 iota_compare_fusion
  42.7 0.3 multiply_cosine_fusion.1
  43.0 0.1 pad_maximum_fusion.4
  43.1 42.7 %reduce-scatter.2.cloned.1.call-done = f32[128,512]{1,0:T(8,128)} async-done(((f32[512,512]{1,0:T(8,128)}), f32[128,512]{1,0:T(8,128)}) %reduce-scatter.2.cloned.1.call-update) | async-done | bytes 262160 | tf_op jit(solution)/shard_map/reduce_scatter | solution.py:184
  85.8 0.9 slice-done
  86.7 0.1 reshape.84
  86.8 0.2 fusion.9
  87.0 0.2 maximum_multiply_fusion.1
  87.2 0.7 copy-done.3
  88.0 16.1 %all_gather.3 = bf16[512,512]{1,0:T(8,128)(2,1)S(1)} all-gather(bf16[128,512]{1,0:T(8,128)(2,1)S(1)} %pad_maximum_fusion.3), channel_id=1, replica_groups=mesh['groups'=2,'ctx'=4,'dp'=2,'mp'=2] {'ctx'}, dimensions={0}, use_global_device_ids=true | all-gather | bytes 655360 | tf_op jit(solution)/shard_map/all_gather | solution.py:190
  104.1 0.1 fusion
  104.2 0.7 slice_bitcast_fusion
  (21 shorter events, 0.2 us)
Async XLA Ops:
  7.2 78.6 %reduce-scatter.2.cloned.1.call-start = ((), (), s32[]{:S(2)}) async-start(), calls=%async_computation.1 | async-start | bytes 1310720 | tf_op jit(solution)/shard_map/reduce_scatter | solution.py:184
  7.2 0.7 copy-start.5
  12.6 0.9 copy-start.2
  12.7 1.0 copy-start.4
  12.7 14.4 %copy-start.1 = (bf16[1,256,2048]{2,1,0:T(8,128)(2,1)S(1)}, bf16[1,256,2048]{2,1,0:T(8,128)(2,1)}, u32[]{:S(2)}) copy-start(bf16[1,256,2048]{2,1,0:T(8,128)(2,1)} %param.9) | copy-start | bytes 3145732
  13.0 14.1 %copy-start = (bf16[1,256,2048]{2,1,0:T(8,128)(2,1)S(1)}, bf16[1,256,2048]{2,1,0:T(8,128)(2,1)}, u32[]{:S(2)}) copy-start(bf16[1,256,2048]{2,1,0:T(8,128)(2,1)} %param.6) | copy-start | bytes 3145732
  13.6 10.5 %collective-permute-start = (bf16[256,512]{1,0:T(8,128)(2,1)S(1)}, bf16[256,512]{1,0:T(8,128)(2,1)S(1)}, u32[]{:S(2)}, u32[]{:S(2)}) collective-permute-start(bf16[256,512]{1,0:T(8,128)(2,1)S(1)} %pad_maximum_fusion.refs_3_), channel_id=1, source_target_pairs={{0,4},{4,8},{8,12},{1,5},{5,9},{9,13},{2,6},{6,10},{10,14},{3,7},{... | collective-permute-start | bytes 786440 | tf_op jit(solution)/shard_map/ppermute | solution.py:174
  24.1 0.7 collective-permute-start.1
  24.8 2.3 %collective-permute-start.2 = (bf16[256,512]{1,0:T(8,128)(2,1)S(1)}, bf16[256,512]{1,0:T(8,128)(2,1)S(1)}, u32[]{:S(2)}, u32[]{:S(2)}) collective-permute-start(bf16[256,512]{1,0:T(8,128)(2,1)S(1)} %collective-permute-done.1.refs_1_), channel_id=1, source_target_pairs={{8,12},{9,13},{10,14},{11,15},{24,28},{25,29},{26,30},{27,31}} | collective-permute-start | bytes 786440 | tf_op jit(solution)/shard_map/ppermute | solution.py:174
  85.8 0.9 slice-start
  87.0 1.0 copy-start.3
Sparse Core Ops, SparseCore 0:
  42.1 43.6 reduce-scatter.1

commit v2 on v1

v2 whole, which is shorter than its diff:
```python
import functools
import math

import jax
import jax.numpy as jnp
import numpy as np
from jax import lax
from jax.experimental import pallas as pl
from jax.experimental.pallas import tpu as pltpu
from jax.sharding import PartitionSpec as P

HEAD_DIM = 128
HALF_DIM = HEAD_DIM // 2
TOK_SHARD = 1024
ROPE_BASE = 500000.0
SCORE_SCALE = 1.0 / math.sqrt(HEAD_DIM)
EXP2_SCALE = SCORE_SCALE * math.log2(math.e)
HIDDEN = -1e30
ALIGN = 16
VMEM_LIMIT = 48 * 1024 * 1024

VMEM = pl.BlockSpec(memory_space=pltpu.VMEM)
SMEM = pl.BlockSpec(memory_space=pltpu.SMEM)


def dot(left, right, contract):
    return lax.dot_general(left, right, (contract, ((), ())), preferred_element_type=jnp.float32)


def turn(field, cos_full, sin_full):
    return field * cos_full + pltpu.roll(field, HALF_DIM, 1) * sin_full


def turn_back(field, cos_full, sin_full):
    return field * cos_full - pltpu.roll(field, HALF_DIM, 1) * sin_full


def rope_rows():
    ladder = np.arange(HALF_DIM, dtype=np.float32)
    exponent = ladder * np.float32(-2.0 * math.log(ROPE_BASE) / HEAD_DIM)
    freq = np.exp(exponent.astype(np.float64)).astype(np.float32)
    sign = np.repeat(np.array([-1.0, 1.0], np.float32), HALF_DIM)
    return np.stack([np.concatenate([freq, freq]), sign])


def prepare_kernel(ctx_size, rows_ref, pos_ref, keys_ref, meta_ref, cos_ref, sin_ref, *key_refs):
    me = lax.axis_index("ctx")
    slots = keys_ref.shape[0]
    pos = pos_ref[...]
    shard_of = pos // TOK_SHARD
    start = jnp.int32(0)
    first = jnp.int32(0)
    my_first = jnp.int32(0)
    my_start = jnp.int32(0)
    my_count = jnp.int32(0)
    for shard in range(ctx_size):
        count = jnp.sum(jnp.where(shard_of == shard, 1.0, 0.0)).astype(jnp.int32)
        meta_ref[shard] = start
        meta_ref[ctx_size + shard] = count
        mine = me == shard
        my_first = jnp.where(mine, first, my_first)
        my_start = jnp.where(mine, start, my_start)
        my_count = jnp.where(mine, count, my_count)
        first = first + count
        start = start + (count + ALIGN - 1) // ALIGN * ALIGN
    meta_ref[2 * ctx_size] = my_start
    meta_ref[2 * ctx_size + 1] = my_count
    meta_ref[2 * ctx_size + 2] = me

    shape = (slots, pos.shape[1])
    gap = lax.broadcasted_iota(jnp.int32, shape, 1) - lax.broadcasted_iota(jnp.int32, shape, 0)
    named = jnp.where(gap == my_first, pos.astype(jnp.float32), 0.0)
    angles = jnp.sum(named, axis=1, keepdims=True) * rows_ref[0:1, :]
    cos_full = jnp.cos(angles)
    sin_full = jnp.sin(angles) * rows_ref[1:2, :]
    cos_ref[...] = cos_full
    sin_ref[...] = sin_full
    for head, key_ref in enumerate(key_refs):
        key = keys_ref[:, head * HEAD_DIM : (head + 1) * HEAD_DIM].astype(jnp.float32)
        key = turn(key, cos_full, sin_full).astype(jnp.bfloat16)
        for shard in range(ctx_size):
            key_ref[shard] = key


def prepare(positions, keys, ctx_size):
    slots, width = keys.shape
    key_heads = width // HEAD_DIM
    table = jax.ShapeDtypeStruct((slots, HEAD_DIM), jnp.float32)
    sent = jax.ShapeDtypeStruct((ctx_size, slots, HEAD_DIM), jnp.bfloat16)
    return pl.pallas_call(
        functools.partial(prepare_kernel, ctx_size),
        out_shape=(
            jax.ShapeDtypeStruct((2 * ctx_size + 3,), jnp.int32),
            table,
            table,
            *[sent] * key_heads,
        ),
        in_specs=[VMEM] * 3,
        out_specs=(SMEM,) + (VMEM,) * (2 + key_heads),
        compiler_params=pltpu.CompilerParams(vmem_limit_bytes=VMEM_LIMIT),
        name="prepare",
    )(jnp.asarray(rope_rows()), positions, keys)


def attention_kernel(
    ctx_size,
    step_heads,
    meta_ref,
    cos_ref,
    sin_ref,
    query_ref,
    grad_ref,
    key_all_ref,
    value_all_ref,
    *refs,
):
    dq_ref, terms_ref, own_ref, key_ref, value_ref, key_t_ref, bias_ref, acc_ref = refs[-8:]
    slots = query_ref.shape[0]
    span = bias_ref.shape[0]
    my_start, my_count, me = [meta_ref[2 * ctx_size + item] for item in range(3)]
    starts = [pl.multiple_of(meta_ref[shard], ALIGN) for shard in range(ctx_size)]

    key_ref[...] = jnp.zeros_like(key_ref)
    value_ref[...] = jnp.zeros_like(value_ref)
    for shard in range(ctx_size):
        key_ref[pl.ds(starts[shard], slots), :] = key_all_ref[shard]
        value_ref[pl.ds(starts[shard], slots), :] = value_all_ref[shard]
    key_t_ref[...] = key_ref[:span, :].astype(jnp.float32).T.astype(jnp.bfloat16)

    place = lax.broadcasted_iota(jnp.int32, (span, slots), 0)
    slot_id = lax.broadcasted_iota(jnp.int32, (span, slots), 1)
    seen = (place >= my_start) & (place - slot_id <= my_start)
    for shard in range(ctx_size):
        count = jnp.where(shard < me, meta_ref[ctx_size + shard], 0)
        seen = seen | ((place >= starts[shard]) & (place < starts[shard] + count))
    bias_ref[...] = jnp.where(seen, 0.0, HIDDEN)
    acc_ref[...] = jnp.zeros_like(acc_ref)
    live = lax.broadcasted_iota(jnp.int32, (slots, HEAD_DIM), 0) < my_count

    def step(index, carry):
        queries, grads, probs, score_grads = [], [], [], []
        for part in range(step_heads):
            head = index * step_heads + part
            columns = pl.ds(pl.multiple_of(head * HEAD_DIM, HEAD_DIM), HEAD_DIM)
            query = turn(query_ref[:, columns].astype(jnp.float32), cos_ref[...], sin_ref[...])
            query = jnp.where(live, query, 0.0).astype(jnp.bfloat16)
            grad = jnp.where(live, grad_ref[:, columns].astype(jnp.float32), 0.0)
            grad = grad.astype(jnp.bfloat16)
            scores = dot(key_ref[:span, :], query, ((1,), (1,))) + bias_ref[...]
            prob_grad = dot(value_ref[:span, :], grad, ((1,), (1,)))
            peak = jnp.max(scores, axis=0, keepdims=True)
            weights = jnp.exp2((scores - peak) * EXP2_SCALE)
            inverse = 1.0 / jnp.sum(weights, axis=0, keepdims=True)
            delta = jnp.sum(weights * prob_grad, axis=0, keepdims=True) * inverse
            prob = weights * inverse
            score_grad = (prob * (prob_grad - delta)).astype(jnp.bfloat16)
            turned = (dot(key_t_ref[...], score_grad, ((1,), (0,))) * SCORE_SCALE).T
            turned = turn_back(turned, cos_ref[...], sin_ref[...])
            dq_ref[:, columns] = turned.astype(jnp.bfloat16)
            queries.append(query)
            grads.append(grad)
            probs.append(prob.astype(jnp.bfloat16))
            score_grads.append(score_grad)
        acc_ref[:span, :HEAD_DIM] += dot(
            jnp.concatenate(score_grads, axis=1), jnp.concatenate(queries, axis=0), ((1,), (0,))
        )
        acc_ref[:span, HEAD_DIM:] += dot(
            jnp.concatenate(probs, axis=1), jnp.concatenate(grads, axis=0), ((1,), (0,))
        )
        return carry

    heads = query_ref.shape[1] // HEAD_DIM
    lax.fori_loop(0, heads // step_heads, step, 0)
    acc_ref[:span, :HEAD_DIM] = acc_ref[:span, :HEAD_DIM] * SCORE_SCALE
    own_ref[...] = acc_ref[pl.ds(pl.multiple_of(my_start, ALIGN), slots), :]
    for shard in range(ctx_size):
        terms_ref[shard] = acc_ref[pl.ds(starts[shard], slots), :].astype(jnp.bfloat16)


def attention(meta, cos_full, sin_full, queries, out_grad, key_all, value_all, routed, head, dq):
    ctx_size, slots, _ = key_all.shape
    width = queries.shape[1] // (value_all.shape[2] // HEAD_DIM)
    span = routed + ctx_size * ALIGN
    columns = pl.BlockSpec((slots, width), lambda step: (0, head))
    whole = lambda *shape: pl.BlockSpec(shape, lambda step: (0,) * len(shape))
    operands = [meta, cos_full, sin_full, queries, out_grad, key_all, value_all]
    in_specs = [
        SMEM,
        whole(slots, HEAD_DIM),
        whole(slots, HEAD_DIM),
        columns,
        columns,
        whole(*key_all.shape),
        pl.BlockSpec((ctx_size, slots, HEAD_DIM), lambda step: (0, 0, head)),
    ]
    aliases = {}
    if dq is not None:
        aliases = {len(operands): 0}
        operands.append(dq)
        in_specs.append(pl.BlockSpec(memory_space=pl.ANY))
    flops = 10 * slots * span * width
    return pl.pallas_call(
        functools.partial(attention_kernel, ctx_size, 4 if routed <= 512 else 1),
        grid=(1,),
        out_shape=(
            jax.ShapeDtypeStruct(queries.shape, jnp.bfloat16),
            jax.ShapeDtypeStruct((ctx_size, slots, 2 * HEAD_DIM), jnp.bfloat16),
            jax.ShapeDtypeStruct((slots, 2 * HEAD_DIM), jnp.float32),
        ),
        in_specs=in_specs,
        out_specs=(columns, whole(ctx_size, slots, 2 * HEAD_DIM), whole(slots, 2 * HEAD_DIM)),
        scratch_shapes=[
            pltpu.VMEM((span + slots, HEAD_DIM), jnp.bfloat16),
            pltpu.VMEM((span + slots, HEAD_DIM), jnp.bfloat16),
            pltpu.VMEM((HEAD_DIM, span), jnp.bfloat16),
            pltpu.VMEM((span, slots), jnp.float32),
            pltpu.VMEM((span + slots, 2 * HEAD_DIM), jnp.float32),
        ],
        input_output_aliases=aliases,
        compiler_params=pltpu.CompilerParams(vmem_limit_bytes=VMEM_LIMIT),
        cost_estimate=pl.CostEstimate(
            flops=flops, bytes_accessed=4 * 1024 * 1024, transcendentals=flops // 1280
        ),
        name="attention_backward",
    )(*operands)


def finish_kernel(ctx_size, key_heads, meta_ref, cos_ref, sin_ref, *refs):
    owns, terms = refs[:key_heads], refs[key_heads : 2 * key_heads]
    key_grad_ref, value_grad_ref = refs[2 * key_heads :]
    my_count, me = meta_ref[2 * ctx_size + 1], meta_ref[2 * ctx_size + 2]
    slots = cos_ref.shape[0]
    live = lax.broadcasted_iota(jnp.int32, (slots, HEAD_DIM), 0) < my_count
    for head in range(key_heads):
        total = owns[head][...]
        for shard in range(ctx_size):
            total += jnp.where(shard > me, terms[head][shard].astype(jnp.float32), 0.0)
        columns = slice(head * HEAD_DIM, (head + 1) * HEAD_DIM)
        turned = turn_back(total[:, :HEAD_DIM], cos_ref[...], sin_ref[...])
        key_grad_ref[:, columns] = jnp.where(live, turned, 0.0).astype(jnp.bfloat16)
        value_grad_ref[:, columns] = jnp.where(live, total[:, HEAD_DIM:], 0.0).astype(jnp.bfloat16)


def finish(meta, cos_full, sin_full, owns, terms):
    ctx_size, slots, _ = terms[0].shape
    key_heads = len(owns)
    grad = jax.ShapeDtypeStruct((slots, key_heads * HEAD_DIM), jnp.bfloat16)
    return pl.pallas_call(
        functools.partial(finish_kernel, ctx_size, key_heads),
        out_shape=(grad, grad),
        in_specs=[SMEM] + [VMEM] * (2 + 2 * key_heads),
        out_specs=(VMEM, VMEM),
        compiler_params=pltpu.CompilerParams(vmem_limit_bytes=VMEM_LIMIT),
        name="finish",
    )(meta, cos_full, sin_full, *owns, *terms)


def exchange(chunks):
    return lax.all_to_all(chunks, "ctx", split_axis=0, concat_axis=0, tiled=True)


def body(positions, queries, keys, values, out_grad):
    ctx_size = lax.axis_size("ctx")
    routed = positions.shape[1]
    value_all = exchange(jnp.broadcast_to(values, (ctx_size, *values.shape[1:])))
    meta, cos_full, sin_full, *own_keys = prepare(positions, keys[0], ctx_size)
    key_alls = [exchange(own_key) for own_key in own_keys]
    dq, owns, arrived = None, [], []
    for head, key_all in enumerate(key_alls):
        dq, terms, own = attention(
            meta, cos_full, sin_full, queries[0], out_grad[0], key_all, value_all, routed, head, dq
        )
        owns.append(own)
        arrived.append(exchange(terms))
    key_grad, value_grad = finish(meta, cos_full, sin_full, owns, arrived)
    return (dq[None], key_grad[None], value_grad[None])


def solution(mesh):
    split = P(("groups", "dp"), "ctx", "mp")
    return jax.shard_map(
        body,
        mesh=mesh,
        in_specs=(P(("groups", "dp"), None), split, split, split, split),
        out_specs=(split, split, split),
        check_vma=False,
    )
```

time: 112 us -> 94.1 us (0.84)
  blocking collectives: 16.1 us -> 65.5 us
  waiting for transfers between devices: 48.2 us -> 0.01 us
  between operations: 16.2 us -> 0.69 us
  other arithmetic: 4.86 us -> 0 us
  Pallas kernels: 14.9 us -> 19.3 us
  starting transfers between devices: 6.32 us -> 3.4 us
    all_to_all x0 -> x4, blocking collectives: none -> 65.5 us  [exchange(): lax.all_to_all(chunks, 'ctx', split_axis=0, concat_axis=0, tiled=True)]
    reduce_scatter x1 -> x0, waiting for transfers between devices: 42.7 us -> none  [body(): total = lax.psum_scatter(terms, 'ctx', scatter_dimension=0, tiled=True)]
    all_gather x1 -> x0, blocking collectives: 16.1 us -> none  [body(): ranked = lax.all_gather(owned, 'ctx', axis=0, tiled=True)]
    ppermute x3 -> x0, starting transfers between devices: 6.29 us -> none  [body(): blocks.append(lax.ppermute(blocks[-1], 'ctx', forward[hop:]))]
    ppermute x3 -> x0, waiting for transfers between devices: 5.54 us -> none  [body(): blocks.append(lax.ppermute(blocks[-1], 'ctx', forward[hop:]))]
    pallas_call x1 -> x4, Pallas kernels: 14.9 us -> 19.3 us  [the longest x2 16.3 us: attention(): pl.pallas_call(functools.partial(attention_kernel, ctx_size, 4 if routed...]
    all_to_all x0 -> x1, starting transfers between devices: none -> 3.4 us  [exchange(): lax.all_to_all(chunks, 'ctx', split_axis=0, concat_axis=0, tiled=True)]
    unnamed x12 -> x14, local copies, waits for them, and re-layouts: 1.85 us -> 4.71 us
  transfers between devices with their start and end apart: 4 -> 1, of which waited for: 2 -> 0; matrix products, arithmetic and copies ran while one was open for 2% -> 0% of each run, Pallas kernels for 0% -> 9%
where the time goes in v2:
time: 94.1 us; the launch traced here: 93.7 us
  blocking collectives  65.5 us (70%)
  Pallas kernels  19.3 us (21%)
  local copies, waits for them, and re-layouts  4.75 us (5%)
  starting transfers between devices  3.4 us (4%)
    all_to_all x4, blocking collectives, exchange(): lax.all_to_all(chunks, 'ctx', split_axis=0, concat_axis=0, tiled=True)  65.5 us
    pallas_call x2, Pallas kernels, attention(): pl.pallas_call(functools.partial(attention_kernel, ctx_size, 4 if routed...  16.3 us
    unnamed x14, local copies, waits for them, and re-layouts  4.71 us
    all_to_all x1, starting transfers between devices, exchange(): lax.all_to_all(chunks, 'ctx', split_axis=0, concat_axis=0, tiled=True)  3.4 us
  transfers between devices with their start and end apart: 1, of which 0 were waited for; matrix products, arithmetic and copies ran while one was open for 0% of the time, Pallas kernels for 9%

profile of v2, /device:TPU:0, one launch (start us, length us, event | category | flops | bytes accessed | tf_op | source)
XLA Modules:
  0.0 93.7 jit_solution(6129420276118709495)
XLA Ops:
  0.6 0.0 copy-start.2
  0.6 0.7 copy-done.2
  1.3 0.0 copy-start
  1.3 0.9 copy-done
  2.2 0.0 copy-start.1
  2.2 0.7 copy-done.1
  2.9 1.5 %prepare.1 = (s32[11]{0:T(128)S(1)}, f32[256,128]{1,0:T(8,128)S(1)}, f32[256,128]{1,0:T(8,128)S(1)}, bf16[4,256,128]{2,1,0:T(8,128)(2,1)S(1)}, bf16[4,256,128]{2,1,0:T(8,128)(2,1)}) custom-call(f32[2,128]{1,0:T(2,128)S(1)} %copy-done.2, s32[1,512]{1,0:T(1,128)S(1)} %copy-done.1, bf16[256,256]{1,0:T(8,128)(2,1)S(1)} %bitcast.7), custom_call_target="tpu_custom_call" | custom-call | tf_op jit(solution)/shard_map/prepare/pallas_call | solution.py:90
  4.4 0.0 copy-start.6
  4.4 15.1 %all_to_all.25.key_all_ref = bf16[4,256,128]{2,1,0:T(8,128)(2,1)S(1)} all-to-all(bf16[4,256,128]{2,1,0:T(8,128)(2,1)S(1)} %get-tuple-element.20), channel_id=1, replica_groups=mesh['groups'=2,'ctx'=4,'dp'=2,'mp'=2] {'ctx'}, dimensions={0} | all-to-all | bytes 524288 | tf_op jit(solution)/shard_map/all_to_all | solution.py:259
  19.5 0.0 copy-done.6
  19.5 0.0 copy-start.3
  19.6 16.7 %all_to_all.26.value_all_ref = bf16[4,256,256]{2,1,0:T(8,128)(2,1)S(1)} all-to-all(bf16[4,256,256]{2,1,0:T(8,128)(2,1)S(1)} %broadcast_in_dim.17), channel_id=1, replica_groups=mesh['groups'=2,'ctx'=4,'dp'=2,'mp'=2] {'ctx'}, dimensions={0} | all-to-all | bytes 1048576 | tf_op jit(solution)/shard_map/all_to_all | solution.py:259
  36.2 3.4 %all-to-all-start = ((bf16[4,256,128]{2,1,0:T(8,128)(2,1)}), bf16[4,256,128]{2,1,0:T(8,128)(2,1)S(1)}, u32[]{:S(2)}, u32[]{:S(2)}) async-start(bf16[4,256,128]{2,1,0:T(8,128)(2,1)} %get-tuple-element.19), calls=%async_computation | async-start | bytes 524288 | tf_op jit(solution)/shard_map/all_to_all | solution.py:259
  39.6 0.0 copy-done.3
  39.7 0.0 copy-start.4
  39.7 1.2 %copy-done.4 = bf16[1,256,2048]{2,1,0:T(8,128)(2,1)S(1)} copy-done((bf16[1,256,2048]{2,1,0:T(8,128)(2,1)S(1)}, bf16[1,256,2048]{2,1,0:T(8,128)(2,1)}, u32[]{:S(2)}) %copy-start.4) | copy-done | bytes 1048600
  40.9 8.1 %attention_backward.2 = (bf16[256,2048]{1,0:T(8,128)(2,1)}, bf16[4,256,256]{2,1,0:T(8,128)(2,1)S(1)}, f32[256,256]{1,0:T(8,128)S(1)}) custom-call(s32[11]{0:T(128)S(1)} %get-tuple-element.16.meta_ref, f32[256,128]{1,0:T(8,128)S(1)} %get-tuple-element.17.cos_ref, f32[256,128]{1,0:T(8,128)S(1)} %get-tuple-element.18.sin_ref, bf16[256,2048]{1,0:T(8,128)(2,1)S(1)} %bitcast.8, ...), custom_call_target="tpu_custom_call" | custom-call | flops 1509949440 | bytes 4194304 | tf_op jit(solution)/shard_map/attention_backward/pallas_call | solution.py:202
  49.0 0.0 all-to-all-done.key_all_ref
  49.0 0.0 copy-start.5
  49.0 1.2 %copy-done.5 = bf16[1,256,2048]{2,1,0:T(8,128)(2,1)S(1)} copy-done((bf16[1,256,2048]{2,1,0:T(8,128)(2,1)S(1)}, bf16[1,256,2048]{2,1,0:T(8,128)(2,1)}, u32[]{:S(2)}) %copy-start.5) | copy-done | bytes 1048600
  50.3 8.1 %attention_backward.3 = (bf16[256,2048]{1,0:T(8,128)(2,1)}, bf16[4,256,256]{2,1,0:T(8,128)(2,1)S(1)}, f32[256,256]{1,0:T(8,128)S(1)}) custom-call(s32[11]{0:T(128)S(1)} %get-tuple-element.16.meta_ref, f32[256,128]{1,0:T(8,128)S(1)} %get-tuple-element.17.cos_ref, f32[256,128]{1,0:T(8,128)S(1)} %get-tuple-element.18.sin_ref, ...), custom_call_target="tpu_custom_call", output_to_operand_aliasing={{0}: (7, {})} | custom-call | flops 1509949440 | bytes 4194304 | tf_op jit(solution)/shard_map/attention_backward/pallas_call | solution.py:202
  58.4 17.8 %all_to_all.27.refs_3_ = bf16[4,256,256]{2,1,0:T(8,128)(2,1)S(1)} all-to-all(bf16[4,256,256]{2,1,0:T(8,128)(2,1)S(1)} %get-tuple-element.26), channel_id=1, replica_groups=mesh['groups'=2,'ctx'=4,'dp'=2,'mp'=2] {'ctx'}, dimensions={0} | all-to-all | bytes 1048576 | tf_op jit(solution)/shard_map/all_to_all | solution.py:259
  76.2 15.9 %all_to_all.28.refs_2_ = bf16[4,256,256]{2,1,0:T(8,128)(2,1)S(1)} all-to-all(bf16[4,256,256]{2,1,0:T(8,128)(2,1)S(1)} %get-tuple-element.25), channel_id=1, replica_groups=mesh['groups'=2,'ctx'=4,'dp'=2,'mp'=2] {'ctx'}, dimensions={0} | all-to-all | bytes 1048576 | tf_op jit(solution)/shard_map/all_to_all | solution.py:259
  92.1 1.5 %finish.1 = (bf16[256,256]{1,0:T(8,128)(2,1)}, bf16[256,256]{1,0:T(8,128)(2,1)}) custom-call(s32[11]{0:T(128)S(1)} %get-tuple-element.16.meta_ref, f32[256,128]{1,0:T(8,128)S(1)} %get-tuple-element.17.cos_ref, f32[256,128]{1,0:T(8,128)S(1)} %get-tuple-element.18.sin_ref, f32[256,256]{1,0:T(8,128)S(1)} %get-tuple-element.23.refs_0_, ...), custom_call_target="tpu_custom_call" | custom-call | tf_op jit(solution)/shard_map/finish/pallas_call | solution.py:248
  (1 shorter events, 0.0 us)
Async XLA Ops:
  0.6 0.7 copy-start.2
  1.3 0.9 copy-start
  2.2 0.7 copy-start.1
  4.4 15.1 %copy-start.6 = (bf16[1,256,256]{2,1,0:T(8,128)(2,1)S(1)}, bf16[1,256,256]{2,1,0:T(8,128)(2,1)}, u32[]{:S(2)}) copy-start(bf16[1,256,256]{2,1,0:T(8,128)(2,1)} %param.9) | copy-start | bytes 393220
  19.5 20.1 %copy-start.3 = (bf16[1,256,2048]{2,1,0:T(8,128)(2,1)S(1)}, bf16[1,256,2048]{2,1,0:T(8,128)(2,1)}, u32[]{:S(2)}) copy-start(bf16[1,256,2048]{2,1,0:T(8,128)(2,1)} %param.7) | copy-start | bytes 3145732
  36.2 12.8 %all-to-all-start = ((bf16[4,256,128]{2,1,0:T(8,128)(2,1)}), bf16[4,256,128]{2,1,0:T(8,128)(2,1)S(1)}, u32[]{:S(2)}, u32[]{:S(2)}) async-start(bf16[4,256,128]{2,1,0:T(8,128)(2,1)} %get-tuple-element.19), calls=%async_computation | async-start | bytes 524288 | tf_op jit(solution)/shard_map/all_to_all | solution.py:259
  39.7 1.2 %copy-start.4 = (bf16[1,256,2048]{2,1,0:T(8,128)(2,1)S(1)}, bf16[1,256,2048]{2,1,0:T(8,128)(2,1)}, u32[]{:S(2)}) copy-start(bf16[1,256,2048]{2,1,0:T(8,128)(2,1)} %param.10) | copy-start | bytes 3145732
  49.0 1.2 %copy-start.5 = (bf16[1,256,2048]{2,1,0:T(8,128)(2,1)S(1)}, bf16[1,256,2048]{2,1,0:T(8,128)(2,1)}, u32[]{:S(2)}) copy-start(bf16[1,256,2048]{2,1,0:T(8,128)(2,1)} %param.10) | copy-start | bytes 3145732

commit v3 on v2

v3 whole, which is shorter than its diff:
```python
import functools
import math

import jax
import jax.numpy as jnp
import numpy as np
from jax import lax
from jax.experimental import pallas as pl
from jax.experimental.pallas import tpu as pltpu
from jax.sharding import PartitionSpec as P

HEAD_DIM = 128
HALF_DIM = HEAD_DIM // 2
TOK_SHARD = 1024
ROPE_BASE = 500000.0
SCORE_SCALE = 1.0 / math.sqrt(HEAD_DIM)
EXP2_SCALE = SCORE_SCALE * math.log2(math.e)
HIDDEN = -1e30
ALIGN = 16
CHUNK = 288
MIB = 1024 * 1024

VMEM = pl.BlockSpec(memory_space=pltpu.VMEM)
SMEM = pl.BlockSpec(memory_space=pltpu.SMEM)


def vmem(routed, small, large):
    return pltpu.CompilerParams(vmem_limit_bytes=(small if routed <= 512 else large) * MIB)


def dot(left, right, contract):
    return lax.dot_general(left, right, (contract, ((), ())), preferred_element_type=jnp.float32)


def turn(field, cos_full, sin_full):
    return field * cos_full + pltpu.roll(field, HALF_DIM, 1) * sin_full


def turn_back(field, cos_full, sin_full):
    return field * cos_full - pltpu.roll(field, HALF_DIM, 1) * sin_full


def rope_rows():
    ladder = np.arange(HALF_DIM, dtype=np.float32)
    exponent = ladder * np.float32(-2.0 * math.log(ROPE_BASE) / HEAD_DIM)
    freq = np.exp(exponent.astype(np.float64)).astype(np.float32)
    sign = np.repeat(np.array([-1.0, 1.0], np.float32), HALF_DIM)
    return np.stack([np.concatenate([freq, freq]), sign])


def shard_layout(ctx_size, me, pos, meta_ref):
    shard_of = pos // TOK_SHARD
    for hop in range(2 * ctx_size):
        meta_ref[hop] = 0
    start = jnp.int32(0)
    first = jnp.int32(0)
    my_first = jnp.int32(0)
    for shard in range(ctx_size):
        count = jnp.sum(jnp.where(shard_of == shard, 1.0, 0.0)).astype(jnp.int32)
        my_first = jnp.where(me == shard, first, my_first)

        @pl.when(me >= shard)
        def _():
            meta_ref[me - shard] = start
            meta_ref[ctx_size + me - shard] = count

        first = first + count
        start = start + (count + ALIGN - 1) // ALIGN * ALIGN
    return my_first


def prepare_kernel(ctx_size, rows_ref, pos_ref, keys_ref, values_ref, meta_ref, cos_ref, sin_ref, sent_ref):
    slots, width = keys_ref.shape
    pos = pos_ref[...]
    my_first = shard_layout(ctx_size, lax.axis_index("ctx"), pos, meta_ref)
    shape = (slots, pos.shape[1])
    gap = lax.broadcasted_iota(jnp.int32, shape, 1) - lax.broadcasted_iota(jnp.int32, shape, 0)
    named = jnp.where(gap == my_first, pos.astype(jnp.float32), 0.0)
    angles = jnp.sum(named, axis=1, keepdims=True) * rows_ref[0:1, :]
    cos_full = jnp.cos(angles)
    sin_full = jnp.sin(angles) * rows_ref[1:2, :]
    cos_ref[...] = cos_full
    sin_ref[...] = sin_full
    for lane in range(0, width, HEAD_DIM):
        key = turn(keys_ref[:, lane : lane + HEAD_DIM].astype(jnp.float32), cos_full, sin_full)
        middle = 2 * lane + HEAD_DIM
        sent_ref[:, 2 * lane : middle] = key.astype(jnp.bfloat16)
        sent_ref[:, middle : middle + HEAD_DIM] = values_ref[:, lane : lane + HEAD_DIM]


def prepare(positions, keys, values, ctx_size):
    slots, width = keys.shape
    table = jax.ShapeDtypeStruct((slots, HEAD_DIM), jnp.float32)
    return pl.pallas_call(
        functools.partial(prepare_kernel, ctx_size),
        out_shape=(
            jax.ShapeDtypeStruct((2 * ctx_size,), jnp.int32),
            table,
            table,
            jax.ShapeDtypeStruct((slots, 2 * width), jnp.bfloat16),
        ),
        in_specs=[VMEM] * 4,
        out_specs=(SMEM, VMEM, VMEM, VMEM),
        compiler_params=vmem(positions.shape[1], 16, 32),
        name="prepare",
    )(jnp.asarray(rope_rows()), positions, keys, values)


def queries_kernel(cos_ref, sin_ref, query_ref, grad_ref, turned_ref, turned_t_ref, grad_t_ref):
    for lane in range(0, query_ref.shape[1], HEAD_DIM):
        lanes = slice(lane, lane + HEAD_DIM)
        query = turn(query_ref[:, lanes].astype(jnp.float32), cos_ref[...], sin_ref[...])
        turned_ref[:, lanes] = query.astype(jnp.bfloat16)
        turned_t_ref[lanes, :] = query.T.astype(jnp.bfloat16)
        grad_t_ref[lanes, :] = grad_ref[:, lanes].astype(jnp.float32).T.astype(jnp.bfloat16)


def rotate_queries(cos_full, sin_full, queries, out_grad):
    slots, width = queries.shape
    straight = jax.ShapeDtypeStruct((slots, width), jnp.bfloat16)
    across = jax.ShapeDtypeStruct((width, slots), jnp.bfloat16)
    return pl.pallas_call(
        queries_kernel,
        out_shape=(straight, across, across),
        in_specs=[VMEM] * 4,
        out_specs=(VMEM,) * 3,
        compiler_params=vmem(0, 16, 16),
        cost_estimate=pl.CostEstimate(
            flops=4 * 10**9, bytes_accessed=5 * 1024 * 1024, transcendentals=0
        ),
        name="rotate_queries",
    )(cos_full, sin_full, queries, out_grad)


def stacked(ref, lane, heads):
    parts = [ref[:, lane + h * HEAD_DIM : lane + (h + 1) * HEAD_DIM] for h in range(heads)]
    return jnp.concatenate(parts, axis=0)


def terms_of(probs, score_grads, queries, grads):
    key_term = dot(score_grads, queries, ((1,), (0,))) * SCORE_SCALE
    return jnp.concatenate([key_term, dot(probs, grads, ((1,), (0,)))], axis=1)


def own_rows(my_start, span, slots):
    return pl.multiple_of(jnp.minimum(my_start, span - slots), ALIGN)


def scores_kernel(ctx_size, key_heads, step_heads, meta_ref, turned_ref, grad_ref, turned_t_ref, grad_t_ref, *refs):
    blocks, refs = refs[:ctx_size], refs[ctx_size:]
    terms, refs = refs[: ctx_size - 1], refs[ctx_size - 1 :]
    score_grad_ref, own_prob_ref, key_t_ref, key_ref, bias_ref, prob_ref, acc_ref = refs
    slots = turned_ref.shape[0]
    span = bias_ref.shape[0]
    width = key_heads * HEAD_DIM
    heads = turned_ref.shape[1] // width
    starts = [pl.multiple_of(meta_ref[hop], ALIGN) for hop in range(ctx_size)]
    my_start = starts[0]

    key_ref[...] = jnp.zeros_like(key_ref)
    for hop in range(ctx_size - 1, -1, -1):
        key_ref[pl.ds(starts[hop], slots), :] = blocks[hop][...]
    place = lax.broadcasted_iota(jnp.int32, (span, slots), 0)
    slot_id = lax.broadcasted_iota(jnp.int32, (span, slots), 1)
    seen = (place >= my_start) & (place - slot_id <= my_start)
    for hop in range(1, ctx_size):
        end = starts[hop] + meta_ref[ctx_size + hop]
        seen = seen | ((place >= starts[hop]) & (place < end))
    bias_ref[...] = jnp.where(seen, 0.0, HIDDEN)
    live = lax.broadcasted_iota(jnp.int32, (1, slots), 1) < meta_ref[ctx_size]
    acc_ref[...] = jnp.zeros_like(acc_ref)

    for key_head in range(key_heads):
        lanes = slice(2 * key_head * HEAD_DIM, (2 * key_head + 1) * HEAD_DIM)
        value_lanes = slice((2 * key_head + 1) * HEAD_DIM, 2 * (key_head + 1) * HEAD_DIM)
        key_t = key_ref[:span, lanes].astype(jnp.float32).T.astype(jnp.bfloat16)
        key_t_ref[key_head * HEAD_DIM : (key_head + 1) * HEAD_DIM, :] = key_t

        def step(index, carry):
            for part in range(step_heads):
                head = index * step_heads + part
                row = pl.multiple_of((key_head * heads + head) * HEAD_DIM, HEAD_DIM)
                rows = pl.ds(row, HEAD_DIM)
                columns = pl.ds(pl.multiple_of(head * slots, slots), slots)
                scores = dot(key_ref[:span, lanes], turned_t_ref[rows, :], ((1,), (0,)))
                scores = scores + bias_ref[...]
                prob_grad = dot(key_ref[:span, value_lanes], grad_t_ref[rows, :], ((1,), (0,)))
                peak = jnp.max(scores, axis=0, keepdims=True)
                weights = jnp.exp2((scores - peak) * EXP2_SCALE)
                inverse = 1.0 / jnp.sum(weights, axis=0, keepdims=True)
                delta = jnp.sum(weights * prob_grad, axis=0, keepdims=True) * inverse
                prob = weights * jnp.where(live, inverse, 0.0)
                prob_ref[:, columns] = prob.astype(jnp.bfloat16)
                score_grad = (prob * (prob_grad - delta)).astype(jnp.bfloat16)
                score_grad_ref[key_head, :, columns] = score_grad
            return carry

        lax.fori_loop(0, heads // step_heads, step, 0)
        own_prob_ref[key_head] = prob_ref[pl.ds(own_rows(my_start, span, slots), slots), :]
        for chunk in range(0, span, CHUNK):

            @pl.when(chunk < my_start)
            def _():
                rows = slice(chunk, chunk + CHUNK)
                acc_ref[rows, :] = terms_of(
                    prob_ref[rows, :],
                    score_grad_ref[key_head, rows, :],
                    stacked(turned_ref, key_head * heads * HEAD_DIM, heads),
                    stacked(grad_ref, key_head * heads * HEAD_DIM, heads),
                )

        for hop in range(1, ctx_size):
            term = acc_ref[pl.ds(starts[hop], slots), :].astype(jnp.bfloat16)
            terms[hop - 1][:, 2 * key_head * HEAD_DIM : 2 * (key_head + 1) * HEAD_DIM] = term


def scores(meta, turned, out_grad, turned_t, grad_t, blocks, routed):
    ctx_size = len(blocks)
    slots, width = blocks[0].shape
    key_heads = width // HEAD_DIM // 2
    heads = turned.shape[1] // HEAD_DIM // key_heads
    span = -(-(routed + ctx_size * ALIGN) // CHUNK) * CHUNK
    term = jax.ShapeDtypeStruct((slots, width), jnp.bfloat16)
    outs = pl.pallas_call(
        functools.partial(scores_kernel, ctx_size, key_heads, 4 if routed <= 512 else 1),
        out_shape=(
            *[term] * (ctx_size - 1),
            jax.ShapeDtypeStruct((key_heads, span, heads * slots), jnp.bfloat16),
            jax.ShapeDtypeStruct((key_heads, slots, heads * slots), jnp.bfloat16),
            jax.ShapeDtypeStruct((key_heads * HEAD_DIM, span), jnp.bfloat16),
        ),
        in_specs=[SMEM] + [VMEM] * (4 + ctx_size),
        out_specs=(VMEM,) * (ctx_size + 2),
        scratch_shapes=[
            pltpu.VMEM((span + slots, width), jnp.bfloat16),
            pltpu.VMEM((span, slots), jnp.float32),
            pltpu.VMEM((span, heads * slots), jnp.bfloat16),
            pltpu.VMEM((span + slots, 2 * HEAD_DIM), jnp.float32),
        ],
        compiler_params=vmem(routed, 28, 60),
        cost_estimate=pl.CostEstimate(
            flops=12 * 10**9, bytes_accessed=12 * 1024 * 1024, transcendentals=0
        ),
        name="scores",
    )(meta, turned, out_grad, turned_t, grad_t, *blocks)
    return outs[: ctx_size - 1], outs[ctx_size - 1 :]


def local_kernel(
    key_heads,
    meta_ref,
    cos_ref,
    sin_ref,
    turned_ref,
    grad_ref,
    score_grad_ref,
    own_prob_ref,
    key_t_ref,
    dq_ref,
    own_ref,
    shift_ref,
):
    slots = turned_ref.shape[0]
    heads = turned_ref.shape[1] // HEAD_DIM // key_heads
    first_row = own_rows(meta_ref[0], score_grad_ref.shape[1], slots)
    shift = pl.multiple_of(meta_ref[0] - first_row, ALIGN)
    shift_ref[slots:, :] = jnp.zeros_like(own_ref)
    for key_head in range(key_heads):
        key_t = key_t_ref[key_head * HEAD_DIM : (key_head + 1) * HEAD_DIM, :]
        for head in range(heads):
            score_grad = score_grad_ref[key_head, :, head * slots : (head + 1) * slots]
            grad = (dot(key_t, score_grad, ((1,), (0,))) * SCORE_SCALE).T
            lane = (key_head * heads + head) * HEAD_DIM
            grad = turn_back(grad, cos_ref[...], sin_ref[...])
            dq_ref[:, lane : lane + HEAD_DIM] = grad.astype(jnp.bfloat16)
        lane = key_head * heads * HEAD_DIM
        shift_ref[:slots, 2 * key_head * HEAD_DIM : 2 * (key_head + 1) * HEAD_DIM] = terms_of(
            own_prob_ref[key_head],
            score_grad_ref[key_head, pl.ds(first_row, slots), :],
            stacked(turned_ref, lane, heads),
            stacked(grad_ref, lane, heads),
        )
    own_ref[...] = shift_ref[pl.ds(shift, slots), :]


def local_terms(meta, cos_full, sin_full, turned, out_grad, score_grad, own_prob, key_t):
    slots = turned.shape[0]
    key_heads = score_grad.shape[0]
    return pl.pallas_call(
        functools.partial(local_kernel, key_heads),
        out_shape=(
            jax.ShapeDtypeStruct(turned.shape, jnp.bfloat16),
            jax.ShapeDtypeStruct((slots, 2 * key_heads * HEAD_DIM), jnp.float32),
        ),
        in_specs=[SMEM] + [VMEM] * 7,
        out_specs=(VMEM, VMEM),
        scratch_shapes=[pltpu.VMEM((2 * slots, 2 * key_heads * HEAD_DIM), jnp.float32)],
        compiler_params=vmem(key_t.shape[1] // 2, 24, 48),
        cost_estimate=pl.CostEstimate(
            flops=5 * 10**9, bytes_accessed=10 * 1024 * 1024, transcendentals=0
        ),
        name="local_terms",
    )(meta, cos_full, sin_full, turned, out_grad, score_grad, own_prob, key_t)


def finish_kernel(ctx_size, meta_ref, cos_ref, sin_ref, own_ref, *refs):
    terms, (key_grad_ref, value_grad_ref) = refs[: ctx_size - 1], refs[ctx_size - 1 :]
    slots = own_ref.shape[0]
    live = lax.broadcasted_iota(jnp.int32, (slots, HEAD_DIM), 0) < meta_ref[ctx_size]
    total = own_ref[...]
    for term in terms:
        total += term[...].astype(jnp.float32)
    for lane in range(0, key_grad_ref.shape[1], HEAD_DIM):
        lanes = slice(lane, lane + HEAD_DIM)
        key_term = turn_back(total[:, 2 * lane : 2 * lane + HEAD_DIM], cos_ref[...], sin_ref[...])
        value_term = total[:, 2 * lane + HEAD_DIM : 2 * (lane + HEAD_DIM)]
        key_grad_ref[:, lanes] = jnp.where(live, key_term, 0.0).astype(jnp.bfloat16)
        value_grad_ref[:, lanes] = jnp.where(live, value_term, 0.0).astype(jnp.bfloat16)


def finish(meta, cos_full, sin_full, own, terms):
    slots, width = own.shape
    grad = jax.ShapeDtypeStruct((slots, width // 2), jnp.bfloat16)
    return pl.pallas_call(
        functools.partial(finish_kernel, len(terms) + 1),
        out_shape=(grad, grad),
        in_specs=[SMEM] + [VMEM] * (3 + len(terms)),
        out_specs=(VMEM, VMEM),
        compiler_params=vmem(0, 16, 16),
        name="finish",
    )(meta, cos_full, sin_full, own, *terms)


def part_of(part, size):
    return slice(part * size, (part + 1) * size)


def body(positions, queries, keys, values, out_grad):
    ctx_size = lax.axis_size("ctx")
    routed = positions.shape[1]
    meta, cos_full, sin_full, sent = prepare(positions, keys[0], values[0], ctx_size)
    hops = range(1, ctx_size)
    blocks = [sent]
    for hop in hops:
        pairs = [(shard, shard + hop) for shard in range(ctx_size - hop)]
        blocks.append(lax.ppermute(sent, "ctx", pairs))
    turned, turned_t, grad_t = rotate_queries(cos_full, sin_full, queries[0], out_grad[0])
    parts = 1 if routed <= 512 else keys.shape[2] // HEAD_DIM
    wide, narrow = queries.shape[2] // parts, sent.shape[1] // parts
    terms, local = [], []
    for part in range(parts):
        columns, lanes = part_of(part, wide), part_of(part, narrow)
        outs = scores(
            meta,
            turned[:, columns],
            out_grad[0][:, columns],
            turned_t[columns],
            grad_t[columns],
            [block[:, lanes] for block in blocks],
            routed,
        )
        terms.append(outs[0])
        local.append(outs[1])
    terms = [jnp.concatenate(term, axis=1) for term in zip(*terms)]
    arrived = []
    for hop in hops:
        pairs = [(shard + hop, shard) for shard in range(ctx_size - hop)]
        arrived.append(lax.ppermute(terms[hop - 1], "ctx", pairs))
    finals = []
    for part in range(parts):
        columns = part_of(part, wide)
        finals.append(
            local_terms(
                meta, cos_full, sin_full, turned[:, columns], out_grad[0][:, columns], *local[part]
            )
        )
    dq, own = [jnp.concatenate(final, axis=1) for final in zip(*finals)]
    key_grad, value_grad = finish(meta, cos_full, sin_full, own, arrived)
    return (dq[None], key_grad[None], value_grad[None])


def solution(mesh):
    split = P(("groups", "dp"), "ctx", "mp")
    return jax.shard_map(
        body,
        mesh=mesh,
        in_specs=(P(("groups", "dp"), None), split, split, split, split),
        out_specs=(split, split, split),
        check_vma=False,
    )
```

time: 94.1 us -> 76 us (0.81)
  blocking collectives: 65.5 us -> 0 us
  waiting for transfers between devices: 0.01 us -> 37.5 us
  starting transfers between devices: 3.4 us -> 14.6 us
  Pallas kernels: 19.3 us -> 17.1 us
    all_to_all x4 -> x0, blocking collectives: 65.5 us -> none  [exchange(): lax.all_to_all(chunks, 'ctx', split_axis=0, concat_axis=0, tiled=True)]
    ppermute x0 -> x6, waiting for transfers between devices: none -> 37.5 us  [the longest x3 28.1 us: body(): arrived.append(lax.ppermute(terms[hop - 1], 'ctx', pairs))]
    ppermute x0 -> x6, starting transfers between devices: none -> 14.6 us  [the longest x3 10.7 us: body(): blocks.append(lax.ppermute(sent, 'ctx', pairs))]
    all_to_all x1 -> x0, starting transfers between devices: 3.4 us -> none  [exchange(): lax.all_to_all(chunks, 'ctx', split_axis=0, concat_axis=0, tiled=True)]
    pallas_call x3 -> x4, Pallas kernels: 17.8 us -> 16 us  [the longest x1 9.63 us: scores(): pl.pallas_call(functools.partial(scores_kernel, ctx_size, key_heads, 4 if...]
  transfers between devices with their start and end apart: 1 -> 6, of which waited for: 0 -> 4; matrix products, arithmetic and copies ran while one was open for 0% -> 0% of each run, Pallas kernels for 9% -> 7%
where the time goes in v3:
time: 76 us; the launch traced here: 75.6 us
  waiting for transfers between devices  37.5 us (49%)
  Pallas kernels  17.1 us (23%)
  starting transfers between devices  14.6 us (19%)
  local copies, waits for them, and re-layouts  5.61 us (7%)
    ppermute x3, waiting for transfers between devices, body(): arrived.append(lax.ppermute(terms[hop - 1], 'ctx', pairs))  28.1 us
    ppermute x3, starting transfers between devices, body(): blocks.append(lax.ppermute(sent, 'ctx', pairs))  10.7 us
    pallas_call x1, Pallas kernels, scores(): pl.pallas_call(functools.partial(scores_kernel, ctx_size, key_heads, 4 if...  9.63 us
    ppermute x3, waiting for transfers between devices, body(): blocks.append(lax.ppermute(sent, 'ctx', pairs))  9.4 us
    unnamed x14, local copies, waits for them, and re-layouts  5.61 us
    ppermute x3, starting transfers between devices, body(): arrived.append(lax.ppermute(terms[hop - 1], 'ctx', pairs))  3.88 us
    pallas_call x1, Pallas kernels, local_terms(): pl.pallas_call(functools.partial(local_kernel, key_heads), out_shape=(jax...  3.8 us
  transfers between devices with their start and end apart: 6, of which 4 were waited for; matrix products, arithmetic and copies ran while one was open for 0% of the time, Pallas kernels for 7%

profile of v3, /device:TPU:0, one launch (start us, length us, event | category | flops | bytes accessed | tf_op | source)
XLA Modules:
  0.0 75.6 jit_solution(355851095463120655)
XLA Ops:
  0.6 0.0 copy-start
  0.6 0.9 %copy-done = bf16[1,256,256]{2,1,0:T(8,128)(2,1)S(1)} copy-done((bf16[1,256,256]{2,1,0:T(8,128)(2,1)S(1)}, bf16[1,256,256]{2,1,0:T(8,128)(2,1)}, u32[]{:S(2)}) %copy-start) | copy-done | bytes 131096
  1.5 0.0 copy-start.1
  1.5 0.9 %copy-done.1 = bf16[1,256,256]{2,1,0:T(8,128)(2,1)S(1)} copy-done((bf16[1,256,256]{2,1,0:T(8,128)(2,1)S(1)}, bf16[1,256,256]{2,1,0:T(8,128)(2,1)}, u32[]{:S(2)}) %copy-start.1) | copy-done | bytes 131096
  2.4 0.0 copy-start.2
  2.4 0.7 copy-done.2
  3.1 0.0 copy-start.3
  3.1 0.7 copy-done.3
  3.8 1.1 %prepare.1 = (s32[8]{0:T(128)S(1)}, f32[256,128]{1,0:T(8,128)S(1)}, f32[256,128]{1,0:T(8,128)S(1)}, bf16[256,512]{1,0:T(8,128)(2,1)S(1)}) custom-call(f32[2,128]{1,0:T(2,128)S(1)} %copy-done.3, s32[1,512]{1,0:T(1,128)S(1)} %copy-done.2, bf16[256,256]{1,0:T(8,128)(2,1)S(1)} %bitcast.7, bf16[256,256]{1,0:T(8,128)(2,1)S(1)} %bitcast.8), custom_call_target="tpu_custom_call" | custom-call | tf_op jit(solution)/shard_map/prepare/pallas_call | solution.py:94
  4.9 7.0 %collective-permute-start.2 = (bf16[256,512]{1,0:T(8,128)(2,1)S(1)}, bf16[256,512]{1,0:T(8,128)(2,1)S(1)}, u32[]{:S(2)}, u32[]{:S(2)}) collective-permute-start(bf16[256,512]{1,0:T(8,128)(2,1)S(1)} %get-tuple-element.26.refs_0_), channel_id=1, source_target_pairs={{0,12},{1,13},{2,14},{3,15},{16,28},{17,29},{18,30},{19,31}} | collective-permute-start | bytes 786440 | tf_op jit(solution)/shard_map/ppermute | solution.py:346
  11.9 1.3 %collective-permute-start.1 = (bf16[256,512]{1,0:T(8,128)(2,1)S(1)}, bf16[256,512]{1,0:T(8,128)(2,1)S(1)}, u32[]{:S(2)}, u32[]{:S(2)}) collective-permute-start(bf16[256,512]{1,0:T(8,128)(2,1)S(1)} %get-tuple-element.26.refs_0_), channel_id=1, source_target_pairs={{0,8},{4,12},{1,9},{5,13},{2,10},{6,14},{3,11},{7,15},{16,24},{20,... | collective-permute-start | bytes 786440 | tf_op jit(solution)/shard_map/ppermute | solution.py:346
  13.2 2.5 %collective-permute-start = (bf16[256,512]{1,0:T(8,128)(2,1)S(1)}, bf16[256,512]{1,0:T(8,128)(2,1)S(1)}, u32[]{:S(2)}, u32[]{:S(2)}) collective-permute-start(bf16[256,512]{1,0:T(8,128)(2,1)S(1)} %get-tuple-element.26.refs_0_), channel_id=1, source_target_pairs={{0,4},{4,8},{8,12},{1,5},{5,9},{9,13},{2,6},{6,10},{10,14},{3,7},{... | collective-permute-start | bytes 786440 | tf_op jit(solution)/shard_map/ppermute | solution.py:346
  15.7 0.0 copy-start.4
  15.7 1.2 %copy-done.4 = bf16[1,256,2048]{2,1,0:T(8,128)(2,1)S(1)} copy-done((bf16[1,256,2048]{2,1,0:T(8,128)(2,1)S(1)}, bf16[1,256,2048]{2,1,0:T(8,128)(2,1)}, u32[]{:S(2)}) %copy-start.4) | copy-done | bytes 1048600
  16.9 0.0 copy-start.5
  16.9 1.2 %copy-done.5 = bf16[1,256,2048]{2,1,0:T(8,128)(2,1)S(1)} copy-done((bf16[1,256,2048]{2,1,0:T(8,128)(2,1)S(1)}, bf16[1,256,2048]{2,1,0:T(8,128)(2,1)}, u32[]{:S(2)}) %copy-start.5) | copy-done | bytes 1048600
  18.1 0.0 copy-start.6
  18.1 1.2 %rotate_queries.1 = (bf16[256,2048]{1,0:T(8,128)(2,1)S(1)}, bf16[2048,256]{1,0:T(8,128)(2,1)S(1)}, bf16[2048,256]{1,0:T(8,128)(2,1)S(1)}) custom-call(f32[256,128]{1,0:T(8,128)S(1)} %get-tuple-element.21.cos_ref, f32[256,128]{1,0:T(8,128)S(1)} %get-tuple-element.22.sin_ref, bf16[256,2048]{1,0:T(8,128)(2,1)S(1)} %bitcast.9, bf16[256,2048]{1,0:T(8,128)(2,1)S(1)} %bitcast.10), custom_call_target="tpu_custom_call" | custom-call | flops 4000000000 | bytes 5242880 | tf_op jit(solution)/shard_map/rotate_queries/pallas_call | solution.py:122
  19.3 0.0 collective-permute-done.2.refs_3_
  19.3 4.9 %collective-permute-done.1.refs_2_ = bf16[256,512]{1,0:T(8,128)(2,1)S(1)} collective-permute-done((bf16[256,512]{1,0:T(8,128)(2,1)S(1)}, bf16[256,512]{1,0:T(8,128)(2,1)S(1)}, u32[]{:S(2)}, u32[]{:S(2)}) %collective-permute-start.1) | collective-permute-done | bytes 262176 | tf_op jit(solution)/shard_map/ppermute | solution.py:346
  24.3 4.5 %collective-permute-done.refs_1_ = bf16[256,512]{1,0:T(8,128)(2,1)S(1)} collective-permute-done((bf16[256,512]{1,0:T(8,128)(2,1)S(1)}, bf16[256,512]{1,0:T(8,128)(2,1)S(1)}, u32[]{:S(2)}, u32[]{:S(2)}) %collective-permute-start) | collective-permute-done | bytes 262176 | tf_op jit(solution)/shard_map/ppermute | solution.py:346
  28.7 0.0 copy-done.6
  28.7 9.6 %scores.1 = (bf16[256,512]{1,0:T(8,128)(2,1)S(1)}, bf16[256,512]{1,0:T(8,128)(2,1)S(1)}, bf16[256,512]{1,0:T(8,128)(2,1)S(1)}, bf16[2,576,2048]{2,1,0:T(8,128)(2...) custom-call(s32[8]{0:T(128)S(1)} %get-tuple-element.20.meta_ref, ...), custom_call_target="tpu_custom_call" | custom-call | flops 12000000000 | bytes 12582912 | tf_op jit(solution)/shard_map/scores/pallas_call | solution.py:224
  38.4 1.3 %collective-permute-start.3 = (bf16[256,512]{1,0:T(8,128)(2,1)S(1)}, bf16[256,512]{1,0:T(8,128)(2,1)S(1)}, u32[]{:S(2)}, u32[]{:S(2)}) collective-permute-start(bf16[256,512]{1,0:T(8,128)(2,1)S(1)} %get-tuple-element.32), channel_id=1, source_target_pairs={{4,0},{8,4},{12,8},{5,1},{9,5},{13,9},{6,2},{10,6},{14,10},{7,3},{... | collective-permute-start | bytes 786440 | tf_op jit(solution)/shard_map/ppermute | solution.py:368
  39.7 1.3 %collective-permute-start.4 = (bf16[256,512]{1,0:T(8,128)(2,1)S(1)}, bf16[256,512]{1,0:T(8,128)(2,1)S(1)}, u32[]{:S(2)}, u32[]{:S(2)}) collective-permute-start(bf16[256,512]{1,0:T(8,128)(2,1)S(1)} %get-tuple-element.33), channel_id=1, source_target_pairs={{8,0},{12,4},{9,1},{13,5},{10,2},{14,6},{11,3},{15,7},{24,16},{28,... | collective-permute-start | bytes 786440 | tf_op jit(solution)/shard_map/ppermute | solution.py:368
  41.0 1.3 %collective-permute-start.5 = (bf16[256,512]{1,0:T(8,128)(2,1)S(1)}, bf16[256,512]{1,0:T(8,128)(2,1)S(1)}, u32[]{:S(2)}, u32[]{:S(2)}) collective-permute-start(bf16[256,512]{1,0:T(8,128)(2,1)S(1)} %get-tuple-element.34), channel_id=1, source_target_pairs={{12,0},{13,1},{14,2},{15,3},{28,16},{29,17},{30,18},{31,19}} | collective-permute-start | bytes 786440 | tf_op jit(solution)/shard_map/ppermute | solution.py:368
  42.3 3.8 %local_terms.1 = (bf16[256,2048]{1,0:T(8,128)(2,1)}, f32[256,512]{1,0:T(8,128)S(1)}) custom-call(s32[8]{0:T(128)S(1)} %get-tuple-element.20.meta_ref, f32[256,128]{1,0:T(8,128)S(1)} %get-tuple-element.21.cos_ref, f32[256,128]{1,0:T(8,128)S(1)} %get-tuple-element.22.sin_ref, bf16[256,2048]{1,0:T(8,128)(2,1)S(1)} %get-tuple-element.23.turned_ref, ...), custom_call_target="tpu_custom_call" | custom-call | flops 5000000000 | bytes 10485760 | tf_op jit(solution)/shard_map/local_terms/pallas_call | solution.py:289
  46.1 7.7 %collective-permute-done.3.refs_0_ = bf16[256,512]{1,0:T(8,128)(2,1)S(1)} collective-permute-done((bf16[256,512]{1,0:T(8,128)(2,1)S(1)}, bf16[256,512]{1,0:T(8,128)(2,1)S(1)}, u32[]{:S(2)}, u32[]{:S(2)}) %collective-permute-start.3) | collective-permute-done | bytes 262176 | tf_op jit(solution)/shard_map/ppermute | solution.py:368
  53.8 20.4 %collective-permute-done.4.refs_1_ = bf16[256,512]{1,0:T(8,128)(2,1)S(1)} collective-permute-done((bf16[256,512]{1,0:T(8,128)(2,1)S(1)}, bf16[256,512]{1,0:T(8,128)(2,1)S(1)}, u32[]{:S(2)}, u32[]{:S(2)}) %collective-permute-start.4) | collective-permute-done | bytes 262176 | tf_op jit(solution)/shard_map/ppermute | solution.py:368
  74.2 0.0 collective-permute-done.5.refs_2_
  74.2 1.4 %finish.1 = (bf16[256,256]{1,0:T(8,128)(2,1)}, bf16[256,256]{1,0:T(8,128)(2,1)}) custom-call(s32[8]{0:T(128)S(1)} %get-tuple-element.20.meta_ref, f32[256,128]{1,0:T(8,128)S(1)} %get-tuple-element.21.cos_ref, f32[256,128]{1,0:T(8,128)S(1)} %get-tuple-element.22.sin_ref, f32[256,512]{1,0:T(8,128)S(1)} %get-tuple-element.31.own_ref, ...), custom_call_target="tpu_custom_call" | custom-call | tf_op jit(solution)/shard_map/finish/pallas_call | solution.py:324
Async XLA Ops:
  0.6 0.9 %copy-start = (bf16[1,256,256]{2,1,0:T(8,128)(2,1)S(1)}, bf16[1,256,256]{2,1,0:T(8,128)(2,1)}, u32[]{:S(2)}) copy-start(bf16[1,256,256]{2,1,0:T(8,128)(2,1)} %param.8) | copy-start | bytes 393220
  1.5 0.9 %copy-start.1 = (bf16[1,256,256]{2,1,0:T(8,128)(2,1)S(1)}, bf16[1,256,256]{2,1,0:T(8,128)(2,1)}, u32[]{:S(2)}) copy-start(bf16[1,256,256]{2,1,0:T(8,128)(2,1)} %param.9) | copy-start | bytes 393220
  2.4 0.7 copy-start.2
  3.1 0.7 copy-start.3
  4.9 14.4 %collective-permute-start.2 = (bf16[256,512]{1,0:T(8,128)(2,1)S(1)}, bf16[256,512]{1,0:T(8,128)(2,1)S(1)}, u32[]{:S(2)}, u32[]{:S(2)}) collective-permute-start(bf16[256,512]{1,0:T(8,128)(2,1)S(1)} %get-tuple-element.26.refs_0_), channel_id=1, source_target_pairs={{0,12},{1,13},{2,14},{3,15},{16,28},{17,29},{18,30},{19,31}} | collective-permute-start | bytes 786440 | tf_op jit(solution)/shard_map/ppermute | solution.py:346
  11.9 12.4 %collective-permute-start.1 = (bf16[256,512]{1,0:T(8,128)(2,1)S(1)}, bf16[256,512]{1,0:T(8,128)(2,1)S(1)}, u32[]{:S(2)}, u32[]{:S(2)}) collective-permute-start(bf16[256,512]{1,0:T(8,128)(2,1)S(1)} %get-tuple-element.26.refs_0_), channel_id=1, source_target_pairs={{0,8},{4,12},{1,9},{5,13},{2,10},{6,14},{3,11},{7,15},{16,24},{20,... | collective-permute-start | bytes 786440 | tf_op jit(solution)/shard_map/ppermute | solution.py:346
  13.2 15.5 %collective-permute-start = (bf16[256,512]{1,0:T(8,128)(2,1)S(1)}, bf16[256,512]{1,0:T(8,128)(2,1)S(1)}, u32[]{:S(2)}, u32[]{:S(2)}) collective-permute-start(bf16[256,512]{1,0:T(8,128)(2,1)S(1)} %get-tuple-element.26.refs_0_), channel_id=1, source_target_pairs={{0,4},{4,8},{8,12},{1,5},{5,9},{9,13},{2,6},{6,10},{10,14},{3,7},{... | collective-permute-start | bytes 786440 | tf_op jit(solution)/shard_map/ppermute | solution.py:346
  15.7 1.2 %copy-start.4 = (bf16[1,256,2048]{2,1,0:T(8,128)(2,1)S(1)}, bf16[1,256,2048]{2,1,0:T(8,128)(2,1)}, u32[]{:S(2)}) copy-start(bf16[1,256,2048]{2,1,0:T(8,128)(2,1)} %param.7) | copy-start | bytes 3145732
  16.9 1.2 %copy-start.5 = (bf16[1,256,2048]{2,1,0:T(8,128)(2,1)S(1)}, bf16[1,256,2048]{2,1,0:T(8,128)(2,1)}, u32[]{:S(2)}) copy-start(bf16[1,256,2048]{2,1,0:T(8,128)(2,1)} %param.10) | copy-start | bytes 3145732
  18.1 10.6 %copy-start.6 = (bf16[1,256,2048]{2,1,0:T(8,128)(2,1)S(1)}, bf16[1,256,2048]{2,1,0:T(8,128)(2,1)}, u32[]{:S(2)}) copy-start(bf16[1,256,2048]{2,1,0:T(8,128)(2,1)} %param.10) | copy-start | bytes 3145732
  38.4 15.4 %collective-permute-start.3 = (bf16[256,512]{1,0:T(8,128)(2,1)S(1)}, bf16[256,512]{1,0:T(8,128)(2,1)S(1)}, u32[]{:S(2)}, u32[]{:S(2)}) collective-permute-start(bf16[256,512]{1,0:T(8,128)(2,1)S(1)} %get-tuple-element.32), channel_id=1, source_target_pairs={{4,0},{8,4},{12,8},{5,1},{9,5},{13,9},{6,2},{10,6},{14,10},{7,3},{... | collective-permute-start | bytes 786440 | tf_op jit(solution)/shard_map/ppermute | solution.py:368
  39.7 34.5 %collective-permute-start.4 = (bf16[256,512]{1,0:T(8,128)(2,1)S(1)}, bf16[256,512]{1,0:T(8,128)(2,1)S(1)}, u32[]{:S(2)}, u32[]{:S(2)}) collective-permute-start(bf16[256,512]{1,0:T(8,128)(2,1)S(1)} %get-tuple-element.33), channel_id=1, source_target_pairs={{8,0},{12,4},{9,1},{13,5},{10,2},{14,6},{11,3},{15,7},{24,16},{28,... | collective-permute-start | bytes 786440 | tf_op jit(solution)/shard_map/ppermute | solution.py:368
  41.0 33.2 %collective-permute-start.5 = (bf16[256,512]{1,0:T(8,128)(2,1)S(1)}, bf16[256,512]{1,0:T(8,128)(2,1)S(1)}, u32[]{:S(2)}, u32[]{:S(2)}) collective-permute-start(bf16[256,512]{1,0:T(8,128)(2,1)S(1)} %get-tuple-element.34), channel_id=1, source_target_pairs={{12,0},{13,1},{14,2},{15,3},{28,16},{29,17},{30,18},{31,19}} | collective-permute-start | bytes 786440 | tf_op jit(solution)/shard_map/ppermute | solution.py:368

commit v4 on v3

--- a/solution.py
+++ b/solution.py
@@ -69,41 +69,61 @@
     return my_first
 
 
-def prepare_kernel(ctx_size, rows_ref, pos_ref, keys_ref, values_ref, meta_ref, cos_ref, sin_ref, sent_ref):
-    slots, width = keys_ref.shape
+def prepare_kernel(
+    ctx_size, rows_hbm, pos_hbm, keys_hbm, values_hbm, meta_ref, cos_ref, sin_ref, *refs
+):
+    sent_refs, (rows_ref, pos_ref, keys_ref, values_ref, sems) = refs[:-5], refs[-5:]
+    sources = (pos_hbm, rows_hbm, keys_hbm, values_hbm)
+    targets = (pos_ref, rows_ref, keys_ref, values_ref)
+    copies = [
+        pltpu.make_async_copy(source, target, sems.at[index])
+        for index, (source, target) in enumerate(zip(sources, targets))
+    ]
+    for copy in copies:
+        copy.start()
+    copies[0].wait()
+    slots = keys_ref.shape[0]
     pos = pos_ref[...]
     my_first = shard_layout(ctx_size, lax.axis_index("ctx"), pos, meta_ref)
     shape = (slots, pos.shape[1])
     gap = lax.broadcasted_iota(jnp.int32, shape, 1) - lax.broadcasted_iota(jnp.int32, shape, 0)
     named = jnp.where(gap == my_first, pos.astype(jnp.float32), 0.0)
+    copies[1].wait()
     angles = jnp.sum(named, axis=1, keepdims=True) * rows_ref[0:1, :]
     cos_full = jnp.cos(angles)
     sin_full = jnp.sin(angles) * rows_ref[1:2, :]
     cos_ref[...] = cos_full
     sin_ref[...] = sin_full
-    for lane in range(0, width, HEAD_DIM):
-        key = turn(keys_ref[:, lane : lane + HEAD_DIM].astype(jnp.float32), cos_full, sin_full)
-        middle = 2 * lane + HEAD_DIM
-        sent_ref[:, 2 * lane : middle] = key.astype(jnp.bfloat16)
-        sent_ref[:, middle : middle + HEAD_DIM] = values_ref[:, lane : lane + HEAD_DIM]
+    copies[2].wait()
+    copies[3].wait()
+    for head, sent_ref in enumerate(sent_refs):
+        lanes = slice(head * HEAD_DIM, (head + 1) * HEAD_DIM)
+        key = turn(keys_ref[:, lanes].astype(jnp.float32), cos_full, sin_full)
+        sent_ref[:, :HEAD_DIM] = key.astype(jnp.bfloat16)
+        sent_ref[:, HEAD_DIM:] = values_ref[:, lanes]
 
 
 def prepare(positions, keys, values, ctx_size):
     slots, width = keys.shape
+    rows = jnp.asarray(rope_rows())
     table = jax.ShapeDtypeStruct((slots, HEAD_DIM), jnp.float32)
+    sent = jax.ShapeDtypeStruct((slots, 2 * HEAD_DIM), jnp.bfloat16)
+    operands = (rows, positions, keys, values)
     return pl.pallas_call(
         functools.partial(prepare_kernel, ctx_size),
         out_shape=(
             jax.ShapeDtypeStruct((2 * ctx_size,), jnp.int32),
             table,
             table,
-            jax.ShapeDtypeStruct((slots, 2 * width), jnp.bfloat16),
-        ),
-        in_specs=[VMEM] * 4,
-        out_specs=(SMEM, VMEM, VMEM, VMEM),
-        compiler_params=vmem(positions.shape[1], 16, 32),
+            *[sent] * (width // HEAD_DIM),
+        ),
+        in_specs=[pl.BlockSpec(memory_space=pl.ANY)] * 4,
+        out_specs=(SMEM,) + (VMEM,) * (2 + width // HEAD_DIM),
+        scratch_shapes=[pltpu.VMEM(operand.shape, operand.dtype) for operand in operands]
+        + [pltpu.SemaphoreType.DMA((4,))],
+        compiler_params=vmem(positions.shape[1], 60, 60),
         name="prepare",
-    )(jnp.asarray(rope_rows()), positions, keys, values)
+    )(*operands)
 
 
 def queries_kernel(cos_ref, sin_ref, query_ref, grad_ref, turned_ref, turned_t_ref, grad_t_ref):
@@ -147,7 +167,7 @@
 
 
 def scores_kernel(ctx_size, key_heads, step_heads, meta_ref, turned_ref, grad_ref, turned_t_ref, grad_t_ref, *refs):
-    blocks, refs = refs[:ctx_size], refs[ctx_size:]
+    blocks, refs = refs[: ctx_size * key_heads], refs[ctx_size * key_heads :]
     terms, refs = refs[: ctx_size - 1], refs[ctx_size - 1 :]
     score_grad_ref, own_prob_ref, key_t_ref, key_ref, bias_ref, prob_ref, acc_ref = refs
     slots = turned_ref.shape[0]
@@ -156,10 +176,16 @@
     heads = turned_ref.shape[1] // width
     starts = [pl.multiple_of(meta_ref[hop], ALIGN) for hop in range(ctx_size)]
     my_start = starts[0]
+    sent_hops = list(range(1, ctx_size))
+    if relayed(ctx_size):
+        last = lax.axis_index("ctx") == ctx_size - 1
+        sent_hops = [jnp.where(last, 3, 1), 2, jnp.where(last, 1, 2)]
 
     key_ref[...] = jnp.zeros_like(key_ref)
     for hop in range(ctx_size - 1, -1, -1):
-        key_ref[pl.ds(starts[hop], slots), :] = blocks[hop][...]
+        for head in range(key_heads):
+            lanes = slice(2 * head * HEAD_DIM, 2 * (head + 1) * HEAD_DIM)
+            key_ref[pl.ds(starts[hop], slots), lanes] = blocks[head * ctx_size + hop][...]
     place = lax.broadcasted_iota(jnp.int32, (span, slots), 0)
     slot_id = lax.broadcasted_iota(jnp.int32, (span, slots), 1)
     seen = (place >= my_start) & (place - slot_id <= my_start)
@@ -209,27 +235,34 @@
                     stacked(grad_ref, key_head * heads * HEAD_DIM, heads),
                 )
 
-        for hop in range(1, ctx_size):
-            term = acc_ref[pl.ds(starts[hop], slots), :].astype(jnp.bfloat16)
-            terms[hop - 1][:, 2 * key_head * HEAD_DIM : 2 * (key_head + 1) * HEAD_DIM] = term
+        for hop, term_ref in zip(sent_hops, terms):
+            start = pl.multiple_of(meta_ref[hop], ALIGN)
+            term = acc_ref[pl.ds(start, slots), :].astype(term_ref.dtype)
+            term_ref[:, 2 * key_head * HEAD_DIM : 2 * (key_head + 1) * HEAD_DIM] = term
+
+
+def relayed(ctx_size):
+    return ctx_size == 4
 
 
 def scores(meta, turned, out_grad, turned_t, grad_t, blocks, routed):
-    ctx_size = len(blocks)
-    slots, width = blocks[0].shape
-    key_heads = width // HEAD_DIM // 2
+    key_heads, ctx_size = len(blocks), len(blocks[0])
+    slots = turned.shape[0]
+    width = 2 * key_heads * HEAD_DIM
     heads = turned.shape[1] // HEAD_DIM // key_heads
     span = -(-(routed + ctx_size * ALIGN) // CHUNK) * CHUNK
-    term = jax.ShapeDtypeStruct((slots, width), jnp.bfloat16)
+    terms = [jax.ShapeDtypeStruct((slots, width), jnp.bfloat16)] * (ctx_size - 1)
+    if relayed(ctx_size):
+        terms[2] = jax.ShapeDtypeStruct((slots, width), jnp.float32)
     outs = pl.pallas_call(
         functools.partial(scores_kernel, ctx_size, key_heads, 4 if routed <= 512 else 1),
         out_shape=(
-            *[term] * (ctx_size - 1),
+            *terms,
             jax.ShapeDtypeStruct((key_heads, span, heads * slots), jnp.bfloat16),
             jax.ShapeDtypeStruct((key_heads, slots, heads * slots), jnp.bfloat16),
             jax.ShapeDtypeStruct((key_heads * HEAD_DIM, span), jnp.bfloat16),
         ),
-        in_specs=[SMEM] + [VMEM] * (4 + ctx_size),
+        in_specs=[SMEM] + [VMEM] * (4 + ctx_size * key_heads),
         out_specs=(VMEM,) * (ctx_size + 2),
         scratch_shapes=[
             pltpu.VMEM((span + slots, width), jnp.bfloat16),
@@ -242,7 +275,7 @@
             flops=12 * 10**9, bytes_accessed=12 * 1024 * 1024, transcendentals=0
         ),
         name="scores",
-    )(meta, turned, out_grad, turned_t, grad_t, *blocks)
+    )(meta, turned, out_grad, turned_t, grad_t, *[block for head in blocks for block in head])
     return outs[: ctx_size - 1], outs[ctx_size - 1 :]
 
 
@@ -308,8 +341,11 @@
     slots = own_ref.shape[0]
     live = lax.broadcasted_iota(jnp.int32, (slots, HEAD_DIM), 0) < meta_ref[ctx_size]
     total = own_ref[...]
-    for term in terms:
-        total += term[...].astype(jnp.float32)
+    for index, term in enumerate(terms):
+        term = term[...].astype(jnp.float32)
+        if index == 0 and relayed(ctx_size):
+            term = jnp.where(lax.axis_index("ctx") == 2, 0.0, term)
+        total += term
     for lane in range(0, key_grad_ref.shape[1], HEAD_DIM):
         lanes = slice(lane, lane + HEAD_DIM)
         key_term = turn_back(total[:, 2 * lane : 2 * lane + HEAD_DIM], cos_ref[...], sin_ref[...])
@@ -335,37 +371,53 @@
     return slice(part * size, (part + 1) * size)
 
 
+def climb(sent, ctx_size):
+    blocks = [sent]
+    for hop in range(1, ctx_size):
+        pairs = [(shard, shard + 1) for shard in range(hop - 1, ctx_size - 1)]
+        blocks.append(lax.ppermute(blocks[-1], "ctx", pairs))
+    return blocks
+
+
+def relay(first, second, third):
+    first = lax.ppermute(first, "ctx", [(3, 2), (2, 1), (1, 0)])
+    second = lax.ppermute(second, "ctx", [(3, 1)])
+    third = (third + first.astype(jnp.float32)).astype(jnp.bfloat16)
+    return [first, second, lax.ppermute(third, "ctx", [(3, 2), (2, 0)])]
+
+
+def descend(terms, ctx_size):
+    arrived = []
+    for hop, term in enumerate(terms, 1):
+        pairs = [(shard + hop, shard) for shard in range(ctx_size - hop)]
+        arrived.append(lax.ppermute(term, "ctx", pairs))
+    return arrived
+
+
 def body(positions, queries, keys, values, out_grad):
     ctx_size = lax.axis_size("ctx")
     routed = positions.shape[1]
-    meta, cos_full, sin_full, sent = prepare(positions, keys[0], values[0], ctx_size)
-    hops = range(1, ctx_size)
-    blocks = [sent]
-    for hop in hops:
-        pairs = [(shard, shard + hop) for shard in range(ctx_size - hop)]
-        blocks.append(lax.ppermute(sent, "ctx", pairs))
+    meta, cos_full, sin_full, *sent = prepare(positions, keys[0], values[0], ctx_size)
+    blocks = [climb(head, ctx_size) for head in sent]
     turned, turned_t, grad_t = rotate_queries(cos_full, sin_full, queries[0], out_grad[0])
-    parts = 1 if routed <= 512 else keys.shape[2] // HEAD_DIM
-    wide, narrow = queries.shape[2] // parts, sent.shape[1] // parts
+    parts = 1 if routed <= 512 else len(sent)
+    wide, key_heads = queries.shape[2] // parts, len(sent) // parts
     terms, local = [], []
     for part in range(parts):
-        columns, lanes = part_of(part, wide), part_of(part, narrow)
+        columns = part_of(part, wide)
         outs = scores(
             meta,
             turned[:, columns],
             out_grad[0][:, columns],
             turned_t[columns],
             grad_t[columns],
-            [block[:, lanes] for block in blocks],
+            blocks[part_of(part, key_heads)],
             routed,
         )
         terms.append(outs[0])
         local.append(outs[1])
     terms = [jnp.concatenate(term, axis=1) for term in zip(*terms)]
-    arrived = []
-    for hop in hops:
-        pairs = [(shard + hop, shard) for shard in range(ctx_size - hop)]
-        arrived.append(lax.ppermute(terms[hop - 1], "ctx", pairs))
+    arrived = relay(*terms) if relayed(ctx_size) else descend(terms, ctx_size)
     finals = []
     for part in range(parts):
         columns = part_of(part, wide)

time: 76 us -> 66.4 us (0.87)
  waiting for transfers between devices: 37.5 us -> 27.9 us
  local copies, waits for them, and re-layouts: 5.61 us -> 4.33 us
  Pallas kernels: 17.1 us -> 18.2 us
    ppermute x6 -> x9, waiting for transfers between devices: 37.5 us -> 27.9 us  [the longest x1 14 us: relay(): first = lax.ppermute(first, 'ctx', [(3, 2), (2, 1), (1, 0)])]
    unnamed x14 -> x20, local copies, waits for them, and re-layouts: 5.61 us -> 4.33 us
    pallas_call x1, Pallas kernels: 1.11 us -> 2.26 us  [prepare(): pl.pallas_call(functools.partial(prepare_kernel, ctx_size), out_shape=(ja...]
    ppermute x6 -> x9, starting transfers between devices: 14.6 us -> 14.5 us  [the longest x6 11.1 us: climb(): blocks.append(lax.ppermute(blocks[-1], 'ctx', pairs))]
  transfers between devices with their start and end apart: 6 -> 9, of which waited for: 4 -> 3; matrix products, arithmetic and copies ran while one was open for 0% -> 0% of each run, Pallas kernels for 7% -> 8%
where the time goes in v4:
time: 66.4 us; the launch traced here: 65.8 us
  waiting for transfers between devices  27.9 us (42%)
  Pallas kernels  18.2 us (27%)
  starting transfers between devices  14.5 us (22%)
  local copies, waits for them, and re-layouts  4.33 us (7%)
  between operations  0.81 us (1%)
    ppermute x1, waiting for transfers between devices, relay(): first = lax.ppermute(first, 'ctx', [(3, 2), (2, 1), (1, 0)])  14 us
    ppermute x1, waiting for transfers between devices, relay(): return [first, second, lax.ppermute(third, 'ctx', [(3, 2), (2, 0)])]  11.7 us
    ppermute x6, starting transfers between devices, climb(): blocks.append(lax.ppermute(blocks[-1], 'ctx', pairs))  11.1 us
    pallas_call x1, Pallas kernels, scores(): pl.pallas_call(functools.partial(scores_kernel, ctx_size, key_heads, 4 if...  9.61 us
    unnamed x20, local copies, waits for them, and re-layouts  4.33 us
    pallas_call x1, Pallas kernels, local_terms(): pl.pallas_call(functools.partial(local_kernel, key_heads), out_shape=(jax...  3.79 us
    pallas_call x1, Pallas kernels, prepare(): pl.pallas_call(functools.partial(prepare_kernel, ctx_size), out_shape=(ja...  2.26 us
    ppermute x6, waiting for transfers between devices, climb(): blocks.append(lax.ppermute(blocks[-1], 'ctx', pairs))  2.14 us
  transfers between devices with their start and end apart: 9, of which 3 were waited for; matrix products, arithmetic and copies ran while one was open for 0% of the time, Pallas kernels for 8%

profile of v4, /device:TPU:0, one launch (start us, length us, event | category | flops | bytes accessed | tf_op | source)
XLA Modules:
  0.0 65.8 jit_solution(18223030304500008831)
XLA Ops:
  0.6 2.3 %prepare.1 = (s32[8]{0:T(128)}, f32[256,128]{1,0:T(8,128)}, f32[256,128]{1,0:T(8,128)}, bf16[256,256]{1,0:T(8,128)(2,1)}, bf16[256,256]{1,0:T(8,128)(2,1)}) custom-call(f32[2,128]{1,0:T(2,128)} %constant.2.clone.rows_hbm, s32[1,512]{1,0:T(1,128)} %pos_hbm.1, bf16[256,256]{1,0:T(8,128)(2,1)} %bitcast.11, bf16[256,256]{1,0:T(8,128)(2,1)} %bitcast.12), custom_call_target="tpu_custom_call" | custom-call | tf_op jit(solution)/shard_map/prepare/pallas_call | solution.py:112
  2.9 4.9 %collective-permute-start = (bf16[256,256]{1,0:T(8,128)(2,1)}, bf16[256,256]{1,0:T(8,128)(2,1)S(1)}, u32[]{:S(2)}, u32[]{:S(2)}) collective-permute-start(bf16[256,256]{1,0:T(8,128)(2,1)} %get-tuple-element.27.refs_0_), channel_id=1, source_target_pairs={{0,4},{4,8},{8,12},{1,5},{5,9},{9,13},{2,6},{6,10},{10,14},{3,7},{... | collective-permute-start | bytes 393224 | tf_op jit(solution)/shard_map/ppermute | solution.py:378
  7.8 3.5 %collective-permute-start.3 = (bf16[256,256]{1,0:T(8,128)(2,1)}, bf16[256,256]{1,0:T(8,128)(2,1)S(1)}, u32[]{:S(2)}, u32[]{:S(2)}) collective-permute-start(bf16[256,256]{1,0:T(8,128)(2,1)} %get-tuple-element.28.refs_4_), channel_id=1, source_target_pairs={{0,4},{4,8},{8,12},{1,5},{5,9},{9,13},{2,6},{6,10},{10,14},{3,7},{... | collective-permute-start | bytes 393224 | tf_op jit(solution)/shard_map/ppermute | solution.py:378
  11.3 0.0 collective-permute-done.refs_1_
  11.3 0.7 %collective-permute-start.1 = (bf16[256,256]{1,0:T(8,128)(2,1)S(1)}, bf16[256,256]{1,0:T(8,128)(2,1)S(1)}, u32[]{:S(2)}, u32[]{:S(2)}) collective-permute-start(bf16[256,256]{1,0:T(8,128)(2,1)S(1)} %collective-permute-done.refs_1_), channel_id=1, source_target_pairs={{4,8},{8,12},{5,9},{9,13},{6,10},{10,14},{7,11},{11,15},{20,24},{2... | collective-permute-start | bytes 393224 | tf_op jit(solution)/shard_map/ppermute | solution.py:378
  12.0 2.1 %collective-permute-done.3.refs_5_ = bf16[256,256]{1,0:T(8,128)(2,1)S(1)} collective-permute-done((bf16[256,256]{1,0:T(8,128)(2,1)}, bf16[256,256]{1,0:T(8,128)(2,1)S(1)}, u32[]{:S(2)}, u32[]{:S(2)}) %collective-permute-start.3) | collective-permute-done | bytes 131104 | tf_op jit(solution)/shard_map/ppermute | solution.py:378
  14.1 0.7 collective-permute-start.4
  14.8 0.0 collective-permute-done.1.refs_2_
  14.8 0.7 %collective-permute-start.2 = (bf16[256,256]{1,0:T(8,128)(2,1)S(1)}, bf16[256,256]{1,0:T(8,128)(2,1)S(1)}, u32[]{:S(2)}, u32[]{:S(2)}) collective-permute-start(bf16[256,256]{1,0:T(8,128)(2,1)S(1)} %collective-permute-done.1.refs_2_), channel_id=1, source_target_pairs={{8,12},{9,13},{10,14},{11,15},{24,28},{25,29},{26,30},{27,31}} | collective-permute-start | bytes 393224 | tf_op jit(solution)/shard_map/ppermute | solution.py:378
  15.5 0.0 collective-permute-done.4.refs_6_
  15.5 0.7 %collective-permute-start.5 = (bf16[256,256]{1,0:T(8,128)(2,1)S(1)}, bf16[256,256]{1,0:T(8,128)(2,1)S(1)}, u32[]{:S(2)}, u32[]{:S(2)}) collective-permute-start(bf16[256,256]{1,0:T(8,128)(2,1)S(1)} %collective-permute-done.4.refs_6_), channel_id=1, source_target_pairs={{8,12},{9,13},{10,14},{11,15},{24,28},{25,29},{26,30},{27,31}} | collective-permute-start | bytes 393224 | tf_op jit(solution)/shard_map/ppermute | solution.py:378
  16.2 0.0 copy-start
  16.2 0.9 %copy-done = f32[256,128]{1,0:T(8,128)S(1)} copy-done((f32[256,128]{1,0:T(8,128)S(1)}, f32[256,128]{1,0:T(8,128)}, u32[]{:S(2)}) %copy-start) | copy-done | bytes 131096
  17.1 0.9 %copy-done.2 = f32[256,128]{1,0:T(8,128)S(1)} copy-done((f32[256,128]{1,0:T(8,128)S(1)}, f32[256,128]{1,0:T(8,128)}, u32[]{:S(2)}) %copy-start.2) | copy-done | bytes 131096
  18.0 1.2 %copy-done.5 = bf16[1,256,2048]{2,1,0:T(8,128)(2,1)S(1)} copy-done((bf16[1,256,2048]{2,1,0:T(8,128)(2,1)S(1)}, bf16[1,256,2048]{2,1,0:T(8,128)(2,1)}, u32[]{:S(2)}) %copy-start.5) | copy-done | bytes 1048600
  19.2 1.2 %copy-done.6 = bf16[1,256,2048]{2,1,0:T(8,128)(2,1)S(1)} copy-done((bf16[1,256,2048]{2,1,0:T(8,128)(2,1)S(1)}, bf16[1,256,2048]{2,1,0:T(8,128)(2,1)}, u32[]{:S(2)}) %copy-start.6) | copy-done | bytes 1048600
  20.5 1.1 %rotate_queries.1 = (bf16[256,2048]{1,0:T(8,128)(2,1)S(1)}, bf16[2048,256]{1,0:T(8,128)(2,1)S(1)}, bf16[2048,256]{1,0:T(8,128)(2,1)S(1)}) custom-call(f32[256,128]{1,0:T(8,128)S(1)} %copy-done, f32[256,128]{1,0:T(8,128)S(1)} %copy-done.2, bf16[256,2048]{1,0:T(8,128)(2,1)S(1)} %bitcast.7, bf16[256,2048]{1,0:T(8,128)(2,1)S(1)} %bitcast.8), custom_call_target="tpu_custom_call" | custom-call | flops 4000000000 | bytes 5242880 | tf_op jit(solution)/shard_map/rotate_queries/pallas_call | solution.py:142
  21.6 0.0 collective-permute-done.2.refs_3_
  21.6 0.0 collective-permute-done.5.refs_7_
  21.6 0.0 copy-done.7
  21.7 0.0 copy-done.8
  21.7 0.0 copy-done.9
  21.7 9.6 %scores.1 = (bf16[256,512]{1,0:T(8,128)(2,1)S(1)}, bf16[256,512]{1,0:T(8,128)(2,1)S(1)}, f32[256,512]{1,0:T(8,128)S(1)}, bf16[2,576,2048]{2,1,0:T(8,128)(2,1)S(1...) custom-call(s32[8]{0:T(128)S(1)} %copy-done.4, bf16[256,2048]{1,0:T(8,128)(2,1)S(1)} %get-tuple-element.24.turned_ref, ...), custom_call_target="tpu_custom_call" | custom-call | flops 12000000000 | bytes 12582912 | tf_op jit(solution)/shard_map/scores/pallas_call | solution.py:257
  31.3 1.3 %collective-permute-start.6 = (bf16[256,512]{1,0:T(8,128)(2,1)S(1)}, bf16[256,512]{1,0:T(8,128)(2,1)S(1)}, u32[]{:S(2)}, u32[]{:S(2)}) collective-permute-start(bf16[256,512]{1,0:T(8,128)(2,1)S(1)} %get-tuple-element.34), channel_id=1, source_target_pairs={{12,8},{8,4},{4,0},{13,9},{9,5},{5,1},{14,10},{10,6},{6,2},{15,11}... | collective-permute-start | bytes 786440 | tf_op jit(solution)/shard_map/ppermute | solution.py:383
  32.6 0.7 %collective-permute-start.7 = (bf16[256,512]{1,0:T(8,128)(2,1)S(1)}, bf16[256,512]{1,0:T(8,128)(2,1)S(1)}, u32[]{:S(2)}, u32[]{:S(2)}) collective-permute-start(bf16[256,512]{1,0:T(8,128)(2,1)S(1)} %get-tuple-element.35), channel_id=1, source_target_pairs={{12,4},{13,5},{14,6},{15,7},{28,20},{29,21},{30,22},{31,23}} | collective-permute-start | bytes 786440 | tf_op jit(solution)/shard_map/ppermute | solution.py:384
  33.3 14.0 %collective-permute-done.6.refs_0_ = bf16[256,512]{1,0:T(8,128)(2,1)S(1)} collective-permute-done((bf16[256,512]{1,0:T(8,128)(2,1)S(1)}, bf16[256,512]{1,0:T(8,128)(2,1)S(1)}, u32[]{:S(2)}, u32[]{:S(2)}) %collective-permute-start.6) | collective-permute-done | bytes 262176 | tf_op jit(solution)/shard_map/ppermute | solution.py:383
  47.3 0.1 add_convert_fusion
  47.4 1.5 %collective-permute-start.8 = (bf16[256,512]{1,0:T(8,128)(2,1)S(1)}, bf16[256,512]{1,0:T(8,128)(2,1)S(1)}, u32[]{:S(2)}, u32[]{:S(2)}) collective-permute-start(bf16[256,512]{1,0:T(8,128)(2,1)S(1)} %add_convert_fusion), channel_id=1, source_target_pairs={{12,8},{8,0},{13,9},{9,1},{14,10},{10,2},{15,11},{11,3},{28,24},{2... | collective-permute-start | bytes 786440 | tf_op jit(solution)/shard_map/ppermute | solution.py:386
  48.9 3.8 %local_terms.1 = (bf16[256,2048]{1,0:T(8,128)(2,1)}, f32[256,512]{1,0:T(8,128)S(1)}) custom-call(s32[8]{0:T(128)S(1)} %copy-done.4, f32[256,128]{1,0:T(8,128)S(1)} %copy-done.1, f32[256,128]{1,0:T(8,128)S(1)} %copy-done.3, bf16[256,2048]{1,0:T(8,128)(2,1)S(1)} %get-tuple-element.24.turned_ref, bf16[256,2048]{1,0:T(8,128)(2,1)S(1)} %bitcast.10, ...), custom_call_target="tpu_custom_call" | custom-call | flops 5000000000 | bytes 10485760 | tf_op jit(solution)/shard_map/local_terms/pallas_call | solution.py:322
  52.7 0.0 collective-permute-done.7.refs_1_
  52.7 11.7 %collective-permute-done.8.refs_2_ = bf16[256,512]{1,0:T(8,128)(2,1)S(1)} collective-permute-done((bf16[256,512]{1,0:T(8,128)(2,1)S(1)}, bf16[256,512]{1,0:T(8,128)(2,1)S(1)}, u32[]{:S(2)}, u32[]{:S(2)}) %collective-permute-start.8) | collective-permute-done | bytes 262176 | tf_op jit(solution)/shard_map/ppermute | solution.py:386
  64.4 1.4 %finish.1 = (bf16[256,256]{1,0:T(8,128)(2,1)}, bf16[256,256]{1,0:T(8,128)(2,1)}) custom-call(s32[8]{0:T(128)S(1)} %copy-done.4, f32[256,128]{1,0:T(8,128)S(1)} %copy-done.1, f32[256,128]{1,0:T(8,128)S(1)} %copy-done.3, f32[256,512]{1,0:T(8,128)S(1)} %get-tuple-element.33.own_ref, bf16[256,512]{1,0:T(8,128)(2,1)S(1)} %collective-permute-done.6.refs_0_, ...), custom_call_target="tpu_custom_call" | custom-call | tf_op jit(solution)/shard_map/finish/pallas_call | solution.py:360
  (12 shorter events, 0.0 us)
Async XLA Ops:
  2.9 8.4 %collective-permute-start = (bf16[256,256]{1,0:T(8,128)(2,1)}, bf16[256,256]{1,0:T(8,128)(2,1)S(1)}, u32[]{:S(2)}, u32[]{:S(2)}) collective-permute-start(bf16[256,256]{1,0:T(8,128)(2,1)} %get-tuple-element.27.refs_0_), channel_id=1, source_target_pairs={{0,4},{4,8},{8,12},{1,5},{5,9},{9,13},{2,6},{6,10},{10,14},{3,7},{... | collective-permute-start | bytes 393224 | tf_op jit(solution)/shard_map/ppermute | solution.py:378
  7.8 6.3 %collective-permute-start.3 = (bf16[256,256]{1,0:T(8,128)(2,1)}, bf16[256,256]{1,0:T(8,128)(2,1)S(1)}, u32[]{:S(2)}, u32[]{:S(2)}) collective-permute-start(bf16[256,256]{1,0:T(8,128)(2,1)} %get-tuple-element.28.refs_4_), channel_id=1, source_target_pairs={{0,4},{4,8},{8,12},{1,5},{5,9},{9,13},{2,6},{6,10},{10,14},{3,7},{... | collective-permute-start | bytes 393224 | tf_op jit(solution)/shard_map/ppermute | solution.py:378
  11.3 3.5 %collective-permute-start.1 = (bf16[256,256]{1,0:T(8,128)(2,1)S(1)}, bf16[256,256]{1,0:T(8,128)(2,1)S(1)}, u32[]{:S(2)}, u32[]{:S(2)}) collective-permute-start(bf16[256,256]{1,0:T(8,128)(2,1)S(1)} %collective-permute-done.refs_1_), channel_id=1, source_target_pairs={{4,8},{8,12},{5,9},{9,13},{6,10},{10,14},{7,11},{11,15},{20,24},{2... | collective-permute-start | bytes 393224 | tf_op jit(solution)/shard_map/ppermute | solution.py:378
  14.1 1.4 %collective-permute-start.4 = (bf16[256,256]{1,0:T(8,128)(2,1)S(1)}, bf16[256,256]{1,0:T(8,128)(2,1)S(1)}, u32[]{:S(2)}, u32[]{:S(2)}) collective-permute-start(bf16[256,256]{1,0:T(8,128)(2,1)S(1)} %collective-permute-done.3.refs_5_), channel_id=1, source_target_pairs={{4,8},{8,12},{5,9},{9,13},{6,10},{10,14},{7,11},{11,15},{20,24},{2... | collective-permute-start | bytes 393224 | tf_op jit(solution)/shard_map/ppermute | solution.py:378
  14.8 6.8 %collective-permute-start.2 = (bf16[256,256]{1,0:T(8,128)(2,1)S(1)}, bf16[256,256]{1,0:T(8,128)(2,1)S(1)}, u32[]{:S(2)}, u32[]{:S(2)}) collective-permute-start(bf16[256,256]{1,0:T(8,128)(2,1)S(1)} %collective-permute-done.1.refs_2_), channel_id=1, source_target_pairs={{8,12},{9,13},{10,14},{11,15},{24,28},{25,29},{26,30},{27,31}} | collective-permute-start | bytes 393224 | tf_op jit(solution)/shard_map/ppermute | solution.py:378
  15.5 6.1 %collective-permute-start.5 = (bf16[256,256]{1,0:T(8,128)(2,1)S(1)}, bf16[256,256]{1,0:T(8,128)(2,1)S(1)}, u32[]{:S(2)}, u32[]{:S(2)}) collective-permute-start(bf16[256,256]{1,0:T(8,128)(2,1)S(1)} %collective-permute-done.4.refs_6_), channel_id=1, source_target_pairs={{8,12},{9,13},{10,14},{11,15},{24,28},{25,29},{26,30},{27,31}} | collective-permute-start | bytes 393224 | tf_op jit(solution)/shard_map/ppermute | solution.py:378
  16.2 0.9 %copy-start = (f32[256,128]{1,0:T(8,128)S(1)}, f32[256,128]{1,0:T(8,128)}, u32[]{:S(2)}) copy-start(f32[256,128]{1,0:T(8,128)} %get-tuple-element.22.cos_ref) | copy-start | bytes 393220
  17.1 0.9 %copy-start.2 = (f32[256,128]{1,0:T(8,128)S(1)}, f32[256,128]{1,0:T(8,128)}, u32[]{:S(2)}) copy-start(f32[256,128]{1,0:T(8,128)} %get-tuple-element.23.sin_ref) | copy-start | bytes 393220
  18.0 1.2 %copy-start.5 = (bf16[1,256,2048]{2,1,0:T(8,128)(2,1)S(1)}, bf16[1,256,2048]{2,1,0:T(8,128)(2,1)}, u32[]{:S(2)}) copy-start(bf16[1,256,2048]{2,1,0:T(8,128)(2,1)} %param.7) | copy-start | bytes 3145732
  19.2 1.2 %copy-start.6 = (bf16[1,256,2048]{2,1,0:T(8,128)(2,1)S(1)}, bf16[1,256,2048]{2,1,0:T(8,128)(2,1)}, u32[]{:S(2)}) copy-start(bf16[1,256,2048]{2,1,0:T(8,128)(2,1)} %param.10) | copy-start | bytes 3145732
  20.4 1.2 %copy-start.4 = (s32[8]{0:T(128)S(1)}, s32[8]{0:T(128)}, u32[]{:S(2)}) copy-start(s32[8]{0:T(128)} %get-tuple-element.21.meta_ref) | copy-start | bytes 100
  20.4 1.2 %copy-start.7 = (bf16[1,256,2048]{2,1,0:T(8,128)(2,1)S(1)}, bf16[1,256,2048]{2,1,0:T(8,128)(2,1)}, u32[]{:S(2)}) copy-start(bf16[1,256,2048]{2,1,0:T(8,128)(2,1)} %param.10) | copy-start | bytes 3145732
  20.4 1.2 %copy-start.8 = (bf16[256,256]{1,0:T(8,128)(2,1)S(1)}, bf16[256,256]{1,0:T(8,128)(2,1)}, u32[]{:S(2)}) copy-start(bf16[256,256]{1,0:T(8,128)(2,1)} %get-tuple-element.27.refs_0_) | copy-start | bytes 393220
  20.5 1.3 %copy-start.9 = (bf16[256,256]{1,0:T(8,128)(2,1)S(1)}, bf16[256,256]{1,0:T(8,128)(2,1)}, u32[]{:S(2)}) copy-start(bf16[256,256]{1,0:T(8,128)(2,1)} %get-tuple-element.28.refs_4_) | copy-start | bytes 393220
  21.7 27.2 %copy-start.1 = (f32[256,128]{1,0:T(8,128)S(1)}, f32[256,128]{1,0:T(8,128)}, u32[]{:S(2)}) copy-start(f32[256,128]{1,0:T(8,128)} %get-tuple-element.22.cos_ref) | copy-start | bytes 393220
  21.7 27.2 %copy-start.3 = (f32[256,128]{1,0:T(8,128)S(1)}, f32[256,128]{1,0:T(8,128)}, u32[]{:S(2)}) copy-start(f32[256,128]{1,0:T(8,128)} %get-tuple-element.23.sin_ref) | copy-start | bytes 393220
  31.3 16.0 %collective-permute-start.6 = (bf16[256,512]{1,0:T(8,128)(2,1)S(1)}, bf16[256,512]{1,0:T(8,128)(2,1)S(1)}, u32[]{:S(2)}, u32[]{:S(2)}) collective-permute-start(bf16[256,512]{1,0:T(8,128)(2,1)S(1)} %get-tuple-element.34), channel_id=1, source_target_pairs={{12,8},{8,4},{4,0},{13,9},{9,5},{5,1},{14,10},{10,6},{6,2},{15,11}... | collective-permute-start | bytes 786440 | tf_op jit(solution)/shard_map/ppermute | solution.py:383
  32.6 20.1 %collective-permute-start.7 = (bf16[256,512]{1,0:T(8,128)(2,1)S(1)}, bf16[256,512]{1,0:T(8,128)(2,1)S(1)}, u32[]{:S(2)}, u32[]{:S(2)}) collective-permute-start(bf16[256,512]{1,0:T(8,128)(2,1)S(1)} %get-tuple-element.35), channel_id=1, source_target_pairs={{12,4},{13,5},{14,6},{15,7},{28,20},{29,21},{30,22},{31,23}} | collective-permute-start | bytes 786440 | tf_op jit(solution)/shard_map/ppermute | solution.py:384
  47.4 17.0 %collective-permute-start.8 = (bf16[256,512]{1,0:T(8,128)(2,1)S(1)}, bf16[256,512]{1,0:T(8,128)(2,1)S(1)}, u32[]{:S(2)}, u32[]{:S(2)}) collective-permute-start(bf16[256,512]{1,0:T(8,128)(2,1)S(1)} %add_convert_fusion), channel_id=1, source_target_pairs={{12,8},{8,0},{13,9},{9,1},{14,10},{10,2},{15,11},{11,3},{28,24},{2... | collective-permute-start | bytes 786440 | tf_op jit(solution)/shard_map/ppermute | solution.py:386

commit v5 on v4

--- a/solution.py
+++ b/solution.py
@@ -70,9 +70,9 @@
 
 
 def prepare_kernel(
-    ctx_size, rows_hbm, pos_hbm, keys_hbm, values_hbm, meta_ref, cos_ref, sin_ref, *refs
+    ctx_size, rows_hbm, pos_hbm, keys_hbm, values_hbm, meta_ref, cos_ref, sin_ref, sent_ref, *refs
 ):
-    sent_refs, (rows_ref, pos_ref, keys_ref, values_ref, sems) = refs[:-5], refs[-5:]
+    rows_ref, pos_ref, keys_ref, values_ref, sems = refs
     sources = (pos_hbm, rows_hbm, keys_hbm, values_hbm)
     targets = (pos_ref, rows_ref, keys_ref, values_ref)
     copies = [
@@ -96,18 +96,19 @@
     sin_ref[...] = sin_full
     copies[2].wait()
     copies[3].wait()
-    for head, sent_ref in enumerate(sent_refs):
-        lanes = slice(head * HEAD_DIM, (head + 1) * HEAD_DIM)
+    for lane in range(0, keys_ref.shape[1], HEAD_DIM):
+        lanes = slice(lane, lane + HEAD_DIM)
         key = turn(keys_ref[:, lanes].astype(jnp.float32), cos_full, sin_full)
-        sent_ref[:, :HEAD_DIM] = key.astype(jnp.bfloat16)
-        sent_ref[:, HEAD_DIM:] = values_ref[:, lanes]
+        middle = 2 * lane + HEAD_DIM
+        sent_ref[:, 2 * lane : middle] = key.astype(jnp.bfloat16)
+        sent_ref[:, middle : middle + HEAD_DIM] = values_ref[:, lanes]
 
 
 def prepare(positions, keys, values, ctx_size):
     slots, width = keys.shape
     rows = jnp.asarray(rope_rows())
     table = jax.ShapeDtypeStruct((slots, HEAD_DIM), jnp.float32)
-    sent = jax.ShapeDtypeStruct((slots, 2 * HEAD_DIM), jnp.bfloat16)
+    sent = jax.ShapeDtypeStruct((slots, 2 * width), jnp.bfloat16)
     operands = (rows, positions, keys, values)
     return pl.pallas_call(
         functools.partial(prepare_kernel, ctx_size),
@@ -115,10 +116,10 @@
             jax.ShapeDtypeStruct((2 * ctx_size,), jnp.int32),
             table,
             table,
-            *[sent] * (width // HEAD_DIM),
+            sent,
         ),
         in_specs=[pl.BlockSpec(memory_space=pl.ANY)] * 4,
-        out_specs=(SMEM,) + (VMEM,) * (2 + width // HEAD_DIM),
+        out_specs=(SMEM, VMEM, VMEM, VMEM),
         scratch_shapes=[pltpu.VMEM(operand.shape, operand.dtype) for operand in operands]
         + [pltpu.SemaphoreType.DMA((4,))],
         compiler_params=vmem(positions.shape[1], 60, 60),
@@ -167,9 +168,11 @@
 
 
 def scores_kernel(ctx_size, key_heads, step_heads, meta_ref, turned_ref, grad_ref, turned_t_ref, grad_t_ref, *refs):
-    blocks, refs = refs[: ctx_size * key_heads], refs[ctx_size * key_heads :]
+    inputs = refs[: -6 - ctx_size]
+    refs = refs[len(inputs) :]
     terms, refs = refs[: ctx_size - 1], refs[ctx_size - 1 :]
     score_grad_ref, own_prob_ref, key_t_ref, key_ref, bias_ref, prob_ref, acc_ref = refs
+    blocks = [block[...] for block in inputs]
     slots = turned_ref.shape[0]
     span = bias_ref.shape[0]
     width = key_heads * HEAD_DIM
@@ -179,13 +182,13 @@
     sent_hops = list(range(1, ctx_size))
     if relayed(ctx_size):
         last = lax.axis_index("ctx") == ctx_size - 1
+        own, alpha, beta, gamma, delta = blocks
+        blocks = [own, jnp.where(last, alpha, gamma), jnp.where(last, beta, alpha), delta]
         sent_hops = [jnp.where(last, 3, 1), 2, jnp.where(last, 1, 2)]
 
     key_ref[...] = jnp.zeros_like(key_ref)
     for hop in range(ctx_size - 1, -1, -1):
-        for head in range(key_heads):
-            lanes = slice(2 * head * HEAD_DIM, 2 * (head + 1) * HEAD_DIM)
-            key_ref[pl.ds(starts[hop], slots), lanes] = blocks[head * ctx_size + hop][...]
+        key_ref[pl.ds(starts[hop], slots), :] = blocks[hop]
     place = lax.broadcasted_iota(jnp.int32, (span, slots), 0)
     slot_id = lax.broadcasted_iota(jnp.int32, (span, slots), 1)
     seen = (place >= my_start) & (place - slot_id <= my_start)
@@ -245,10 +248,9 @@
     return ctx_size == 4
 
 
-def scores(meta, turned, out_grad, turned_t, grad_t, blocks, routed):
-    key_heads, ctx_size = len(blocks), len(blocks[0])
-    slots = turned.shape[0]
-    width = 2 * key_heads * HEAD_DIM
+def scores(meta, turned, out_grad, turned_t, grad_t, blocks, routed, ctx_size):
+    slots, width = blocks[0].shape
+    key_heads = width // HEAD_DIM // 2
     heads = turned.shape[1] // HEAD_DIM // key_heads
     span = -(-(routed + ctx_size * ALIGN) // CHUNK) * CHUNK
     terms = [jax.ShapeDtypeStruct((slots, width), jnp.bfloat16)] * (ctx_size - 1)
@@ -262,7 +264,7 @@
             jax.ShapeDtypeStruct((key_heads, slots, heads * slots), jnp.bfloat16),
             jax.ShapeDtypeStruct((key_heads * HEAD_DIM, span), jnp.bfloat16),
         ),
-        in_specs=[SMEM] + [VMEM] * (4 + ctx_size * key_heads),
+        in_specs=[SMEM] + [VMEM] * (4 + len(blocks)),
         out_specs=(VMEM,) * (ctx_size + 2),
         scratch_shapes=[
             pltpu.VMEM((span + slots, width), jnp.bfloat16),
@@ -275,7 +277,7 @@
             flops=12 * 10**9, bytes_accessed=12 * 1024 * 1024, transcendentals=0
         ),
         name="scores",
-    )(meta, turned, out_grad, turned_t, grad_t, *[block for head in blocks for block in head])
+    )(meta, turned, out_grad, turned_t, grad_t, *blocks)
     return outs[: ctx_size - 1], outs[ctx_size - 1 :]
 
 
@@ -289,10 +291,13 @@
     score_grad_ref,
     own_prob_ref,
     key_t_ref,
-    dq_ref,
-    own_ref,
-    shift_ref,
+    *refs,
 ):
+    later = (len(refs) - 3) // 2
+    dq_ref, own_ref = refs[later : later + 2]
+    shift_ref = refs[-1]
+    for index in range(later):
+        refs[later + 2 + index][...] = refs[index][...]
     slots = turned_ref.shape[0]
     heads = turned_ref.shape[1] // HEAD_DIM // key_heads
     first_row = own_rows(meta_ref[0], score_grad_ref.shape[1], slots)
@@ -316,7 +321,7 @@
     own_ref[...] = shift_ref[pl.ds(shift, slots), :]
 
 
-def local_terms(meta, cos_full, sin_full, turned, out_grad, score_grad, own_prob, key_t):
+def local_terms(meta, cos_full, sin_full, turned, out_grad, score_grad, own_prob, key_t, later):
     slots = turned.shape[0]
     key_heads = score_grad.shape[0]
     return pl.pallas_call(
@@ -324,16 +329,17 @@
         out_shape=(
             jax.ShapeDtypeStruct(turned.shape, jnp.bfloat16),
             jax.ShapeDtypeStruct((slots, 2 * key_heads * HEAD_DIM), jnp.float32),
-        ),
-        in_specs=[SMEM] + [VMEM] * 7,
-        out_specs=(VMEM, VMEM),
+            *[jax.ShapeDtypeStruct(term.shape, term.dtype) for term in later],
+        ),
+        in_specs=[SMEM] + [VMEM] * (7 + len(later)),
+        out_specs=(VMEM,) * (2 + len(later)),
         scratch_shapes=[pltpu.VMEM((2 * slots, 2 * key_heads * HEAD_DIM), jnp.float32)],
         compiler_params=vmem(key_t.shape[1] // 2, 24, 48),
         cost_estimate=pl.CostEstimate(
             flops=5 * 10**9, bytes_accessed=10 * 1024 * 1024, transcendentals=0
         ),
         name="local_terms",
-    )(meta, cos_full, sin_full, turned, out_grad, score_grad, own_prob, key_t)
+    )(meta, cos_full, sin_full, turned, out_grad, score_grad, own_prob, key_t, *later)
 
 
 def finish_kernel(ctx_size, meta_ref, cos_ref, sin_ref, own_ref, *refs):
@@ -371,7 +377,12 @@
     return slice(part * size, (part + 1) * size)
 
 
-def climb(sent, ctx_size):
+def spread(sent, ctx_size):
+    if relayed(ctx_size):
+        alpha = lax.ppermute(sent, "ctx", [(0, 2), (2, 3)])
+        beta = lax.ppermute(sent, "ctx", [(1, 3)])
+        gamma = lax.ppermute(sent, "ctx", [(0, 1), (1, 2)])
+        return [sent, alpha, beta, gamma, lax.ppermute(alpha, "ctx", [(2, 3)])]
     blocks = [sent]
     for hop in range(1, ctx_size):
         pairs = [(shard, shard + 1) for shard in range(hop - 1, ctx_size - 1)]
@@ -379,11 +390,10 @@
     return blocks
 
 
-def relay(first, second, third):
+def relay_first(first, third):
     first = lax.ppermute(first, "ctx", [(3, 2), (2, 1), (1, 0)])
-    second = lax.ppermute(second, "ctx", [(3, 1)])
     third = (third + first.astype(jnp.float32)).astype(jnp.bfloat16)
-    return [first, second, lax.ppermute(third, "ctx", [(3, 2), (2, 0)])]
+    return [first, lax.ppermute(third, "ctx", [(3, 2), (2, 0)])]
 
 
 def descend(terms, ctx_size):
@@ -397,11 +407,11 @@
 def body(positions, queries, keys, values, out_grad):
     ctx_size = lax.axis_size("ctx")
     routed = positions.shape[1]
-    meta, cos_full, sin_full, *sent = prepare(positions, keys[0], values[0], ctx_size)
-    blocks = [climb(head, ctx_size) for head in sent]
+    meta, cos_full, sin_full, sent = prepare(positions, keys[0], values[0], ctx_size)
+    blocks = spread(sent, ctx_size)
     turned, turned_t, grad_t = rotate_queries(cos_full, sin_full, queries[0], out_grad[0])
-    parts = 1 if routed <= 512 else len(sent)
-    wide, key_heads = queries.shape[2] // parts, len(sent) // parts
+    parts = 1 if routed <= 512 else keys.shape[2] // HEAD_DIM
+    wide, narrow = queries.shape[2] // parts, sent.shape[1] // parts
     terms, local = [], []
     for part in range(parts):
         columns = part_of(part, wide)
@@ -411,22 +421,34 @@
             out_grad[0][:, columns],
             turned_t[columns],
             grad_t[columns],
-            blocks[part_of(part, key_heads)],
+            [block[:, part_of(part, narrow)] for block in blocks],
             routed,
+            ctx_size,
         )
         terms.append(outs[0])
         local.append(outs[1])
     terms = [jnp.concatenate(term, axis=1) for term in zip(*terms)]
-    arrived = relay(*terms) if relayed(ctx_size) else descend(terms, ctx_size)
+    if relayed(ctx_size):
+        arrived, later = relay_first(terms[0], terms[2]), [terms[1]]
+    else:
+        arrived, later = descend(terms, ctx_size), []
     finals = []
     for part in range(parts):
         columns = part_of(part, wide)
         finals.append(
             local_terms(
-                meta, cos_full, sin_full, turned[:, columns], out_grad[0][:, columns], *local[part]
+                meta,
+                cos_full,
+                sin_full,
+                turned[:, columns],
+                out_grad[0][:, columns],
+                *local[part],
+                later,
             )
         )
-    dq, own = [jnp.concatenate(final, axis=1) for final in zip(*finals)]
+    dq, own = [jnp.concatenate(final, axis=1) for final in zip(*[final[:2] for final in finals])]
+    for term in finals[0][2:]:
+        arrived.append(lax.ppermute(term, "ctx", [(3, 1)]))
     key_grad, value_grad = finish(meta, cos_full, sin_full, own, arrived)
     return (dq[None], key_grad[None], value_grad[None])
 

time: 66.4 us -> 63.8 us (0.961); the launches traced: 65.8 us -> 62.5 us
  starting transfers between devices: 14.5 us -> 11.9 us
  waiting for transfers between devices: 27.9 us -> 27.1 us
    ppermute x9 -> x7, starting transfers between devices: 14.5 us -> 11.9 us  [the longest x1 5.96 us: spread(): alpha = lax.ppermute(sent, 'ctx', [(0, 2), (2, 3)])]
    ppermute x9 -> x7, waiting for transfers between devices: 27.9 us -> 27.1 us  [the longest x1 12.6 us: relay_first(): return [first, lax.ppermute(third, 'ctx', [(3, 2), (2, 0)])]]
    unnamed x20 -> x18, local copies, waits for them, and re-layouts: 4.33 us -> 4.33 us
  transfers between devices with their start and end apart: 9 -> 7, of which waited for: 3 -> 3; matrix products, arithmetic and copies ran while one was open for 0% -> 0% of each run, Pallas kernels for 8% -> 8%
where the time goes in v5:
time: 63.8 us; the launch traced here: 62.5 us
  waiting for transfers between devices  27.1 us (42%)
  Pallas kernels  18.4 us (29%)
  starting transfers between devices  11.9 us (19%)
  local copies, waits for them, and re-layouts  4.33 us (7%)
  between operations  0.78 us (1%)
    ppermute x1, waiting for transfers between devices, relay_first(): return [first, lax.ppermute(third, 'ctx', [(3, 2), (2, 0)])]  12.6 us
    pallas_call x1, Pallas kernels, scores(): pl.pallas_call(functools.partial(scores_kernel, ctx_size, key_heads, 4 if...  9.68 us
    ppermute x1, waiting for transfers between devices, relay_first(): first = lax.ppermute(first, 'ctx', [(3, 2), (2, 1), (1, 0)])  9.51 us
    ppermute x1, starting transfers between devices, spread(): alpha = lax.ppermute(sent, 'ctx', [(0, 2), (2, 3)])  5.96 us
    ppermute x1, waiting for transfers between devices, spread(): alpha = lax.ppermute(sent, 'ctx', [(0, 2), (2, 3)])  5.04 us
    unnamed x18, local copies, waits for them, and re-layouts  4.33 us
    pallas_call x1, Pallas kernels, local_terms(): pl.pallas_call(functools.partial(local_kernel, key_heads), out_shape=(jax...  3.85 us
    pallas_call x1, Pallas kernels, prepare(): pl.pallas_call(functools.partial(prepare_kernel, ctx_size), out_shape=(ja...  2.28 us
  transfers between devices with their start and end apart: 7, of which 3 were waited for; matrix products, arithmetic and copies ran while one was open for 0% of the time, Pallas kernels for 8%

profile of v5, /device:TPU:0, one launch (start us, length us, event | category | flops | bytes accessed | tf_op | source)
XLA Modules:
  0.0 62.5 jit_solution(11864817472475386932)
XLA Ops:
  0.6 2.3 %prepare.1 = (s32[8]{0:T(128)}, f32[256,128]{1,0:T(8,128)}, f32[256,128]{1,0:T(8,128)}, bf16[256,512]{1,0:T(8,128)(2,1)}) custom-call(f32[2,128]{1,0:T(2,128)} %constant.2.clone.rows_hbm, s32[1,512]{1,0:T(1,128)} %pos_hbm.1, bf16[256,256]{1,0:T(8,128)(2,1)} %bitcast.11, bf16[256,256]{1,0:T(8,128)(2,1)} %bitcast.12), custom_call_target="tpu_custom_call" | custom-call | tf_op jit(solution)/shard_map/prepare/pallas_call | solution.py:113
  2.9 6.0 %collective-permute-start = (bf16[256,512]{1,0:T(8,128)(2,1)}, bf16[256,512]{1,0:T(8,128)(2,1)S(1)}, u32[]{:S(2)}, u32[]{:S(2)}) collective-permute-start(bf16[256,512]{1,0:T(8,128)(2,1)} %get-tuple-element.27.refs_0_), channel_id=1, source_target_pairs={{0,8},{8,12},{1,9},{9,13},{2,10},{10,14},{3,11},{11,15},{16,24},{2... | collective-permute-start | bytes 786440 | tf_op jit(solution)/shard_map/ppermute | solution.py:382
  8.9 1.3 %collective-permute-start.2 = (bf16[256,512]{1,0:T(8,128)(2,1)}, bf16[256,512]{1,0:T(8,128)(2,1)S(1)}, u32[]{:S(2)}, u32[]{:S(2)}) collective-permute-start(bf16[256,512]{1,0:T(8,128)(2,1)} %get-tuple-element.27.refs_0_), channel_id=1, source_target_pairs={{0,4},{4,8},{1,5},{5,9},{2,6},{6,10},{3,7},{7,11},{16,20},{20,24},... | collective-permute-start | bytes 786440 | tf_op jit(solution)/shard_map/ppermute | solution.py:384
  10.2 0.7 %collective-permute-start.1 = (bf16[256,512]{1,0:T(8,128)(2,1)}, bf16[256,512]{1,0:T(8,128)(2,1)S(1)}, u32[]{:S(2)}, u32[]{:S(2)}) collective-permute-start(bf16[256,512]{1,0:T(8,128)(2,1)} %get-tuple-element.27.refs_0_), channel_id=1, source_target_pairs={{4,12},{5,13},{6,14},{7,15},{20,28},{21,29},{22,30},{23,31}} | collective-permute-start | bytes 786440 | tf_op jit(solution)/shard_map/ppermute | solution.py:383
  10.9 5.0 %collective-permute-done.refs_1_ = bf16[256,512]{1,0:T(8,128)(2,1)S(1)} collective-permute-done((bf16[256,512]{1,0:T(8,128)(2,1)}, bf16[256,512]{1,0:T(8,128)(2,1)S(1)}, u32[]{:S(2)}, u32[]{:S(2)}) %collective-permute-start) | collective-permute-done | bytes 262176 | tf_op jit(solution)/shard_map/ppermute | solution.py:382
  15.9 0.7 %collective-permute-start.3 = (bf16[256,512]{1,0:T(8,128)(2,1)S(1)}, bf16[256,512]{1,0:T(8,128)(2,1)S(1)}, u32[]{:S(2)}, u32[]{:S(2)}) collective-permute-start(bf16[256,512]{1,0:T(8,128)(2,1)S(1)} %collective-permute-done.refs_1_), channel_id=1, source_target_pairs={{8,12},{9,13},{10,14},{11,15},{24,28},{25,29},{26,30},{27,31}} | collective-permute-start | bytes 786440 | tf_op jit(solution)/shard_map/ppermute | solution.py:385
  16.6 0.0 copy-start
  16.6 0.9 %copy-done = f32[256,128]{1,0:T(8,128)S(1)} copy-done((f32[256,128]{1,0:T(8,128)S(1)}, f32[256,128]{1,0:T(8,128)}, u32[]{:S(2)}) %copy-start) | copy-done | bytes 131096
  17.5 0.0 copy-start.2
  17.5 0.9 %copy-done.2 = f32[256,128]{1,0:T(8,128)S(1)} copy-done((f32[256,128]{1,0:T(8,128)S(1)}, f32[256,128]{1,0:T(8,128)}, u32[]{:S(2)}) %copy-start.2) | copy-done | bytes 131096
  18.4 0.0 copy-start.5
  18.4 1.2 %copy-done.5 = bf16[1,256,2048]{2,1,0:T(8,128)(2,1)S(1)} copy-done((bf16[1,256,2048]{2,1,0:T(8,128)(2,1)S(1)}, bf16[1,256,2048]{2,1,0:T(8,128)(2,1)}, u32[]{:S(2)}) %copy-start.5) | copy-done | bytes 1048600
  19.6 1.2 %copy-done.6 = bf16[1,256,2048]{2,1,0:T(8,128)(2,1)S(1)} copy-done((bf16[1,256,2048]{2,1,0:T(8,128)(2,1)S(1)}, bf16[1,256,2048]{2,1,0:T(8,128)(2,1)}, u32[]{:S(2)}) %copy-start.6) | copy-done | bytes 1048600
  20.9 1.1 %rotate_queries.1 = (bf16[256,2048]{1,0:T(8,128)(2,1)S(1)}, bf16[2048,256]{1,0:T(8,128)(2,1)S(1)}, bf16[2048,256]{1,0:T(8,128)(2,1)S(1)}) custom-call(f32[256,128]{1,0:T(8,128)S(1)} %copy-done, f32[256,128]{1,0:T(8,128)S(1)} %copy-done.2, bf16[256,2048]{1,0:T(8,128)(2,1)S(1)} %bitcast.7, bf16[256,2048]{1,0:T(8,128)(2,1)S(1)} %bitcast.8), custom_call_target="tpu_custom_call" | custom-call | flops 4000000000 | bytes 5242880 | tf_op jit(solution)/shard_map/rotate_queries/pallas_call | solution.py:143
  22.0 0.0 collective-permute-done.2.refs_3_
  22.0 0.0 collective-permute-done.1.refs_2_
  22.0 0.0 collective-permute-done.3.refs_4_
  22.0 0.0 copy-done.4
  22.1 0.0 copy-done.7
  22.1 0.0 copy-done.8
  22.1 9.7 %scores.1 = (bf16[256,512]{1,0:T(8,128)(2,1)S(1)}, bf16[256,512]{1,0:T(8,128)(2,1)S(1)}, f32[256,512]{1,0:T(8,128)S(1)}, bf16[2,576,2048]{2,1,0:T(8,128)(2,1)S(1...) custom-call(s32[8]{0:T(128)S(1)} %copy-done.4, bf16[256,2048]{1,0:T(8,128)(2,1)S(1)} %get-tuple-element.24.turned_ref, ...), custom_call_target="tpu_custom_call" | custom-call | flops 12000000000 | bytes 12582912 | tf_op jit(solution)/shard_map/scores/pallas_call | solution.py:259
  31.8 1.3 %collective-permute-start.4 = (bf16[256,512]{1,0:T(8,128)(2,1)S(1)}, bf16[256,512]{1,0:T(8,128)(2,1)S(1)}, u32[]{:S(2)}, u32[]{:S(2)}) collective-permute-start(bf16[256,512]{1,0:T(8,128)(2,1)S(1)} %get-tuple-element.34), channel_id=1, source_target_pairs={{12,8},{8,4},{4,0},{13,9},{9,5},{5,1},{14,10},{10,6},{6,2},{15,11}... | collective-permute-start | bytes 786440 | tf_op jit(solution)/shard_map/ppermute | solution.py:394
  33.1 0.0 copy-done.1
  33.1 0.0 copy-done.3
  33.1 3.9 %local_terms.1 = (bf16[256,2048]{1,0:T(8,128)(2,1)}, f32[256,512]{1,0:T(8,128)S(1)}, bf16[256,512]{1,0:T(8,128)(2,1)S(1)}) custom-call(s32[8]{0:T(128)S(1)} %copy-done.4, f32[256,128]{1,0:T(8,128)S(1)} %copy-done.1, f32[256,128]{1,0:T(8,128)S(1)} %copy-done.3, bf16[256,2048]{1,0:T(8,128)(2,1)S(1)} %get-tuple-element.24.turned_ref, ...), custom_call_target="tpu_custom_call" | custom-call | flops 5000000000 | bytes 10485760 | tf_op jit(solution)/shard_map/local_terms/pallas_call | solution.py:327
  37.0 0.7 %collective-permute-start.6 = (bf16[256,512]{1,0:T(8,128)(2,1)S(1)}, bf16[256,512]{1,0:T(8,128)(2,1)S(1)}, u32[]{:S(2)}, u32[]{:S(2)}) collective-permute-start(bf16[256,512]{1,0:T(8,128)(2,1)S(1)} %get-tuple-element.36), channel_id=1, source_target_pairs={{12,4},{13,5},{14,6},{15,7},{28,20},{29,21},{30,22},{31,23}} | collective-permute-start | bytes 786440 | tf_op jit(solution)/shard_map/ppermute | solution.py:451
  37.7 9.5 %collective-permute-done.4.refs_0_ = bf16[256,512]{1,0:T(8,128)(2,1)S(1)} collective-permute-done((bf16[256,512]{1,0:T(8,128)(2,1)S(1)}, bf16[256,512]{1,0:T(8,128)(2,1)S(1)}, u32[]{:S(2)}, u32[]{:S(2)}) %collective-permute-start.4) | collective-permute-done | bytes 262176 | tf_op jit(solution)/shard_map/ppermute | solution.py:394
  47.2 0.1 add_convert_fusion
  47.2 1.3 %collective-permute-start.5 = (bf16[256,512]{1,0:T(8,128)(2,1)S(1)}, bf16[256,512]{1,0:T(8,128)(2,1)S(1)}, u32[]{:S(2)}, u32[]{:S(2)}) collective-permute-start(bf16[256,512]{1,0:T(8,128)(2,1)S(1)} %add_convert_fusion), channel_id=1, source_target_pairs={{12,8},{8,0},{13,9},{9,1},{14,10},{10,2},{15,11},{11,3},{28,24},{2... | collective-permute-start | bytes 786440 | tf_op jit(solution)/shard_map/ppermute | solution.py:396
  48.5 0.0 collective-permute-done.6.refs_2_
  48.6 12.6 %collective-permute-done.5.refs_1_ = bf16[256,512]{1,0:T(8,128)(2,1)S(1)} collective-permute-done((bf16[256,512]{1,0:T(8,128)(2,1)S(1)}, bf16[256,512]{1,0:T(8,128)(2,1)S(1)}, u32[]{:S(2)}, u32[]{:S(2)}) %collective-permute-start.5) | collective-permute-done | bytes 262176 | tf_op jit(solution)/shard_map/ppermute | solution.py:396
  61.1 1.4 %finish.1 = (bf16[256,256]{1,0:T(8,128)(2,1)}, bf16[256,256]{1,0:T(8,128)(2,1)}) custom-call(s32[8]{0:T(128)S(1)} %copy-done.4, f32[256,128]{1,0:T(8,128)S(1)} %copy-done.1, f32[256,128]{1,0:T(8,128)S(1)} %copy-done.3, f32[256,512]{1,0:T(8,128)S(1)} %get-tuple-element.33.own_ref, bf16[256,512]{1,0:T(8,128)(2,1)S(1)} %collective-permute-done.4.refs_0_, ...), custom_call_target="tpu_custom_call" | custom-call | tf_op jit(solution)/shard_map/finish/pallas_call | solution.py:366
  (6 shorter events, 0.0 us)
Async XLA Ops:
  2.9 13.0 %collective-permute-start = (bf16[256,512]{1,0:T(8,128)(2,1)}, bf16[256,512]{1,0:T(8,128)(2,1)S(1)}, u32[]{:S(2)}, u32[]{:S(2)}) collective-permute-start(bf16[256,512]{1,0:T(8,128)(2,1)} %get-tuple-element.27.refs_0_), channel_id=1, source_target_pairs={{0,8},{8,12},{1,9},{9,13},{2,10},{10,14},{3,11},{11,15},{16,24},{2... | collective-permute-start | bytes 786440 | tf_op jit(solution)/shard_map/ppermute | solution.py:382
  8.9 13.1 %collective-permute-start.2 = (bf16[256,512]{1,0:T(8,128)(2,1)}, bf16[256,512]{1,0:T(8,128)(2,1)S(1)}, u32[]{:S(2)}, u32[]{:S(2)}) collective-permute-start(bf16[256,512]{1,0:T(8,128)(2,1)} %get-tuple-element.27.refs_0_), channel_id=1, source_target_pairs={{0,4},{4,8},{1,5},{5,9},{2,6},{6,10},{3,7},{7,11},{16,20},{20,24},... | collective-permute-start | bytes 786440 | tf_op jit(solution)/shard_map/ppermute | solution.py:384
  10.2 11.8 %collective-permute-start.1 = (bf16[256,512]{1,0:T(8,128)(2,1)}, bf16[256,512]{1,0:T(8,128)(2,1)S(1)}, u32[]{:S(2)}, u32[]{:S(2)}) collective-permute-start(bf16[256,512]{1,0:T(8,128)(2,1)} %get-tuple-element.27.refs_0_), channel_id=1, source_target_pairs={{4,12},{5,13},{6,14},{7,15},{20,28},{21,29},{22,30},{23,31}} | collective-permute-start | bytes 786440 | tf_op jit(solution)/shard_map/ppermute | solution.py:383
  15.9 6.1 %collective-permute-start.3 = (bf16[256,512]{1,0:T(8,128)(2,1)S(1)}, bf16[256,512]{1,0:T(8,128)(2,1)S(1)}, u32[]{:S(2)}, u32[]{:S(2)}) collective-permute-start(bf16[256,512]{1,0:T(8,128)(2,1)S(1)} %collective-permute-done.refs_1_), channel_id=1, source_target_pairs={{8,12},{9,13},{10,14},{11,15},{24,28},{25,29},{26,30},{27,31}} | collective-permute-start | bytes 786440 | tf_op jit(solution)/shard_map/ppermute | solution.py:385
  16.6 0.9 %copy-start = (f32[256,128]{1,0:T(8,128)S(1)}, f32[256,128]{1,0:T(8,128)}, u32[]{:S(2)}) copy-start(f32[256,128]{1,0:T(8,128)} %get-tuple-element.22.cos_ref) | copy-start | bytes 393220
  17.5 0.9 %copy-start.2 = (f32[256,128]{1,0:T(8,128)S(1)}, f32[256,128]{1,0:T(8,128)}, u32[]{:S(2)}) copy-start(f32[256,128]{1,0:T(8,128)} %get-tuple-element.23.sin_ref) | copy-start | bytes 393220
  18.4 1.2 %copy-start.5 = (bf16[1,256,2048]{2,1,0:T(8,128)(2,1)S(1)}, bf16[1,256,2048]{2,1,0:T(8,128)(2,1)}, u32[]{:S(2)}) copy-start(bf16[1,256,2048]{2,1,0:T(8,128)(2,1)} %param.7) | copy-start | bytes 3145732
  19.6 1.2 %copy-start.6 = (bf16[1,256,2048]{2,1,0:T(8,128)(2,1)S(1)}, bf16[1,256,2048]{2,1,0:T(8,128)(2,1)}, u32[]{:S(2)}) copy-start(bf16[1,256,2048]{2,1,0:T(8,128)(2,1)} %param.10) | copy-start | bytes 3145732
  20.9 1.2 %copy-start.4 = (s32[8]{0:T(128)S(1)}, s32[8]{0:T(128)}, u32[]{:S(2)}) copy-start(s32[8]{0:T(128)} %get-tuple-element.21.meta_ref) | copy-start | bytes 100
  20.9 1.2 %copy-start.7 = (bf16[1,256,2048]{2,1,0:T(8,128)(2,1)S(1)}, bf16[1,256,2048]{2,1,0:T(8,128)(2,1)}, u32[]{:S(2)}) copy-start(bf16[1,256,2048]{2,1,0:T(8,128)(2,1)} %param.10) | copy-start | bytes 3145732
  20.9 1.3 %copy-start.8 = (bf16[256,512]{1,0:T(8,128)(2,1)S(1)}, bf16[256,512]{1,0:T(8,128)(2,1)}, u32[]{:S(2)}) copy-start(bf16[256,512]{1,0:T(8,128)(2,1)} %get-tuple-element.27.refs_0_) | copy-start | bytes 786436
  22.1 11.0 %copy-start.1 = (f32[256,128]{1,0:T(8,128)S(1)}, f32[256,128]{1,0:T(8,128)}, u32[]{:S(2)}) copy-start(f32[256,128]{1,0:T(8,128)} %get-tuple-element.22.cos_ref) | copy-start | bytes 393220
  22.1 11.0 %copy-start.3 = (f32[256,128]{1,0:T(8,128)S(1)}, f32[256,128]{1,0:T(8,128)}, u32[]{:S(2)}) copy-start(f32[256,128]{1,0:T(8,128)} %get-tuple-element.23.sin_ref) | copy-start | bytes 393220
  31.8 15.4 %collective-permute-start.4 = (bf16[256,512]{1,0:T(8,128)(2,1)S(1)}, bf16[256,512]{1,0:T(8,128)(2,1)S(1)}, u32[]{:S(2)}, u32[]{:S(2)}) collective-permute-start(bf16[256,512]{1,0:T(8,128)(2,1)S(1)} %get-tuple-element.34), channel_id=1, source_target_pairs={{12,8},{8,4},{4,0},{13,9},{9,5},{5,1},{14,10},{10,6},{6,2},{15,11}... | collective-permute-start | bytes 786440 | tf_op jit(solution)/shard_map/ppermute | solution.py:394
  37.0 11.6 %collective-permute-start.6 = (bf16[256,512]{1,0:T(8,128)(2,1)S(1)}, bf16[256,512]{1,0:T(8,128)(2,1)S(1)}, u32[]{:S(2)}, u32[]{:S(2)}) collective-permute-start(bf16[256,512]{1,0:T(8,128)(2,1)S(1)} %get-tuple-element.36), channel_id=1, source_target_pairs={{12,4},{13,5},{14,6},{15,7},{28,20},{29,21},{30,22},{31,23}} | collective-permute-start | bytes 786440 | tf_op jit(solution)/shard_map/ppermute | solution.py:451
  47.2 13.9 %collective-permute-start.5 = (bf16[256,512]{1,0:T(8,128)(2,1)S(1)}, bf16[256,512]{1,0:T(8,128)(2,1)S(1)}, u32[]{:S(2)}, u32[]{:S(2)}) collective-permute-start(bf16[256,512]{1,0:T(8,128)(2,1)S(1)} %add_convert_fusion), channel_id=1, source_target_pairs={{12,8},{8,0},{13,9},{9,1},{14,10},{10,2},{15,11},{11,3},{28,24},{2... | collective-permute-start | bytes 786440 | tf_op jit(solution)/shard_map/ppermute | solution.py:396

commit v6 on v5

--- a/solution.py
+++ b/solution.py
@@ -22,6 +22,7 @@
 
 VMEM = pl.BlockSpec(memory_space=pltpu.VMEM)
 SMEM = pl.BlockSpec(memory_space=pltpu.SMEM)
+HBM = pl.BlockSpec(memory_space=pltpu.HBM)
 
 
 def vmem(routed, small, large):
@@ -118,7 +119,7 @@
             table,
             sent,
         ),
-        in_specs=[pl.BlockSpec(memory_space=pl.ANY)] * 4,
+        in_specs=[HBM] * 4,
         out_specs=(SMEM, VMEM, VMEM, VMEM),
         scratch_shapes=[pltpu.VMEM(operand.shape, operand.dtype) for operand in operands]
         + [pltpu.SemaphoreType.DMA((4,))],
@@ -127,7 +128,18 @@
     )(*operands)
 
 
-def queries_kernel(cos_ref, sin_ref, query_ref, grad_ref, turned_ref, turned_t_ref, grad_t_ref):
+def queries_kernel(
+    cos_ref,
+    sin_ref,
+    query_ref,
+    grad_ref,
+    sent_ref,
+    turned_ref,
+    turned_t_ref,
+    grad_t_ref,
+    sent_again_ref,
+):
+    sent_again_ref[...] = sent_ref[...]
     for lane in range(0, query_ref.shape[1], HEAD_DIM):
         lanes = slice(lane, lane + HEAD_DIM)
         query = turn(query_ref[:, lanes].astype(jnp.float32), cos_ref[...], sin_ref[...])
@@ -136,21 +148,21 @@
         grad_t_ref[lanes, :] = grad_ref[:, lanes].astype(jnp.float32).T.astype(jnp.bfloat16)
 
 
-def rotate_queries(cos_full, sin_full, queries, out_grad):
+def rotate_queries(cos_full, sin_full, queries, out_grad, sent):
     slots, width = queries.shape
     straight = jax.ShapeDtypeStruct((slots, width), jnp.bfloat16)
     across = jax.ShapeDtypeStruct((width, slots), jnp.bfloat16)
     return pl.pallas_call(
         queries_kernel,
-        out_shape=(straight, across, across),
-        in_specs=[VMEM] * 4,
-        out_specs=(VMEM,) * 3,
+        out_shape=(straight, across, across, jax.ShapeDtypeStruct(sent.shape, sent.dtype)),
+        in_specs=[VMEM] * 5,
+        out_specs=(VMEM,) * 4,
         compiler_params=vmem(0, 16, 16),
         cost_estimate=pl.CostEstimate(
-            flops=4 * 10**9, bytes_accessed=5 * 1024 * 1024, transcendentals=0
+            flops=3 * 10**9, bytes_accessed=4 * 1024 * 1024, transcendentals=0
         ),
         name="rotate_queries",
-    )(cos_full, sin_full, queries, out_grad)
+    )(cos_full, sin_full, queries, out_grad, sent)
 
 
 def stacked(ref, lane, heads):
@@ -161,6 +173,13 @@
 def terms_of(probs, score_grads, queries, grads):
     key_term = dot(score_grads, queries, ((1,), (0,))) * SCORE_SCALE
     return jnp.concatenate([key_term, dot(probs, grads, ((1,), (0,)))], axis=1)
+
+
+def fold(field, join, reduce):
+    while field.shape[0] % 16 == 0:
+        half = field.shape[0] // 2
+        field = join(field[:half], field[half:])
+    return reduce(field, axis=0, keepdims=True)
 
 
 def own_rows(my_start, span, slots):
@@ -214,10 +233,10 @@
                 scores = dot(key_ref[:span, lanes], turned_t_ref[rows, :], ((1,), (0,)))
                 scores = scores + bias_ref[...]
                 prob_grad = dot(key_ref[:span, value_lanes], grad_t_ref[rows, :], ((1,), (0,)))
-                peak = jnp.max(scores, axis=0, keepdims=True)
+                peak = fold(scores, jnp.maximum, jnp.max)
                 weights = jnp.exp2((scores - peak) * EXP2_SCALE)
-                inverse = 1.0 / jnp.sum(weights, axis=0, keepdims=True)
-                delta = jnp.sum(weights * prob_grad, axis=0, keepdims=True) * inverse
+                inverse = 1.0 / fold(weights, jnp.add, jnp.sum)
+                delta = fold(weights * prob_grad, jnp.add, jnp.sum) * inverse
                 prob = weights * jnp.where(live, inverse, 0.0)
                 prob_ref[:, columns] = prob.astype(jnp.bfloat16)
                 score_grad = (prob * (prob_grad - delta)).astype(jnp.bfloat16)
@@ -377,11 +396,11 @@
     return slice(part * size, (part + 1) * size)
 
 
-def spread(sent, ctx_size):
+def spread(sent, sent_again, ctx_size):
     if relayed(ctx_size):
         alpha = lax.ppermute(sent, "ctx", [(0, 2), (2, 3)])
         beta = lax.ppermute(sent, "ctx", [(1, 3)])
-        gamma = lax.ppermute(sent, "ctx", [(0, 1), (1, 2)])
+        gamma = lax.ppermute(sent_again, "ctx", [(0, 1), (1, 2)])
         return [sent, alpha, beta, gamma, lax.ppermute(alpha, "ctx", [(2, 3)])]
     blocks = [sent]
     for hop in range(1, ctx_size):
@@ -408,8 +427,10 @@
     ctx_size = lax.axis_size("ctx")
     routed = positions.shape[1]
     meta, cos_full, sin_full, sent = prepare(positions, keys[0], values[0], ctx_size)
-    blocks = spread(sent, ctx_size)
-    turned, turned_t, grad_t = rotate_queries(cos_full, sin_full, queries[0], out_grad[0])
+    turned, turned_t, grad_t, sent_again = rotate_queries(
+        cos_full, sin_full, queries[0], out_grad[0], sent
+    )
+    blocks = spread(sent, sent_again, ctx_size)
     parts = 1 if routed <= 512 else keys.shape[2] // HEAD_DIM
     wide, narrow = queries.shape[2] // parts, sent.shape[1] // parts
     terms, local = [], []

time: 63.8 us -> 63.8 us (level); the launches traced: 62.5 us -> 63.9 us
  starting transfers between devices: 11.9 us -> 14.1 us
  waiting for transfers between devices: 27.1 us -> 25.3 us
  local copies, waits for them, and re-layouts: 4.33 us -> 5.22 us
    ppermute x1, waiting for transfers between devices: 5.04 us -> 0.01 us  [spread(): alpha = lax.ppermute(sent, 'ctx', [(0, 2), (2, 3)])]
    ppermute x1, waiting for transfers between devices: 0.01 us -> 4.54 us  [spread(): gamma = lax.ppermute(sent_again, 'ctx', [(0, 1), (1, 2)])]
    ppermute x1, waiting for transfers between devices: 9.51 us -> 6.26 us  [relay_first(): first = lax.ppermute(first, 'ctx', [(3, 2), (2, 1), (1, 0)])]
    ppermute x1, starting transfers between devices: 1.31 us -> 3.5 us  [spread(): gamma = lax.ppermute(sent_again, 'ctx', [(0, 1), (1, 2)])]
    ppermute x1, waiting for transfers between devices: 12.6 us -> 14.5 us  [relay_first(): return [first, lax.ppermute(third, 'ctx', [(3, 2), (2, 0)])]]
    unnamed x18 -> x20, local copies, waits for them, and re-layouts: 4.33 us -> 5.22 us
where the time goes in v6:
time: 63.8 us; the launch traced here: 63.9 us
  waiting for transfers between devices  25.3 us (40%)
  Pallas kernels  18.4 us (29%)
  starting transfers between devices  14.1 us (22%)
  local copies, waits for them, and re-layouts  5.22 us (8%)
  between operations  0.79 us (1%)
    ppermute x1, waiting for transfers between devices, relay_first(): return [first, lax.ppermute(third, 'ctx', [(3, 2), (2, 0)])]  14.5 us
    pallas_call x1, Pallas kernels, scores(): pl.pallas_call(functools.partial(scores_kernel, ctx_size, key_heads, 4 if...  9.74 us
    ppermute x1, waiting for transfers between devices, relay_first(): first = lax.ppermute(first, 'ctx', [(3, 2), (2, 1), (1, 0)])  6.26 us
    ppermute x1, starting transfers between devices, spread(): alpha = lax.ppermute(sent, 'ctx', [(0, 2), (2, 3)])  5.96 us
    unnamed x20, local copies, waits for them, and re-layouts  5.22 us
    ppermute x1, waiting for transfers between devices, spread(): gamma = lax.ppermute(sent_again, 'ctx', [(0, 1), (1, 2)])  4.54 us
    pallas_call x1, Pallas kernels, local_terms(): pl.pallas_call(functools.partial(local_kernel, key_heads), out_shape=(jax...  3.85 us
    ppermute x1, starting transfers between devices, spread(): gamma = lax.ppermute(sent_again, 'ctx', [(0, 1), (1, 2)])  3.5 us
  transfers between devices with their start and end apart: 7, of which 3 were waited for; matrix products, arithmetic and copies ran while one was open for 0% of the time, Pallas kernels for 8%

profile of v6, /device:TPU:0, one launch (start us, length us, event | category | flops | bytes accessed | tf_op | source)
XLA Modules:
  0.0 63.9 jit_solution(1801729878209169621)
XLA Ops:
  0.6 2.3 %prepare.1 = (s32[8]{0:T(128)}, f32[256,128]{1,0:T(8,128)}, f32[256,128]{1,0:T(8,128)}, bf16[256,512]{1,0:T(8,128)(2,1)}) custom-call(f32[2,128]{1,0:T(2,128)} %constant.2.clone.rows_hbm, s32[1,512]{1,0:T(1,128)} %pos_hbm.1, bf16[256,256]{1,0:T(8,128)(2,1)} %bitcast.11, bf16[256,256]{1,0:T(8,128)(2,1)} %bitcast.12), custom_call_target="tpu_custom_call" | custom-call | tf_op jit(solution)/shard_map/prepare/pallas_call | solution.py:114
  2.9 0.7 %collective-permute-start.1 = (bf16[256,512]{1,0:T(8,128)(2,1)}, bf16[256,512]{1,0:T(8,128)(2,1)S(1)}, u32[]{:S(2)}, u32[]{:S(2)}) collective-permute-start(bf16[256,512]{1,0:T(8,128)(2,1)} %get-tuple-element.25.sent_ref.refs_0_), channel_id=1, source_target_pairs={{4,12},{5,13},{6,14},{7,15},{20,28},{21,29},{22,30},{23,31}} | collective-permute-start | bytes 786440 | tf_op jit(solution)/shard_map/ppermute | solution.py:402
  3.6 6.0 %collective-permute-start = (bf16[256,512]{1,0:T(8,128)(2,1)}, bf16[256,512]{1,0:T(8,128)(2,1)S(1)}, u32[]{:S(2)}, u32[]{:S(2)}) collective-permute-start(bf16[256,512]{1,0:T(8,128)(2,1)} %get-tuple-element.25.sent_ref.refs_0_), channel_id=1, source_target_pairs={{0,8},{8,12},{1,9},{9,13},{2,10},{10,14},{3,11},{11,15},{16,24},{2... | collective-permute-start | bytes 786440 | tf_op jit(solution)/shard_map/ppermute | solution.py:401
  9.6 0.0 copy-start
  9.6 0.9 %copy-done = f32[256,128]{1,0:T(8,128)S(1)} copy-done((f32[256,128]{1,0:T(8,128)S(1)}, f32[256,128]{1,0:T(8,128)}, u32[]{:S(2)}) %copy-start) | copy-done | bytes 131096
  10.5 0.9 %copy-done.2 = f32[256,128]{1,0:T(8,128)S(1)} copy-done((f32[256,128]{1,0:T(8,128)S(1)}, f32[256,128]{1,0:T(8,128)}, u32[]{:S(2)}) %copy-start.2) | copy-done | bytes 131096
  11.4 1.2 %copy-done.5 = bf16[1,256,2048]{2,1,0:T(8,128)(2,1)S(1)} copy-done((bf16[1,256,2048]{2,1,0:T(8,128)(2,1)S(1)}, bf16[1,256,2048]{2,1,0:T(8,128)(2,1)}, u32[]{:S(2)}) %copy-start.5) | copy-done | bytes 1048600
  12.6 1.2 %copy-done.6 = bf16[1,256,2048]{2,1,0:T(8,128)(2,1)S(1)} copy-done((bf16[1,256,2048]{2,1,0:T(8,128)(2,1)S(1)}, bf16[1,256,2048]{2,1,0:T(8,128)(2,1)}, u32[]{:S(2)}) %copy-start.6) | copy-done | bytes 1048600
  13.8 0.9 %copy-done.8 = bf16[256,512]{1,0:T(8,128)(2,1)S(1)} copy-done((bf16[256,512]{1,0:T(8,128)(2,1)S(1)}, bf16[256,512]{1,0:T(8,128)(2,1)}, u32[]{:S(2)}) %copy-start.8) | copy-done | bytes 262168
  14.8 1.1 %rotate_queries.1 = (bf16[256,2048]{1,0:T(8,128)(2,1)S(1)}, bf16[2048,256]{1,0:T(8,128)(2,1)S(1)}, bf16[2048,256]{1,0:T(8,128)(2,1)S(1)}, bf16[256,512]{1,0:T(8,128)(2,1)S(1)}) custom-call(f32[256,128]{1,0:T(8,128)S(1)} %copy-done, f32[256,128]{1,0:T(8,128)S(1)} %copy-done.2, bf16[256,2048]{1,0:T(8,128)(2,1)S(1)} %bitcast.7, bf16[256,2048]{1,0:T(8,128)(2,1)S(1)} %bitcast.8, ...), custom_call_target="tpu_custom_call" | custom-call | flops 3000000000 | bytes 4194304 | tf_op jit(solution)/shard_map/rotate_queries/pallas_call | solution.py:155
  15.9 3.5 %collective-permute-start.2 = (bf16[256,512]{1,0:T(8,128)(2,1)S(1)}, bf16[256,512]{1,0:T(8,128)(2,1)S(1)}, u32[]{:S(2)}, u32[]{:S(2)}) collective-permute-start(bf16[256,512]{1,0:T(8,128)(2,1)S(1)} %get-tuple-element.29), channel_id=1, source_target_pairs={{0,4},{4,8},{1,5},{5,9},{2,6},{6,10},{3,7},{7,11},{16,20},{20,24},... | collective-permute-start | bytes 786440 | tf_op jit(solution)/shard_map/ppermute | solution.py:403
  19.4 0.0 collective-permute-done.refs_1_
  19.5 0.7 %collective-permute-start.3 = (bf16[256,512]{1,0:T(8,128)(2,1)S(1)}, bf16[256,512]{1,0:T(8,128)(2,1)S(1)}, u32[]{:S(2)}, u32[]{:S(2)}) collective-permute-start(bf16[256,512]{1,0:T(8,128)(2,1)S(1)} %collective-permute-done.refs_1_), channel_id=1, source_target_pairs={{8,12},{9,13},{10,14},{11,15},{24,28},{25,29},{26,30},{27,31}} | collective-permute-start | bytes 786440 | tf_op jit(solution)/shard_map/ppermute | solution.py:404
  20.1 0.0 collective-permute-done.1.refs_2_
  20.2 4.5 %collective-permute-done.2.refs_3_ = bf16[256,512]{1,0:T(8,128)(2,1)S(1)} collective-permute-done((bf16[256,512]{1,0:T(8,128)(2,1)S(1)}, bf16[256,512]{1,0:T(8,128)(2,1)S(1)}, u32[]{:S(2)}, u32[]{:S(2)}) %collective-permute-start.2) | collective-permute-done | bytes 262176 | tf_op jit(solution)/shard_map/ppermute | solution.py:403
  24.7 0.0 collective-permute-done.3.refs_4_
  24.7 0.0 copy-done.4
  24.7 0.0 copy-done.7
  24.7 0.0 copy-done.9
  24.7 0.0 copy-start.1
  24.7 0.0 copy-start.3
  24.7 9.7 %scores.1 = (bf16[256,512]{1,0:T(8,128)(2,1)S(1)}, bf16[256,512]{1,0:T(8,128)(2,1)S(1)}, f32[256,512]{1,0:T(8,128)S(1)}, bf16[2,576,2048]{2,1,0:T(8,128)(2,1)S(1...) custom-call(s32[8]{0:T(128)S(1)} %copy-done.4, bf16[256,2048]{1,0:T(8,128)(2,1)S(1)} %get-tuple-element.26.turned_ref, ...), custom_call_target="tpu_custom_call" | custom-call | flops 12000000000 | bytes 12582912 | tf_op jit(solution)/shard_map/scores/pallas_call | solution.py:278
  34.5 1.3 %collective-permute-start.4 = (bf16[256,512]{1,0:T(8,128)(2,1)S(1)}, bf16[256,512]{1,0:T(8,128)(2,1)S(1)}, u32[]{:S(2)}, u32[]{:S(2)}) collective-permute-start(bf16[256,512]{1,0:T(8,128)(2,1)S(1)} %get-tuple-element.36), channel_id=1, source_target_pairs={{12,8},{8,4},{4,0},{13,9},{9,5},{5,1},{14,10},{10,6},{6,2},{15,11}... | collective-permute-start | bytes 786440 | tf_op jit(solution)/shard_map/ppermute | solution.py:413
  35.8 0.0 copy-done.1
  35.8 3.9 %local_terms.1 = (bf16[256,2048]{1,0:T(8,128)(2,1)}, f32[256,512]{1,0:T(8,128)S(1)}, bf16[256,512]{1,0:T(8,128)(2,1)S(1)}) custom-call(s32[8]{0:T(128)S(1)} %copy-done.4, f32[256,128]{1,0:T(8,128)S(1)} %copy-done.1, f32[256,128]{1,0:T(8,128)S(1)} %copy-done.3, bf16[256,2048]{1,0:T(8,128)(2,1)S(1)} %get-tuple-element.26.turned_ref, ...), custom_call_target="tpu_custom_call" | custom-call | flops 5000000000 | bytes 10485760 | tf_op jit(solution)/shard_map/local_terms/pallas_call | solution.py:346
  39.6 0.7 %collective-permute-start.6 = (bf16[256,512]{1,0:T(8,128)(2,1)S(1)}, bf16[256,512]{1,0:T(8,128)(2,1)S(1)}, u32[]{:S(2)}, u32[]{:S(2)}) collective-permute-start(bf16[256,512]{1,0:T(8,128)(2,1)S(1)} %get-tuple-element.38), channel_id=1, source_target_pairs={{12,4},{13,5},{14,6},{15,7},{28,20},{29,21},{30,22},{31,23}} | collective-permute-start | bytes 786440 | tf_op jit(solution)/shard_map/ppermute | solution.py:472
  40.3 6.3 %collective-permute-done.4.refs_0_ = bf16[256,512]{1,0:T(8,128)(2,1)S(1)} collective-permute-done((bf16[256,512]{1,0:T(8,128)(2,1)S(1)}, bf16[256,512]{1,0:T(8,128)(2,1)S(1)}, u32[]{:S(2)}, u32[]{:S(2)}) %collective-permute-start.4) | collective-permute-done | bytes 262176 | tf_op jit(solution)/shard_map/ppermute | solution.py:413
  46.6 0.1 add_convert_fusion
  46.7 1.3 %collective-permute-start.5 = (bf16[256,512]{1,0:T(8,128)(2,1)S(1)}, bf16[256,512]{1,0:T(8,128)(2,1)S(1)}, u32[]{:S(2)}, u32[]{:S(2)}) collective-permute-start(bf16[256,512]{1,0:T(8,128)(2,1)S(1)} %add_convert_fusion), channel_id=1, source_target_pairs={{12,8},{8,0},{13,9},{9,1},{14,10},{10,2},{15,11},{11,3},{28,24},{2... | collective-permute-start | bytes 786440 | tf_op jit(solution)/shard_map/ppermute | solution.py:415
  48.0 0.0 collective-permute-done.6.refs_2_
  48.0 14.5 %collective-permute-done.5.refs_1_ = bf16[256,512]{1,0:T(8,128)(2,1)S(1)} collective-permute-done((bf16[256,512]{1,0:T(8,128)(2,1)S(1)}, bf16[256,512]{1,0:T(8,128)(2,1)S(1)}, u32[]{:S(2)}, u32[]{:S(2)}) %collective-permute-start.5) | collective-permute-done | bytes 262176 | tf_op jit(solution)/shard_map/ppermute | solution.py:415
  62.5 1.4 %finish.1 = (bf16[256,256]{1,0:T(8,128)(2,1)}, bf16[256,256]{1,0:T(8,128)(2,1)}) custom-call(s32[8]{0:T(128)S(1)} %copy-done.4, f32[256,128]{1,0:T(8,128)S(1)} %copy-done.1, f32[256,128]{1,0:T(8,128)S(1)} %copy-done.3, f32[256,512]{1,0:T(8,128)S(1)} %get-tuple-element.35.own_ref, bf16[256,512]{1,0:T(8,128)(2,1)S(1)} %collective-permute-done.4.refs_0_, ...), custom_call_target="tpu_custom_call" | custom-call | tf_op jit(solution)/shard_map/finish/pallas_call | solution.py:385
  (8 shorter events, 0.0 us)
Async XLA Ops:
  2.9 17.2 %collective-permute-start.1 = (bf16[256,512]{1,0:T(8,128)(2,1)}, bf16[256,512]{1,0:T(8,128)(2,1)S(1)}, u32[]{:S(2)}, u32[]{:S(2)}) collective-permute-start(bf16[256,512]{1,0:T(8,128)(2,1)} %get-tuple-element.25.sent_ref.refs_0_), channel_id=1, source_target_pairs={{4,12},{5,13},{6,14},{7,15},{20,28},{21,29},{22,30},{23,31}} | collective-permute-start | bytes 786440 | tf_op jit(solution)/shard_map/ppermute | solution.py:402
  3.6 15.8 %collective-permute-start = (bf16[256,512]{1,0:T(8,128)(2,1)}, bf16[256,512]{1,0:T(8,128)(2,1)S(1)}, u32[]{:S(2)}, u32[]{:S(2)}) collective-permute-start(bf16[256,512]{1,0:T(8,128)(2,1)} %get-tuple-element.25.sent_ref.refs_0_), channel_id=1, source_target_pairs={{0,8},{8,12},{1,9},{9,13},{2,10},{10,14},{3,11},{11,15},{16,24},{2... | collective-permute-start | bytes 786440 | tf_op jit(solution)/shard_map/ppermute | solution.py:401
  9.6 0.9 %copy-start = (f32[256,128]{1,0:T(8,128)S(1)}, f32[256,128]{1,0:T(8,128)}, u32[]{:S(2)}) copy-start(f32[256,128]{1,0:T(8,128)} %get-tuple-element.23.cos_ref) | copy-start | bytes 393220
  10.5 0.9 %copy-start.2 = (f32[256,128]{1,0:T(8,128)S(1)}, f32[256,128]{1,0:T(8,128)}, u32[]{:S(2)}) copy-start(f32[256,128]{1,0:T(8,128)} %get-tuple-element.24.sin_ref) | copy-start | bytes 393220
  11.4 1.2 %copy-start.5 = (bf16[1,256,2048]{2,1,0:T(8,128)(2,1)S(1)}, bf16[1,256,2048]{2,1,0:T(8,128)(2,1)}, u32[]{:S(2)}) copy-start(bf16[1,256,2048]{2,1,0:T(8,128)(2,1)} %param.7) | copy-start | bytes 3145732
  12.6 1.2 %copy-start.6 = (bf16[1,256,2048]{2,1,0:T(8,128)(2,1)S(1)}, bf16[1,256,2048]{2,1,0:T(8,128)(2,1)}, u32[]{:S(2)}) copy-start(bf16[1,256,2048]{2,1,0:T(8,128)(2,1)} %param.10) | copy-start | bytes 3145732
  13.8 0.9 %copy-start.8 = (bf16[256,512]{1,0:T(8,128)(2,1)S(1)}, bf16[256,512]{1,0:T(8,128)(2,1)}, u32[]{:S(2)}) copy-start(bf16[256,512]{1,0:T(8,128)(2,1)} %get-tuple-element.25.sent_ref.refs_0_) | copy-start | bytes 786436
  14.8 9.9 %copy-start.4 = (s32[8]{0:T(128)S(1)}, s32[8]{0:T(128)}, u32[]{:S(2)}) copy-start(s32[8]{0:T(128)} %get-tuple-element.22.meta_ref) | copy-start | bytes 100
  14.8 9.9 %copy-start.7 = (bf16[1,256,2048]{2,1,0:T(8,128)(2,1)S(1)}, bf16[1,256,2048]{2,1,0:T(8,128)(2,1)}, u32[]{:S(2)}) copy-start(bf16[1,256,2048]{2,1,0:T(8,128)(2,1)} %param.10) | copy-start | bytes 3145732
  14.8 9.9 %copy-start.9 = (bf16[256,512]{1,0:T(8,128)(2,1)S(1)}, bf16[256,512]{1,0:T(8,128)(2,1)}, u32[]{:S(2)}) copy-start(bf16[256,512]{1,0:T(8,128)(2,1)} %get-tuple-element.25.sent_ref.refs_0_) | copy-start | bytes 786436
  15.9 8.8 %collective-permute-start.2 = (bf16[256,512]{1,0:T(8,128)(2,1)S(1)}, bf16[256,512]{1,0:T(8,128)(2,1)S(1)}, u32[]{:S(2)}, u32[]{:S(2)}) collective-permute-start(bf16[256,512]{1,0:T(8,128)(2,1)S(1)} %get-tuple-element.29), channel_id=1, source_target_pairs={{0,4},{4,8},{1,5},{5,9},{2,6},{6,10},{3,7},{7,11},{16,20},{20,24},... | collective-permute-start | bytes 786440 | tf_op jit(solution)/shard_map/ppermute | solution.py:403
  19.5 5.2 %collective-permute-start.3 = (bf16[256,512]{1,0:T(8,128)(2,1)S(1)}, bf16[256,512]{1,0:T(8,128)(2,1)S(1)}, u32[]{:S(2)}, u32[]{:S(2)}) collective-permute-start(bf16[256,512]{1,0:T(8,128)(2,1)S(1)} %collective-permute-done.refs_1_), channel_id=1, source_target_pairs={{8,12},{9,13},{10,14},{11,15},{24,28},{25,29},{26,30},{27,31}} | collective-permute-start | bytes 786440 | tf_op jit(solution)/shard_map/ppermute | solution.py:404
  24.7 11.1 %copy-start.1 = (f32[256,128]{1,0:T(8,128)S(1)}, f32[256,128]{1,0:T(8,128)}, u32[]{:S(2)}) copy-start(f32[256,128]{1,0:T(8,128)} %get-tuple-element.23.cos_ref) | copy-start | bytes 393220
  24.7 11.1 %copy-start.3 = (f32[256,128]{1,0:T(8,128)S(1)}, f32[256,128]{1,0:T(8,128)}, u32[]{:S(2)}) copy-start(f32[256,128]{1,0:T(8,128)} %get-tuple-element.24.sin_ref) | copy-start | bytes 393220
  34.5 12.1 %collective-permute-start.4 = (bf16[256,512]{1,0:T(8,128)(2,1)S(1)}, bf16[256,512]{1,0:T(8,128)(2,1)S(1)}, u32[]{:S(2)}, u32[]{:S(2)}) collective-permute-start(bf16[256,512]{1,0:T(8,128)(2,1)S(1)} %get-tuple-element.36), channel_id=1, source_target_pairs={{12,8},{8,4},{4,0},{13,9},{9,5},{5,1},{14,10},{10,6},{6,2},{15,11}... | collective-permute-start | bytes 786440 | tf_op jit(solution)/shard_map/ppermute | solution.py:413
  39.6 8.3 %collective-permute-start.6 = (bf16[256,512]{1,0:T(8,128)(2,1)S(1)}, bf16[256,512]{1,0:T(8,128)(2,1)S(1)}, u32[]{:S(2)}, u32[]{:S(2)}) collective-permute-start(bf16[256,512]{1,0:T(8,128)(2,1)S(1)} %get-tuple-element.38), channel_id=1, source_target_pairs={{12,4},{13,5},{14,6},{15,7},{28,20},{29,21},{30,22},{31,23}} | collective-permute-start | bytes 786440 | tf_op jit(solution)/shard_map/ppermute | solution.py:472
  46.7 15.8 %collective-permute-start.5 = (bf16[256,512]{1,0:T(8,128)(2,1)S(1)}, bf16[256,512]{1,0:T(8,128)(2,1)S(1)}, u32[]{:S(2)}, u32[]{:S(2)}) collective-permute-start(bf16[256,512]{1,0:T(8,128)(2,1)S(1)} %add_convert_fusion), channel_id=1, source_target_pairs={{12,8},{8,0},{13,9},{9,1},{14,10},{10,2},{15,11},{11,3},{28,24},{2... | collective-permute-start | bytes 786440 | tf_op jit(solution)/shard_map/ppermute | solution.py:415
